TPU v7x, 128 devices: a whole 4x4x4 slice. The times are simulated.
128 devices in a mesh: ctx: 16 (over x, z_lo, core), tp: 8 (over y, z_hi).
Axes of the slice: x: 4, y: 4, z: 4 (z_hi: 2, z_lo: 2; z = z_hi * 2 + z_lo), core: 2. Of those that a mesh axis runs over, the one named last changes fastest.
Arguments:
- tokens: bfloat16 [16384, 1024], P(('ctx', 'tp')), may hold values from -6 to 6
- block_ids: int32 [16384], P('ctx'), may hold values from 0 to 127, never falling along the last dimension, each value on 1 to 256 neighbouring positions
- ln1_gain: bfloat16 [1024], replicated, may hold values from 0.099609375 to 1.8984375
- ln1_shift: bfloat16 [1024], replicated, may hold values from -1.75 to 1.75
- qkv_weight: bfloat16 [1024, 3, 1024], P(None, None, 'tp'), may hold values from -0.1875 to 0.1875
- qv_bias: bfloat16 [2, 1024], P(None, 'tp'), may hold values from -3 to 3
- out_weight: bfloat16 [1024, 1024], P('tp'), may hold values from -0.5 to 0.5
- out_bias: bfloat16 [1024], replicated, may hold values from -1.75 to 1.75
- ln2_gain: bfloat16 [1024], replicated, may hold values from 0.099609375 to 1.8984375
- ln2_shift: bfloat16 [1024], replicated, may hold values from -1.75 to 1.75
- up_weight: bfloat16 [1024, 4096], P(None, 'tp'), may hold values from -0.1875 to 0.1875
- up_bias: bfloat16 [4096], P('tp'), may hold values from -3 to 3
- down_weight: bfloat16 [4096, 1024], P('tp'), may hold values from -0.09375 to 0.09375
- down_bias: bfloat16 [1024], replicated, may hold values from -1.75 to 1.75
- cotangent: bfloat16 [16384, 1024], P(('ctx', 'tp')), may hold values from -6 to 6
Outputs:
- output: float32 [16384, 1024], P(('ctx', 'tp'))
- grad_tokens: float32 [16384, 1024], P(('ctx', 'tp'))
- grad_ln1_gain: float32 [1024], replicated
- grad_ln1_shift: float32 [1024], replicated
- grad_qkv_weight: float32 [1024, 3, 1024], P(None, None, 'tp')
- grad_qv_bias: float32 [2, 1024], P(None, 'tp')
- grad_out_weight: float32 [1024, 1024], P('tp')
- grad_out_bias: float32 [1024], replicated
- grad_ln2_gain: float32 [1024], replicated
- grad_ln2_shift: float32 [1024], replicated
- grad_up_weight: float32 [1024, 4096], P(None, 'tp')
- grad_up_bias: float32 [4096], P('tp')
- grad_down_weight: float32 [4096, 1024], P('tp')
- grad_down_bias: float32 [1024], replicated
Inputs may be any that keep to these rules, and one draw needn't show every extreme that they name: `block_ids`: block numbers never fall along the sequence; each block holds 1 to 256 positions, one exactly 256, and every number is used.
All inputs are finite; a program needn't handle non-finite values.
Results may differ from a plain program's by a relative error of at most 0.019.
Values may be sent and summed in bfloat16 or wider, within the bound.
No kernel may reach another device: no remote copies, remote signals or barrier semaphores. Data moves between devices by JAX's collectives and lax.ppermute only.
A program may use at most 128 MiB of HBM per device.

v0:
```python
import jax
import jax.numpy as jnp
from jax import lax
from jax.sharding import PartitionSpec as P

HEAD_DIM = 64


EPSILON = 1e-05
MASKED = -1e30


def layer_norm(values, norm_gain, norm_shift):
    average = jnp.mean(values, axis=-1, keepdims=True)
    centered = values - average
    variance = jnp.mean(centered * centered, axis=-1, keepdims=True)
    return centered * lax.rsqrt(variance + EPSILON) * norm_gain + norm_shift


def gelu_tanh(values):
    return (
        0.5
        * values
        * (1.0 + jnp.tanh(0.7978845608028654 * (values + 0.044715 * values * values * values)))
    )


def head_rows(values):
    return values.reshape(values.shape[0], -1, HEAD_DIM)


def contract_rows(left, right):
    return lax.dot_general(
        left, right, (((0,), (0,)), ((), ())), preferred_element_type=jnp.float32
    )


def contract_cols(left, right):
    return lax.dot_general(
        left, right, (((1,), (1,)), ((), ())), preferred_element_type=jnp.float32
    )


def take_rows(values, first_row, amount):
    return lax.dynamic_slice_in_dim(values, first_row, amount, 0)


def add_rows(buffer, first_row, addend):
    current = lax.dynamic_slice_in_dim(buffer, first_row, addend.shape[0], 0)
    return lax.dynamic_update_slice_in_dim(buffer, current + addend, first_row, 0)


def over_blocks(total_rows, block_rows, visit, carried):
    block_rows = min(block_rows, total_rows)

    def advance(counter, inner):
        return visit(counter * block_rows, block_rows, inner)

    return lax.fori_loop(0, total_rows // block_rows, advance, carried)


def unchanged(carried):
    return carried


def block_scores(query_rows, key_rows, query_ids, key_ids):
    scores = jnp.einsum(
        "qhd,khd->hqk",
        head_rows(query_rows),
        head_rows(key_rows),
        preferred_element_type=jnp.float32,
    ) * HEAD_DIM ** (-0.5)
    allowed = key_ids[None, None, :] <= query_ids[None, :, None]
    return (scores, allowed)


def forward_block(carried, query_rows, query_ids, key_rows, value_rows, key_ids):
    row_max, row_sum, running = carried
    scores, allowed = block_scores(query_rows, key_rows, query_ids, key_ids)
    masked = jnp.where(allowed, scores, MASKED)
    new_max = jnp.maximum(row_max, jnp.max(masked, axis=-1))
    weights = jnp.where(allowed, jnp.exp(masked - new_max[:, :, None]), 0.0)
    factor = jnp.exp(row_max - new_max)
    row_sum = row_sum * factor + jnp.sum(weights, axis=-1)
    running = running * factor[:, :, None] + jnp.einsum(
        "hqk,khd->hqd",
        weights.astype(jnp.bfloat16),
        head_rows(value_rows),
        preferred_element_type=jnp.float32,
    )
    return (new_max, row_sum, running)


def grad_block(query_rows, grad_out, log_norms, deltas, query_ids, key_rows, value_rows, key_ids):
    scores, allowed = block_scores(query_rows, key_rows, query_ids, key_ids)
    exponent = jnp.where(allowed, scores - log_norms.T[:, :, None], MASKED)
    weights = jnp.where(allowed, jnp.exp(exponent), 0.0)
    grad_weights = jnp.einsum(
        "qhd,khd->hqk",
        head_rows(grad_out),
        head_rows(value_rows),
        preferred_element_type=jnp.float32,
    )
    grad_scores = (weights * (grad_weights - deltas.T[:, :, None])).astype(jnp.bfloat16)
    scale = HEAD_DIM ** (-0.5)
    grad_query = (
        jnp.einsum(
            "hqk,khd->qhd", grad_scores, head_rows(key_rows), preferred_element_type=jnp.float32
        )
        * scale
    )
    grad_key = (
        jnp.einsum(
            "hqk,qhd->khd", grad_scores, head_rows(query_rows), preferred_element_type=jnp.float32
        )
        * scale
    )
    grad_value = jnp.einsum(
        "hqk,qhd->khd",
        weights.astype(jnp.bfloat16),
        head_rows(grad_out),
        preferred_element_type=jnp.float32,
    )
    return (
        grad_query.reshape(query_rows.shape),
        grad_key.reshape(key_rows.shape),
        grad_value.reshape(value_rows.shape),
    )


def on_device(
    tokens,
    block_ids,
    ln1_gain,
    ln1_shift,
    qkv_weight,
    qv_bias,
    out_weight,
    out_bias,
    ln2_gain,
    ln2_shift,
    up_weight,
    up_bias,
    down_weight,
    down_bias,
    cotangent,
):
    tok_dev, width = tokens.shape
    tok_ctx = block_ids.shape[0]
    half_rows = tok_ctx // 2
    local_width = out_weight.shape[0]
    heads_local = local_width // HEAD_DIM
    total_rows = tok_ctx * lax.axis_size("ctx")
    tokens_wide = tokens.astype(jnp.float32)
    normed_own, norm_one_back = jax.vjp(
        layer_norm, tokens_wide, ln1_gain.astype(jnp.float32), ln1_shift.astype(jnp.float32)
    )
    normed_all = lax.all_gather(normed_own.astype(jnp.bfloat16), "tp", axis=0, tiled=True)
    flat_qkv = qkv_weight.reshape(width, 3 * local_width)
    projected = jnp.dot(normed_all, flat_qkv, preferred_element_type=jnp.float32).reshape(
        tok_ctx, 3, local_width
    )
    bias_pair = qv_bias.astype(jnp.float32)
    queries = (projected[:, 0] + bias_pair[0]).astype(jnp.bfloat16)
    keys = projected[:, 1].astype(jnp.bfloat16)
    values = (projected[:, 2] + bias_pair[1]).astype(jnp.bfloat16)
    half_state = (
        jnp.full((heads_local, half_rows), MASKED, jnp.float32),
        jnp.zeros((heads_local, half_rows), jnp.float32),
        jnp.zeros((heads_local, half_rows, HEAD_DIM), jnp.float32),
    )
    key_part = lax.all_gather(keys, "ctx", axis=0, tiled=True)
    value_part = lax.all_gather(values, "ctx", axis=0, tiled=True)
    id_part = lax.all_gather(block_ids, "ctx", axis=0, tiled=True)

    def visit(offset, amount, inner):
        key_rows = take_rows(key_part, offset, amount)
        value_rows = take_rows(value_part, offset, amount)
        key_ids = take_rows(id_part, offset, amount)
        updated = []
        for which_half in range(2):
            query_rows = queries[which_half * half_rows : (which_half + 1) * half_rows]
            query_ids = block_ids[which_half * half_rows : (which_half + 1) * half_rows]

            def attend(current, query_rows=query_rows, query_ids=query_ids):
                return forward_block(current, query_rows, query_ids, key_rows, value_rows, key_ids)

            updated.append(
                lax.cond(key_ids[0] > query_ids[-1], unchanged, attend, inner[which_half])
            )
        return tuple(updated)

    first_state, second_state = over_blocks(
        key_part.shape[0], half_rows, visit, (half_state, half_state)
    )
    row_max = jnp.concatenate([first_state[0], second_state[0]], axis=1)
    row_sum = jnp.concatenate([first_state[1], second_state[1]], axis=1)
    running = jnp.concatenate([first_state[2], second_state[2]], axis=1)
    out_heads = running / row_sum[:, :, None]
    log_norms = (row_max + jnp.log(row_sum)).T
    out_rows = jnp.transpose(out_heads, (1, 0, 2)).reshape(tok_ctx, local_width)
    attended = out_rows.astype(jnp.bfloat16)
    branch = lax.psum_scatter(
        jnp.dot(
            take_rows(attended, jnp.int32(0), tok_dev * lax.axis_size("tp")),
            out_weight,
            preferred_element_type=jnp.float32,
        ),
        "tp",
        scatter_dimension=0,
        tiled=True,
    )
    resid = tokens_wide + branch + out_bias.astype(jnp.float32)
    normed_mid, norm_two_back = jax.vjp(
        layer_norm, resid, ln2_gain.astype(jnp.float32), ln2_shift.astype(jnp.float32)
    )
    mid_all = lax.all_gather(normed_mid.astype(jnp.bfloat16), "tp", axis=0, tiled=True)
    hidden = jnp.dot(mid_all, up_weight, preferred_element_type=jnp.float32) + up_bias.astype(
        jnp.float32
    )
    active_wide, gelu_back = jax.vjp(gelu_tanh, hidden)
    active = active_wide.astype(jnp.bfloat16)
    output = (
        resid
        + lax.psum_scatter(
            jnp.dot(
                take_rows(active, jnp.int32(0), tok_dev * lax.axis_size("tp")),
                down_weight,
                preferred_element_type=jnp.float32,
            ),
            "tp",
            scatter_dimension=0,
            tiled=True,
        )
        + down_bias.astype(jnp.float32)
    )
    grad_all = lax.all_gather(cotangent, "tp", axis=0, tiled=True)
    grad_down_weight = contract_rows(active, grad_all)
    grad_active = contract_cols(grad_all, down_weight)
    grad_hidden = gelu_back(grad_active)[0].astype(jnp.bfloat16)
    grad_up_weight = contract_rows(mid_all, grad_hidden)
    grad_up_bias = jnp.sum(grad_hidden.astype(jnp.float32), axis=0)
    grad_mid = lax.psum_scatter(
        contract_cols(
            take_rows(grad_hidden, jnp.int32(0), tok_dev * lax.axis_size("tp")), up_weight
        ),
        "tp",
        scatter_dimension=0,
        tiled=True,
    )
    grad_resid_norm, grad_ln2_gain, grad_ln2_shift = norm_two_back(grad_mid)
    grad_resid = cotangent.astype(jnp.float32) + grad_resid_norm
    grad_out_bias = jnp.sum(grad_resid, axis=0)
    grad_branch_all = lax.all_gather(grad_resid.astype(jnp.bfloat16), "tp", axis=0, tiled=True)
    grad_out_weight = contract_rows(attended, grad_branch_all)
    grad_attended = contract_cols(grad_branch_all, out_weight).astype(jnp.bfloat16)
    deltas = jnp.sum(head_rows(grad_attended.astype(jnp.float32)) * head_rows(out_rows), axis=-1)
    grad_state = (
        jnp.zeros((tok_ctx, local_width), jnp.float32),
        jnp.zeros((total_rows, local_width), jnp.float32),
        jnp.zeros((total_rows, local_width), jnp.float32),
    )
    fold_key_part = lax.all_gather(keys, "ctx", axis=0, tiled=True)
    fold_value_part = lax.all_gather(values, "ctx", axis=0, tiled=True)
    fold_id_part = lax.all_gather(block_ids, "ctx", axis=0, tiled=True)

    def visit(offset, amount, inner):
        key_rows = take_rows(fold_key_part, offset, amount)
        value_rows = take_rows(fold_value_part, offset, amount)
        key_ids = take_rows(fold_id_part, offset, amount)
        target = offset
        for which_half in range(2):
            low_row = which_half * half_rows
            query_ids = block_ids[low_row : low_row + half_rows]

            def accumulate(buffers, low_row=low_row, query_ids=query_ids):
                query_sum, key_buffer, value_buffer = buffers
                grad_query, grad_key, grad_value = grad_block(
                    queries[low_row : low_row + half_rows],
                    grad_attended[low_row : low_row + half_rows],
                    log_norms[low_row : low_row + half_rows],
                    deltas[low_row : low_row + half_rows],
                    query_ids,
                    key_rows,
                    value_rows,
                    key_ids,
                )
                return (
                    add_rows(query_sum, low_row, grad_query),
                    add_rows(key_buffer, target, grad_key),
                    add_rows(value_buffer, target, grad_value),
                )

            inner = lax.cond(key_ids[0] > query_ids[-1], unchanged, accumulate, inner)
        return inner

    query_grad, key_buffer, value_buffer = over_blocks(
        fold_key_part.shape[0], half_rows, visit, grad_state
    )
    key_grad, value_grad = (
        lax.psum_scatter(key_buffer, "ctx", scatter_dimension=0, tiled=True),
        lax.psum_scatter(value_buffer, "ctx", scatter_dimension=0, tiled=True),
    )
    grad_projected = jnp.stack([query_grad, key_grad, value_grad], axis=1).astype(jnp.bfloat16)
    grad_flat = grad_projected.reshape(tok_ctx, 3 * local_width)
    grad_qkv_weight = contract_rows(normed_all, grad_flat).reshape(width, 3, local_width)
    grad_qv_bias = jnp.stack(
        [
            jnp.sum(grad_projected[:, 0].astype(jnp.float32), axis=0),
            jnp.sum(grad_projected[:, 2].astype(jnp.float32), axis=0),
        ]
    )
    grad_normed = lax.psum_scatter(
        contract_cols(take_rows(grad_flat, jnp.int32(0), tok_dev * lax.axis_size("tp")), flat_qkv),
        "tp",
        scatter_dimension=0,
        tiled=True,
    )
    grad_tokens_norm, grad_ln1_gain, grad_ln1_shift = norm_one_back(grad_normed)
    grad_tokens = grad_resid + grad_tokens_norm
    grad_down_bias = jnp.sum(cotangent.astype(jnp.float32), axis=0)
    (
        grad_qkv_weight,
        grad_qv_bias,
        grad_out_weight,
        grad_up_weight,
        grad_up_bias,
        grad_down_weight,
    ) = lax.psum(
        (
            grad_qkv_weight,
            grad_qv_bias,
            grad_out_weight,
            grad_up_weight,
            grad_up_bias,
            grad_down_weight,
        ),
        "ctx",
    )
    grad_ln1_gain, grad_ln1_shift, grad_out_bias, grad_ln2_gain, grad_ln2_shift, grad_down_bias = (
        lax.psum(
            (
                grad_ln1_gain,
                grad_ln1_shift,
                grad_out_bias,
                grad_ln2_gain,
                grad_ln2_shift,
                grad_down_bias,
            ),
            ("ctx", "tp"),
        )
    )
    return (
        output,
        grad_tokens,
        grad_ln1_gain,
        grad_ln1_shift,
        grad_qkv_weight,
        grad_qv_bias,
        grad_out_weight,
        grad_out_bias,
        grad_ln2_gain,
        grad_ln2_shift,
        grad_up_weight,
        grad_up_bias,
        grad_down_weight,
        grad_down_bias,
    )


def solution(mesh):
    placed = (
        P(("ctx", "tp"), None),
        P("ctx"),
        P(),
        P(),
        P(None, None, "tp"),
        P(None, "tp"),
        P("tp", None),
        P(),
        P(),
        P(),
        P(None, "tp"),
        P("tp"),
        P("tp", None),
        P(),
        P(("ctx", "tp"), None),
    )
    return jax.shard_map(
        on_device,
        mesh=mesh,
        in_specs=placed,
        out_specs=(
            P(("ctx", "tp"), None),
            P(("ctx", "tp"), None),
            P(),
            P(),
            P(None, None, "tp"),
            P(None, "tp"),
            P("tp", None),
            P(),
            P(),
            P(),
            P(None, "tp"),
            P("tp"),
            P("tp", None),
            P(),
        ),
        check_vma=False,
    )
```

profile of v0, /device:TPU:1, one launch (start us, length us, event | category | flops | bytes accessed | tf_op | source)
XLA Modules:
  0.0 1919.6 jit_solution(6207052196714477245)
XLA Ops:
  10.9 1.9 fusion.45
  12.9 2.3 copy.57
  15.2 54.7 %all-gather.8.cloned.1.call-done = bf16[1024,1024]{1,0:T(8,128)(2,1)} async-done(((bf16[128,1024]{1,0:T(8,128)(2,1)}), bf16[1024,1024]{1,0:T(8,128)(2,1)}) %all-gather.8.cloned.1.call-update) | async-done | bytes 2097168 | tf_op jit(solution)/shard_map/all_gather | solution.py:158
  69.9 3.0 fusion.34
  74.7 21.0 %all_gather.24 = s32[16384]{0:T(1024)S(1)} all-gather(s32[1024]{0:T(1024)S(1)} %copy-done.10), channel_id=1, replica_groups=mesh['ctx'=16,'tp'=8] {'ctx'}, dimensions={0}, use_global_device_ids=true | all-gather | bytes 69632 | tf_op jit(solution)/shard_map/all_gather | solution.py:174
  95.8 15.8 all-gather.18.cloned.1.call-done
  111.6 6.4 copy.58
  118.0 33.5 %all-gather.10.cloned.1.call-done = bf16[16384,128]{1,0:T(8,128)(2,1)} async-done(((bf16[1024,128]{1,0:T(8,128)(2,1)}), bf16[16384,128]{1,0:T(8,128)(2,1)}) %all-gather.10.cloned.1.call-update) | async-done | bytes 4194320 | tf_op jit(solution)/shard_map/all_gather | solution.py:173
  151.5 6.5 copy.59
  158.1 177.1 %while.40 = (s32[]{:T(128)}, f32[2,512]{1,0:T(2,128)S(1)}, f32[2,512]{1,0:T(2,128)S(1)}, f32[2,512,64]{1,2,0:T(8,128)S(1)}, f32[2,512]{1,0:T(2,128)S(1)}, /*inde...) while((s32[]{:T(128)}, f32[2,512]{1,0:T(2,128)S(1)}, ...), condition=%wide.region_11.12_spmd, body=%wide.region_2.11_spmd.sunk | while | flops 282857472 | bytes 17715680 | solution.py:59
  162.9 2.3 conditional.8
  165.2 2.3 conditional.9
  172.3 2.3 conditional.8
  174.6 2.3 conditional.9
  181.8 2.3 conditional.8
  184.1 2.3 conditional.9
  191.2 2.3 conditional.8
  193.5 2.3 conditional.9
  200.7 2.3 conditional.9
  335.3 2.7 fusion.72
  338.7 207.0 %reduce-scatter.7.cloned.1.call-done = f32[128,1024]{1,0:T(8,128)} async-done(((f32[1024,1024]{1,0:T(8,128)}), f32[128,1024]{1,0:T(8,128)}) %reduce-scatter.7.cloned.1.call-update) | async-done | bytes 524304 | tf_op jit(solution)/shard_map/reduce_scatter | solution.py:203
  548.9 52.9 %all-gather.12.cloned.1.call-done = bf16[1024,1024]{1,0:T(8,128)(2,1)} async-done(((bf16[128,1024]{1,0:T(8,128)(2,1)}), bf16[1024,1024]{1,0:T(8,128)(2,1)}) %all-gather.12.cloned.1.call-update) | async-done | bytes 2097168 | tf_op jit(solution)/shard_map/all_gather | solution.py:217
  601.8 4.4 fusion.73
  606.2 51.5 %all-gather.14.cloned.1.call-done = bf16[1024,1024]{1,0:T(8,128)(2,1)} async-done(((bf16[128,1024]{1,0:T(8,128)(2,1)}), bf16[1024,1024]{1,0:T(8,128)(2,1)}) %all-gather.14.cloned.1.call-update) | async-done | bytes 2097168 | tf_op jit(solution)/shard_map/all_gather | solution.py:237
  657.7 5.2 convert_reduce_fusion
  663.8 3.3 fusion.74
  667.2 5.0 fusion.64
  672.9 78.2 %reduce-scatter.11.cloned.1.call-done = f32[128,1024]{1,0:T(8,128)} async-done(((f32[1024,1024]{1,0:T(8,128)}), f32[128,1024]{1,0:T(8,128)}) %reduce-scatter.11.cloned.1.call-update) | async-done | bytes 524304 | tf_op jit(solution)/shard_map/reduce_scatter | solution.py:243
  752.5 86.1 %reduce-scatter.9.cloned.1.call-done = f32[128,1024]{1,0:T(8,128)} async-done(((f32[1024,1024]{1,0:T(8,128)}), f32[128,1024]{1,0:T(8,128)}) %reduce-scatter.9.cloned.1.call-update) | async-done | bytes 524304 | tf_op jit(solution)/shard_map/reduce_scatter | solution.py:225
  838.6 2.2 fusion.67
  841.9 53.2 %all-gather.16.cloned.1.call-done = bf16[1024,1024]{1,0:T(8,128)(2,1)} async-done(((bf16[128,1024]{1,0:T(8,128)(2,1)}), bf16[1024,1024]{1,0:T(8,128)(2,1)}) %all-gather.16.cloned.1.call-update) | async-done | bytes 2097168 | tf_op jit(solution)/shard_map/all_gather | solution.py:254
  895.1 2.4 fusion.55
  897.6 4.1 broadcast.227.clone
  901.7 4.1 broadcast.227
  905.8 210.2 %while.41 = (s32[]{:T(128)}, f32[1024,128]{0,1:T(8,128)S(1)}, f32[16384,128]{0,1:T(8,128)}, f32[16384,128]{0,1:T(8,128)}, s32[16384]{0:T(1024)S(1)}, /*index=5*/...) while((s32[]{:T(128)}, f32[1024,128]{0,1:T(8,128)S(1)}, ...), condition=%wide.region_25.26_spmd, body=%wide.region_20.25_spmd.sunk | while | flops 680656896 | bytes 29692524 | solution.py:59
  910.6 6.1 conditional.10
  916.7 6.1 conditional.11
  927.6 6.1 conditional.10
  930.3 1.7 constant_dynamic-update-slice_fusion.1
  933.7 6.1 conditional.11
  938.1 1.7 constant_dynamic-update-slice_fusion.4
  944.6 6.2 conditional.10
  947.4 1.7 constant_dynamic-update-slice_fusion.1
  949.1 1.7 constant_dynamic-update-slice_fusion
  950.8 6.1 conditional.11
  952.7 1.7 constant_dynamic-update-slice_fusion.3
  955.1 1.7 constant_dynamic-update-slice_fusion.4
  961.7 6.1 conditional.10
  967.8 6.1 conditional.11
  978.7 6.1 conditional.11
  1116.0 9.0 copy.66
  1125.1 9.0 copy.65
  1134.3 419.6 %reduce-scatter.15.cloned.1.call-done = f32[1024,128]{1,0:T(8,128)} async-done(((f32[16384,128]{1,0:T(8,128)}), f32[1024,128]{1,0:T(8,128)}) %reduce-scatter.15.cloned.1.call-update) | async-done | bytes 524304 | tf_op jit(solution)/shard_map/reduce_scatter | solution.py:302
  1553.9 100.3 %reduce-scatter.13.cloned.1.call-done = f32[1024,128]{1,0:T(8,128)} async-done(((f32[16384,128]{1,0:T(8,128)}), f32[1024,128]{1,0:T(8,128)}) %reduce-scatter.13.cloned.1.call-update) | async-done | bytes 524304 | tf_op jit(solution)/shard_map/reduce_scatter | solution.py:301
  1655.5 4.4 convolution_bitcast_fusion
  1660.3 4.6 fusion.76
  1664.9 2.7 fusion.63
  1669.2 4.4 fusion.32
  1673.7 26.6 %all-reduce.1 = (f32[2,128]{1,0:T(2,128)}, f32[512]{0:T(512)}) all-reduce(f32[2,128]{1,0:T(2,128)S(1)} %pad_maximum_fusion, f32[512]{0:T(512)S(1)} %get-tuple-element.754), channel_id=1, replica_groups=mesh['ctx'=16,'tp'=8] {'ctx'}, use_global_device_ids=true, to_apply=%region_38.39 | all-reduce | flops 768 | bytes 6144 | tf_op jit(solution)/shard_map/psum | solution.py:329
  1700.3 44.4 %reduce-scatter.17.cloned.1.call-done = f32[128,1024]{1,0:T(8,128)} async-done(((f32[1024,1024]{1,0:T(8,128)}), f32[128,1024]{1,0:T(8,128)}) %reduce-scatter.17.cloned.1.call-update) | async-done | bytes 524304 | tf_op jit(solution)/shard_map/reduce_scatter | solution.py:313
  1747.4 2.2 convert_reduce_fusion.2
  1749.6 68.9 %all-reduce = (f32[1024]{0:T(1024)}, f32[1024]{0:T(1024)}, f32[1024]{0:T(1024)}, f32[1024]{0:T(1024)}, f32[1024]{0:T(1024)}, /*index=5*/f32[1024]{0:T(1024)}) all-reduce(f32[1024]{0:T(1024)S(1)} %get-tuple-element.681, f32[1024]{0:T(1024)S(1)} %get-tuple-element.686, ...), channel_id=1, replica_groups=mesh['ctx'=16,'tp'=8] {'ctx','tp'}, use_global_device_ids=true, to_apply=%region_32.0 | all-reduce | flops 6144 | bytes 49152 | tf_op jit(solution)/shard_map/psum | solution.py:341
  1818.4 87.4 %all-reduce.5.cloned.1.call-done = (f32[1024,3,128]{2,0,1:T(8,128)}, f32[128,1024]{1,0:T(8,128)}, f32[1024,512]{1,0:T(8,128)}, f32[512,1024]{1,0:T(8,128)}) async-done(((f32[1024,3,128]{2,0,1:T(8,128)}, f32[128,1024]{1,0:T(8,128)}, f32[1024,512]{1,0:T(8,128)}, f32[512,1024]{1,0:T(8,128)}), (f32[1024,3,128]{2,0,1:T(8,128)}, f32[128,1024]{1,0:T(8,128)}, f32[1024,512]{1,0:T(8,128)}, ...) | async-done | bytes 6291472 | tf_op jit(solution)/shard_map/psum | solution.py:329
  1905.8 2.8 copy.141
  (815 shorter events, 230.9 us)
Async XLA Ops:
  7.2 650.5 %copy-start = (bf16[512,1024]{1,0:T(8,128)(2,1)S(1)}, bf16[512,1024]{1,0:T(8,128)(2,1)}, u32[]{:S(2)}) copy-start(bf16[512,1024]{1,0:T(8,128)(2,1)} %param.39) | copy-start | bytes 3145732
  7.2 62.7 %all-gather.8.cloned.1.call-start = ((), (), s32[]{:S(2)}) async-start(), calls=%async_computation.6 | async-start | bytes 2359296 | tf_op jit(solution)/shard_map/all_gather | solution.py:158
  12.9 98.8 %all-gather.18.cloned.1.call-start = ((), (), s32[]{:S(2)}) async-start(), calls=%async_computation.17 | async-start | bytes 4456448 | tf_op jit(solution)/shard_map/all_gather | solution.py:172
  15.2 58.6 %copy-start.19 = (bf16[2,128]{1,0:T(2,128)(2,1)S(1)}, bf16[2,128]{1,0:T(2,128)(2,1)}, u32[]{:S(2)}) copy-start(bf16[2,128]{1,0:T(2,128)(2,1)} %param.32) | copy-start | bytes 1540
  73.0 1.7 copy-start.10
  73.7 77.8 %all-gather.10.cloned.1.call-start = ((), (), s32[]{:S(2)}) async-start(), calls=%async_computation.7 | async-start | bytes 4456448 | tf_op jit(solution)/shard_map/all_gather | solution.py:173
  74.6 471.1 %reduce-scatter.7.cloned.1.call-start = ((), (), s32[]{:S(2)}) async-start(), calls=%async_computation.8 | async-start | bytes 4718592 | tf_op jit(solution)/shard_map/reduce_scatter | solution.py:203
  158.1 177.2 %copy-start.8 = (bf16[128,1024]{1,0:T(8,128)(2,1)S(1)}, bf16[128,1024]{1,0:T(8,128)(2,1)}, u32[]{:S(2)}) copy-start(bf16[128,1024]{1,0:T(8,128)(2,1)} %param.33) | copy-start | bytes 786436
  338.0 0.7 copy-start.12
  338.0 0.7 copy-start.13
  338.0 0.7 copy-start.14
  338.0 207.7 %copy-start.2 = (bf16[128,1024]{1,0:T(8,128)(2,1)S(1)}, bf16[128,1024]{1,0:T(8,128)(2,1)}, u32[]{:S(2)}) copy-start(bf16[128,1024]{1,0:T(8,128)(2,1)} %param.27) | copy-start | bytes 786436
  338.0 210.8 %copy-start.16 = (bf16[512]{0:T(512)(128)(2,1)S(1)}, bf16[512]{0:T(512)(128)(2,1)}, u32[]{:S(2)}) copy-start(bf16[512]{0:T(512)(128)(2,1)} %param.38) | copy-start | bytes 3076
  338.0 263.8 %all-gather.12.cloned.1.call-start = ((), (), s32[]{:S(2)}) async-start(), calls=%async_computation.9 | async-start | bytes 2359296 | tf_op jit(solution)/shard_map/all_gather | solution.py:217
  548.0 109.6 %all-gather.14.cloned.1.call-start = ((), (), s32[]{:S(2)}) async-start(), calls=%async_computation.11 | async-start | bytes 2359296 | tf_op jit(solution)/shard_map/all_gather | solution.py:237
  548.6 202.5 %reduce-scatter.11.cloned.1.call-start = ((), (), s32[]{:S(2)}) async-start(), calls=%async_computation.12 | async-start | bytes 4718592 | tf_op jit(solution)/shard_map/reduce_scatter | solution.py:243
  657.7 6.2 copy-start.18
  662.9 1.0 copy-start.20
  667.1 171.5 %reduce-scatter.9.cloned.1.call-start = ((), (), s32[]{:S(2)}) async-start(), calls=%async_computation.10 | async-start | bytes 4718592 | tf_op jit(solution)/shard_map/reduce_scatter | solution.py:225
  672.2 0.7 copy-start.15
  672.2 168.5 %copy-start.4 = (bf16[128,1024]{1,0:T(8,128)(2,1)S(1)}, bf16[128,1024]{1,0:T(8,128)(2,1)}, u32[]{:S(2)}) copy-start(bf16[128,1024]{1,0:T(8,128)(2,1)} %param.41) | copy-start | bytes 786436
  672.2 222.9 %all-gather.16.cloned.1.call-start = ((), (), s32[]{:S(2)}) async-start(), calls=%async_computation.13 | async-start | bytes 2359296 | tf_op jit(solution)/shard_map/all_gather | solution.py:254
  752.4 142.7 %copy-start.9 = (bf16[128,1024]{1,0:T(8,128)(2,1)S(1)}, bf16[128,1024]{1,0:T(8,128)(2,1)}, u32[]{:S(2)}) copy-start(bf16[128,1024]{1,0:T(8,128)(2,1)} %param.33) | copy-start | bytes 786436
  841.6 712.3 %reduce-scatter.15.cloned.1.call-start = ((), (), s32[]{:S(2)}) async-start(), calls=%async_computation.15 | async-start | bytes 8912896 | tf_op jit(solution)/shard_map/reduce_scatter | solution.py:302
  1125.0 529.2 %reduce-scatter.13.cloned.1.call-start = ((), (), s32[]{:S(2)}) async-start(), calls=%async_computation.14 | async-start | bytes 8912896 | tf_op jit(solution)/shard_map/reduce_scatter | solution.py:301
  1134.1 610.6 %reduce-scatter.17.cloned.1.call-start = ((), (), s32[]{:S(2)}) async-start(), calls=%async_computation.16 | async-start | bytes 4718592 | tf_op jit(solution)/shard_map/reduce_scatter | solution.py:313
  1659.9 245.9 %all-reduce.5.cloned.1.call-start = ((), (), s32[]{:S(2)}) async-start(), calls=%async_computation.18 | async-start | bytes 12582912 | tf_op jit(solution)/shard_map/psum | solution.py:329
  1660.2 4.6 copy-start.17
  1660.3 4.6 copy-start.21
  1664.9 2.7 copy-start.3
  1673.5 73.8 %copy-start.5 = (bf16[128,1024]{1,0:T(8,128)(2,1)S(1)}, bf16[128,1024]{1,0:T(8,128)(2,1)}, u32[]{:S(2)}) copy-start(bf16[128,1024]{1,0:T(8,128)(2,1)} %param.41) | copy-start | bytes 786436
  1905.8 2.8 copy-start.11
  1905.8 3.6 copy-start.7
  1909.4 2.3 copy-start.6
  1909.4 3.7 copy-start.1
Sparse Core Ops, SparseCore 0:
  13.0 56.9 all-gather.7
  73.9 37.7 all-gather.17
  113.9 37.5 all-gather.9
  338.1 207.5 reduce-scatter.6
  548.5 53.2 all-gather.11
  604.0 53.6 all-gather.13
  667.2 83.8 reduce-scatter.10
  755.0 83.5 reduce-scatter.8
  841.8 53.3 all-gather.15
  1125.1 428.6 reduce-scatter.14
  1556.3 97.8 reduce-scatter.12
  1660.1 84.5 reduce-scatter.16
  1748.6 157.1 all-reduce.4
where the time goes:
time: 1930 us; the launch traced here: 1920 us
  waiting for transfers between devices  1290 us (67%)
  local copies, waits for them, and re-layouts  192 us (10%)
  loops' own time  174 us (9%)
  blocking collectives  116 us (6%)
  matrix products  77.2 us (4%)
  other arithmetic  59.7 us (3%)
    reduce_scatter x1, waiting for transfers between devices, on_device(): lax.psum_scatter(value_buffer, 'ctx', scatter_dimension=0, tiled=True)  420 us
    reduce_scatter x1, waiting for transfers between devices, on_device(): lax.psum_scatter(jnp.dot(take_rows(attended, jnp.int32(0), tok_dev * lax....  207 us
    another operation x2, loops' own time, over_blocks(): return lax.fori_loop(0, total_rows // block_rows, advance, carried)  169 us
    reduce_scatter x1, waiting for transfers between devices, on_device(): lax.psum_scatter(key_buffer, 'ctx', scatter_dimension=0, tiled=True)  100 us
    psum x1, waiting for transfers between devices, on_device(): lax.psum((grad_qkv_weight, grad_qv_bias, grad_out_weight, grad_up_weight,...  87.4 us
    reduce_scatter x1, waiting for transfers between devices, on_device(): lax.psum_scatter(jnp.dot(take_rows(active, jnp.int32(0), tok_dev * lax.ax...  86.1 us
    reduce_scatter x1, waiting for transfers between devices, on_device(): lax.psum_scatter(contract_cols(take_rows(grad_hidden, jnp.int32(0), tok_d...  78.2 us
    psum x1, blocking collectives, on_device(): lax.psum((grad_ln1_gain, grad_ln1_shift, grad_out_bias, grad_ln2_gain, gr...  68.9 us
  transfers between devices with their start and end apart: 13, of which 13 were waited for; matrix products, arithmetic and copies ran while one was open for 2% of the time, Pallas kernels for 0%

commit v1 on v0

v1 whole, which is shorter than its diff:
```python
import functools

import jax
import jax.numpy as jnp
from jax import lax
from jax.experimental import pallas as pl
from jax.experimental.pallas import tpu as pltpu
from jax.sharding import Mesh
from jax.sharding import PartitionSpec as P

HEAD_DIM = 64
EPSILON = 1e-05
MASKED = -1e30
LOG2E = 1.4426950408889634
TO_LOG2 = LOG2E * HEAD_DIM ** (-0.5)
AXES = ("x", "zl", "co", "y", "zh")
BF16, F32 = jnp.bfloat16, jnp.float32
SLICE = 1024
FWD_Q, FWD_K = 1024, 1024
BWD_Q, BWD_K = 512, 1024


def layer_norm(values, norm_gain, norm_shift):
    average = jnp.mean(values, axis=-1, keepdims=True)
    centered = values - average
    variance = jnp.mean(centered * centered, axis=-1, keepdims=True)
    return centered * lax.rsqrt(variance + EPSILON) * norm_gain + norm_shift


def gelu_tanh(values):
    return (
        0.5
        * values
        * (1.0 + jnp.tanh(0.7978845608028654 * (values + 0.044715 * values * values * values)))
    )


def contract(left, right, left_dim, right_dim):
    return lax.dot_general(
        left, right, (((left_dim,), (right_dim,)), ((), ())), preferred_element_type=F32
    )


def matmul(left, right):
    return contract(left, right, 1, 0)


def shift(values, axis, steps):
    return lax.ppermute(values, axis, [(i, (i + steps) % 4) for i in range(4)])


def swap(values, axis):
    return lax.ppermute(values, axis, [(0, 1), (1, 0)])


def mirror(values):
    return lax.ppermute(values, ("x", "co"), [(i, 7 - i) for i in range(8)])


def exchange(blocks, axes):
    return lax.all_to_all(blocks, axes, 0, 0, tiled=True)


def gather_y(rows):
    out = exchange(jnp.broadcast_to(rows[None], (4,) + rows.shape), "y")
    return out.reshape((4 * rows.shape[0],) + rows.shape[1:])


def scatter_y(partial):
    parts = exchange(partial.astype(BF16).reshape(4, -1, partial.shape[1]), "y")
    return jnp.sum(parts.astype(F32), axis=0)


def in_order(own, other, index):
    return jnp.where(index == 0, jnp.stack([own, other]), jnp.stack([other, own]))


def to_z(rows):
    n = rows.shape[-1]
    return rows.reshape(2, 4, 2, 128, n).transpose(0, 2, 1, 3, 4).reshape(4, 512, n)


def from_z(blocks):
    n = blocks.shape[-1]
    return blocks.reshape(2, 2, 4, 128, n).transpose(0, 2, 1, 3, 4).reshape(2, SLICE, n)


def pack(blocks):
    half = blocks.shape[1] // 2
    return jnp.concatenate([blocks[:, :half], blocks[:, half:]], axis=2)


def unpack(blocks):
    return jnp.concatenate([blocks[..., :HEAD_DIM], blocks[..., HEAD_DIM:]], axis=1)


def forward_kernel(spot, q_ref, end_ref, *refs):
    pieces, (out_t, out, lse_ref, kv_ref, vt_ref, qt_ref, sems) = refs[:10], refs[10:]
    x, core = spot[0], spot[1]
    copies = []

    def bring(piece, half, x_from, slice_in_x, parity):
        where = (4 * x_from + 2 * slice_in_x + parity) * SLICE
        copy = pltpu.make_async_copy(
            piece.at[pl.ds(half * SLICE, SLICE), :],
            kv_ref.at[pl.ds(pl.multiple_of(where, SLICE), SLICE), :],
            sems.at[len(copies)],
        )
        copy.start()
        copies.append(copy)

    for side in range(2):
        parity = core if side == 0 else 1 - core
        own, before, after, far_first, far_second = pieces[5 * side : 5 * side + 5]
        for half in range(2):
            bring(own, half, x, half, parity)
            bring(before, half, lax.rem(x + 3, 4), half, parity)
            bring(after, half, lax.rem(x + 1, 4), half, parity)
        bring(far_first, 0, lax.rem(x + 2, 4), 0, parity)
        bring(far_second, 0, lax.rem(x + 2, 4), 1, parity)
    qt_ref[...] = q_ref[...].T
    vt_ref[HEAD_DIM:, :] = jnp.ones((16, vt_ref.shape[1]), BF16)
    for copy in copies:
        copy.wait()

    @pl.loop(0, 16)
    def _(i):
        rows = pl.ds(pl.multiple_of(i * SLICE, SLICE), SLICE)
        vt_ref[:HEAD_DIM, rows] = kv_ref[rows, :].T[HEAD_DIM:, :]

    parts = 2
    wide = FWD_Q // parts
    for tile in range(2 * SLICE // FWD_Q):
        spans = [pl.ds(tile * FWD_Q + j * wide, wide) for j in range(parts)]
        queries = [qt_ref[:, span] for span in spans]
        ends = [end_ref[:, span] for span in spans]

        def step(masked, at, carry):
            rows = pl.ds(pl.multiple_of(at * FWD_K, FWD_K), FWD_K)
            kv, vt = kv_ref[rows, :], vt_ref[:, rows]
            scores = [matmul(kv, query) for query in queries]
            after = []
            for (top, total), score, end in zip(carry, scores, ends):
                if masked:
                    place = at * FWD_K + lax.broadcasted_iota(jnp.int32, score.shape, 0)
                    score = jnp.where(place < end, score, MASKED)
                new_top = jnp.maximum(top, jnp.max(score, axis=0, keepdims=True))
                weights = jnp.exp2(score * TO_LOG2 - new_top * TO_LOG2)
                factor = jnp.exp2((top - new_top) * TO_LOG2)
                total = total * factor + matmul(vt, weights.astype(BF16))
                after.append((new_top, total))
            return tuple(after)

        start = (jnp.full((1, wide), MASKED, F32), jnp.zeros((HEAD_DIM + 16, wide), F32))
        full, last = spot[2 + 2 * tile], spot[3 + 2 * tile]
        carry = lax.fori_loop(0, full, functools.partial(step, False), (start,) * parts)
        carry = lax.fori_loop(full, last, functools.partial(step, True), carry)
        for (top, total), span in zip(carry, spans):
            weight_sum = total[HEAD_DIM : HEAD_DIM + 1]
            mixed = total[:HEAD_DIM] / weight_sum
            out_t[:, span] = mixed
            out[span, :] = mixed.T.astype(BF16)
            lse_ref[:, span] = top * TO_LOG2 + jnp.log2(weight_sum)


def attention_forward(spot, padded_q, end, pieces):
    rows, total = 2 * SLICE, 16 * SLICE
    whole = pl.BlockSpec(memory_space=pltpu.VMEM)
    return pl.pallas_call(
        forward_kernel,
        out_shape=[
            jax.ShapeDtypeStruct((HEAD_DIM, rows), F32),
            jax.ShapeDtypeStruct((rows, HEAD_DIM), BF16),
            jax.ShapeDtypeStruct((1, rows), F32),
            jax.ShapeDtypeStruct((total, 2 * HEAD_DIM), BF16),
        ],
        in_specs=[pl.BlockSpec(memory_space=pltpu.SMEM), whole, whole]
        + [pl.BlockSpec(memory_space=pl.ANY)] * 10,
        out_specs=[whole] * 4,
        scratch_shapes=[
            pltpu.VMEM((HEAD_DIM + 16, total), BF16),
            pltpu.VMEM((2 * HEAD_DIM, rows), BF16),
            pltpu.SemaphoreType.DMA((16,)),
        ],
        compiler_params=pltpu.CompilerParams(vmem_limit_bytes=40 << 20),
        cost_estimate=pl.CostEstimate(
            flops=40_000_000_000, bytes_accessed=9 << 20, transcendentals=16 << 20
        ),
        name="attention_forward",
    )(spot, padded_q, end, *pieces)


def backward_kernel(spot, qdo_ref, out_t, lse_ref, end_ref, kv_ref, dq_ref, own_ref, other_ref, *rest):
    kt_ref, q_ref, do_ref, qt_ref, dot_ref, sum_ref = rest
    core = spot[1]
    first = lax.broadcasted_iota(jnp.int32, qdo_ref.shape, 1) < HEAD_DIM
    both = qdo_ref[...]
    none = jnp.zeros_like(both)
    q_ref[...] = jnp.where(first, both, none)
    do_ref[...] = jnp.where(first, none, both)
    qt_ref[...] = q_ref[...].T
    dot_ref[...] = do_ref[...].T

    @pl.loop(0, 16)
    def _(i):
        rows = pl.ds(pl.multiple_of(i * SLICE, SLICE), SLICE)
        kt_ref[:, rows] = kv_ref[rows, :].T[:HEAD_DIM, :]
        sum_ref[rows, :] = jnp.zeros((SLICE, 2 * HEAD_DIM), F32)

    for tile in range(2 * SLICE // BWD_Q):
        span = pl.ds(tile * BWD_Q, BWD_Q)
        query_t, grad_t = qt_ref[:, span], dot_ref[:, span]
        query, grad = q_ref[span, :], do_ref[span, :]
        end, lse = end_ref[:, span], lse_ref[:, span]
        delta = jnp.sum(out_t[:, span] * grad_t[HEAD_DIM:].astype(F32), axis=0, keepdims=True)

        def step(masked, at, grad_query):
            rows = pl.ds(pl.multiple_of(at * BWD_K, BWD_K), BWD_K)
            kv = kv_ref[rows, :]
            weights = jnp.exp2(matmul(kv, query_t) * TO_LOG2 - lse)
            if masked:
                place = at * BWD_K + lax.broadcasted_iota(jnp.int32, weights.shape, 0)
                weights = jnp.where(place < end, weights, 0.0)
            grad_scores = (weights * (matmul(kv, grad_t) - delta)).astype(BF16)
            sum_ref[rows, :] += matmul(weights.astype(BF16), grad) + matmul(grad_scores, query)
            return grad_query + matmul(kt_ref[:, rows], grad_scores)

        full, last = spot[2 + 2 * tile], spot[3 + 2 * tile]
        grad_query = jnp.zeros((HEAD_DIM, BWD_Q), F32)
        grad_query = lax.fori_loop(0, full, functools.partial(step, False), grad_query)
        grad_query = lax.fori_loop(full, last, functools.partial(step, True), grad_query)
        dq_ref[span, :] = (grad_query * HEAD_DIM ** (-0.5)).T.astype(BF16)

    is_key = lax.broadcasted_iota(jnp.int32, (1, 2 * HEAD_DIM), 1) < HEAD_DIM
    scale = jnp.where(is_key, HEAD_DIM ** (-0.5), 1.0)

    @pl.loop(0, 8)
    def _(i):
        to = pl.ds(pl.multiple_of(i * SLICE, SLICE), SLICE)
        for ref, parity in ((own_ref, core), (other_ref, 1 - core)):
            rows = pl.ds(pl.multiple_of((2 * i + parity) * SLICE, SLICE), SLICE)
            ref[to, :] = (sum_ref[rows, :] * scale).astype(BF16)


def attention_backward(spot, queries_grads, out_t, lse, end, kv):
    rows, total, wide = 2 * SLICE, 16 * SLICE, 2 * HEAD_DIM
    whole = pl.BlockSpec(memory_space=pltpu.VMEM)
    return pl.pallas_call(
        backward_kernel,
        out_shape=[
            jax.ShapeDtypeStruct((rows, HEAD_DIM), BF16),
            jax.ShapeDtypeStruct((total // 2, wide), BF16),
            jax.ShapeDtypeStruct((total // 2, wide), BF16),
        ],
        in_specs=[pl.BlockSpec(memory_space=pltpu.SMEM)] + [whole] * 5,
        out_specs=[whole] * 3,
        scratch_shapes=[
            pltpu.VMEM((HEAD_DIM, total), BF16),
            pltpu.VMEM((rows, wide), BF16),
            pltpu.VMEM((rows, wide), BF16),
            pltpu.VMEM((wide, rows), BF16),
            pltpu.VMEM((wide, rows), BF16),
            pltpu.VMEM((total, wide), F32),
        ],
        compiler_params=pltpu.CompilerParams(vmem_limit_bytes=48 << 20),
        cost_estimate=pl.CostEstimate(
            flops=60_000_000_000, bytes_accessed=9 << 20, transcendentals=16 << 20
        ),
        name="attention_backward",
    )(spot, queries_grads, out_t, lse, end, kv)


def all_ids(block_ids, place):
    table = jnp.zeros((16, SLICE), jnp.int32)
    table = lax.dynamic_update_slice(table, block_ids[None], (place, 0))
    table = table + swap(table, "co")
    table = table + swap(table, "zl")
    table = table + lax.ppermute(table, "x", [(i, i ^ 1) for i in range(4)])
    return table + lax.ppermute(table, "x", [(i, i ^ 2) for i in range(4)])


def tile_bounds(end, query_tile, key_tile):
    ends = end.reshape(-1, query_tile)
    return jnp.stack([ends[:, 0] // key_tile, (ends[:, -1] + key_tile - 1) // key_tile], axis=1)


def core_half(parts, core):
    kept = lax.dynamic_index_in_dim(parts, core, 1, False)
    sent = lax.dynamic_index_in_dim(parts, 1 - core, 1, False)
    return kept.astype(F32) + swap(sent, "co").astype(F32)


def zh_half(parts, zh):
    parts = parts.astype(BF16)
    kept = lax.dynamic_index_in_dim(parts, zh, 0, False)
    sent = lax.dynamic_index_in_dim(parts, 1 - zh, 0, False)
    return (kept.astype(F32) + swap(sent, "zh").astype(F32)).astype(BF16)


def on_device(
    tokens,
    block_ids,
    ln1_gain,
    ln1_shift,
    qkv_weight,
    qv_bias,
    out_weight,
    out_bias,
    ln2_gain,
    ln2_shift,
    up_weight,
    up_bias,
    down_weight,
    down_bias,
    cotangent,
):
    x, zl, core, zh = (lax.axis_index(name) for name in ("x", "zl", "co", "zh"))
    width = tokens.shape[1]

    qkv_pair = in_order(qkv_weight, swap(qkv_weight, "zh"), zh)
    bias_pair = in_order(qv_bias, swap(qv_bias, "zh"), zh).astype(F32)
    up_pair = lax.all_gather(up_weight, "zh", axis=0)
    down_pair = lax.all_gather(down_weight, "zh", axis=0, tiled=True)
    up_bias_pair = in_order(up_bias, swap(up_bias, "zh"), zh).astype(F32).reshape(-1)
    out_whole = lax.all_gather(out_weight, ("y", "zh"), axis=0, tiled=True)
    cotangent_all = lax.all_gather(cotangent, "y", axis=0, tiled=True)

    by_head = qkv_pair.reshape(2, width, 3, 2, HEAD_DIM)
    kv_cols = jnp.stack([by_head[:, :, 1], by_head[:, :, 2]], axis=3)
    kv_cols = kv_cols.transpose(1, 2, 0, 3, 4).reshape(width, 512)
    q_cols = by_head[:, :, 0].transpose(1, 2, 0, 3).reshape(width, 256)
    flat_qkv = jnp.concatenate([kv_cols, q_cols], axis=1)
    bias_heads = bias_pair.reshape(2, 2, 2, HEAD_DIM).transpose(1, 2, 0, 3)
    kv_bias = jnp.stack([jnp.zeros_like(bias_heads[1]), bias_heads[1]], axis=2).reshape(512)
    flat_bias = jnp.concatenate([kv_bias, bias_heads[0].reshape(256)])

    table = all_ids(block_ids, 4 * x + 2 * zl + core)
    counts = jnp.sum(
        (table.reshape(-1)[None, :] <= jnp.arange(128, dtype=jnp.int32)[:, None]).astype(jnp.int32),
        axis=1,
    )
    early = lax.dynamic_index_in_dim(table, 4 * x + core, 0, False)
    late = lax.dynamic_index_in_dim(table, 15 - 4 * x - core, 0, False)
    query_ids = jnp.concatenate([early, late])
    same = query_ids[None, :] == jnp.arange(128, dtype=jnp.int32)[:, None]
    end = jnp.sum(jnp.where(same, counts[:, None], 0), axis=0)
    spot = jnp.stack([x, core]).astype(jnp.int32)
    forward_spot = jnp.concatenate([spot, tile_bounds(end, FWD_Q, FWD_K).reshape(-1)])
    backward_spot = jnp.concatenate([spot, tile_bounds(end, BWD_Q, BWD_K).reshape(-1)])
    end = end[None, :]

    gain_one, shift_one = ln1_gain.astype(F32), ln1_shift.astype(F32)
    tokens_all = gather_y(tokens).astype(F32)
    centered = tokens_all - jnp.mean(tokens_all, axis=-1, keepdims=True)
    spread = lax.rsqrt(jnp.mean(centered * centered, axis=-1, keepdims=True) + EPSILON)
    unit_all = centered * spread
    normed_all = (unit_all * gain_one + shift_one).astype(BF16)
    projected = (matmul(normed_all, flat_qkv) + flat_bias).astype(BF16)
    kv_blocks = projected[:, :512].reshape(512, 4, 128).transpose(1, 0, 2)
    q_blocks = projected[:, 512:].reshape(512, 4, HEAD_DIM).transpose(1, 0, 2)
    mine = exchange(jnp.concatenate([kv_blocks, pack(q_blocks)], axis=1), ("zl", "zh"))
    queries = from_z(unpack(mine[:, 512:]))
    queries = jnp.concatenate([queries[0], mirror(queries[1])], axis=0)
    kv_own = from_z(mine[:, :512]).reshape(2 * SLICE, 128)

    before, after = shift(kv_own, "x", 1), shift(kv_own, "x", -1)
    far_first, far_second = shift(before[:SLICE], "x", 1), shift(after[SLICE:], "x", -1)
    pieces = [kv_own, before, after, far_first, far_second]
    pieces += [swap(piece, "co") for piece in pieces]
    padded = jnp.pad(queries, ((0, 0), (0, HEAD_DIM)))
    out_t, mixed, lse, kv = attention_forward(forward_spot, padded, end, pieces)

    mixed = jnp.stack([mixed[:SLICE], mirror(mixed[SLICE:])])
    by_z = unpack(exchange(pack(to_z(mixed)), ("zl", "zh")))
    attended_all = (
        by_z.reshape(2, 2, 512, HEAD_DIM).transpose(2, 1, 0, 3).reshape(512, 256)
    )
    attended = exchange(attended_all.reshape(4, 128, 256), "y")
    branch = lax.dot_general(
        attended,
        out_whole.reshape(4, 256, width),
        (((0, 2), (0, 1)), ((), ())),
        preferred_element_type=F32,
    )
    resid = tokens.astype(F32) + branch + out_bias.astype(F32)
    normed_mid, norm_two_back = jax.vjp(
        layer_norm, resid, ln2_gain.astype(F32), ln2_shift.astype(F32)
    )

    mid_all = gather_y(normed_mid.astype(BF16))
    up_cols = up_pair.transpose(1, 0, 2).reshape(width, 1024)
    hidden = matmul(mid_all, up_cols) + up_bias_pair
    active_wide, gelu_back = jax.vjp(gelu_tanh, hidden)
    active = active_wide.astype(BF16)
    grad_active = contract(cotangent_all, down_pair, 1, 1)
    grad_hidden = gelu_back(grad_active)[0].astype(BF16)
    grad_mid = scatter_y(contract(grad_hidden, up_cols, 1, 1))
    down_partial = matmul(active, down_pair).astype(BF16)
    down_sum = lax.psum_scatter(down_partial, "y", scatter_dimension=0, tiled=True)
    output = resid + down_sum.astype(F32) + down_bias.astype(F32)
    grad_down = contract(active, cotangent_all, 0, 0)
    grad_up = contract(mid_all, grad_hidden, 0, 0)
    grad_up_bias = jnp.sum(grad_hidden.astype(F32), axis=0)

    grad_resid_norm, grad_ln2_gain, grad_ln2_shift = norm_two_back(grad_mid)
    grad_resid = cotangent.astype(F32) + grad_resid_norm
    grad_branch = grad_resid.astype(BF16)
    grad_branch_all = lax.all_gather(grad_branch, "y", axis=0, tiled=True)

    grad_down = core_half(grad_down.astype(BF16).reshape(2, 2, 256, width), core)
    grad_up = grad_up.astype(BF16).reshape(2, 512, 2, 512).transpose(2, 0, 1, 3)
    grad_up = core_half(grad_up, core)
    grad_down, grad_up = zh_half(grad_down, zh), zh_half(grad_up, zh)
    grad_down, grad_up = lax.psum((grad_down, grad_up), ("x", "zl"))

    grad_attended = contract(grad_branch, out_whole, 1, 1).astype(BF16)
    grad_y = exchange(grad_attended.reshape(128, 4, 256).transpose(1, 0, 2), "y")
    grad_z = grad_y.reshape(512, 2, 2, HEAD_DIM).transpose(2, 1, 0, 3).reshape(4, 512, HEAD_DIM)
    grad_mixed = from_z(unpack(exchange(pack(grad_z), ("zl", "zh"))))
    grad_mixed = jnp.concatenate([grad_mixed[0], mirror(grad_mixed[1])], axis=0)
    queries_grads = jnp.concatenate([queries, grad_mixed], axis=1)
    grad_q, grad_kv, grad_kv_other = attention_backward(
        backward_spot, queries_grads, out_t, lse, end, kv
    )
    grad_q = jnp.stack([grad_q[:SLICE], mirror(grad_q[SLICE:])])
    grad_kv = (grad_kv.astype(F32) + swap(grad_kv_other, "co").astype(F32)).astype(BF16)
    grad_kv = exchange(grad_kv.reshape(4, 2 * SLICE, 128), "x").astype(F32)
    grad_kv = jnp.sum(grad_kv, axis=0).astype(BF16).reshape(2, SLICE, 128)
    blocks = jnp.concatenate([to_z(grad_kv), pack(to_z(grad_q))], axis=1)
    blocks = exchange(blocks, ("zl", "zh"))
    grad_projected = jnp.concatenate(
        [
            blocks[:, :512].transpose(1, 0, 2).reshape(512, 512),
            unpack(blocks[:, 512:]).transpose(1, 0, 2).reshape(512, 256),
        ],
        axis=1,
    )
    grad_normed_part = contract(grad_projected, flat_qkv, 1, 1)
    grad_qkv = contract(normed_all, grad_projected, 0, 0)
    grad_bias = jnp.sum(grad_projected.astype(F32), axis=0)
    grad_out = contract(attended_all, grad_branch_all, 0, 0)
    part_gain = jnp.sum(grad_normed_part * unit_all, axis=0)
    part_shift = jnp.sum(grad_normed_part, axis=0)
    grad_normed = scatter_y(grad_normed_part)
    _, norm_one_back = jax.vjp(
        lambda v: layer_norm(v, gain_one, shift_one), tokens.astype(F32)
    )
    grad_tokens = grad_resid + norm_one_back(grad_normed)[0]

    kv_bias_grad = grad_bias[:512].reshape(2, 2, 2, HEAD_DIM)[:, :, 1]
    q_bias_grad = grad_bias[512:].reshape(2, 2, HEAD_DIM)
    bias_grad = jnp.stack([q_bias_grad, kv_bias_grad]).transpose(2, 0, 1, 3).reshape(512)
    quarter = 0.25 * jnp.sum(cotangent_all.astype(F32), axis=0)
    rows = [
        part_gain,
        part_shift,
        jnp.sum(grad_resid, axis=0),
        grad_ln2_gain,
        grad_ln2_shift,
        quarter,
        grad_up_bias,
        jnp.pad(bias_grad, (0, 512)),
    ]
    small = jnp.stack(rows)
    for axis in ("co", "zl", "zh"):
        small = small + swap(small, axis)
    for step in (1, 2):
        small = small + lax.ppermute(small, "x", [(i, i ^ step) for i in range(4)])
    tall = small[:6]
    for step in (1, 2):
        tall = tall + lax.ppermute(tall, "y", [(i, i ^ step) for i in range(4)])
    grad_up_bias = lax.dynamic_slice_in_dim(small[6], zh * 512, 512, 0)
    grad_qv_bias = lax.dynamic_slice_in_dim(small[7], zh * 256, 256, 0).reshape(2, 128)

    qkv_kv = grad_qkv[:, :512].reshape(2, 512, 2, 2, 2, HEAD_DIM)
    qkv_q = grad_qkv[:, 512:].reshape(2, 512, 2, 2, HEAD_DIM)
    qkv_all = jnp.concatenate([qkv_q[:, :, :, :, None], qkv_kv], axis=4).astype(BF16)
    qkv_all = qkv_all.transpose(3, 0, 4, 1, 2, 5).reshape(2, 2, 1536, 128)
    out_all = grad_out.astype(BF16).reshape(2, 2, 64, 8, 128).transpose(0, 1, 3, 2, 4)
    rest = jnp.concatenate([qkv_all, out_all.reshape(2, 2, 512, 128)], axis=2)
    rest = zh_half(core_half(rest, core), zh)
    shares = exchange(rest.reshape(8, 256, 128), ("x", "zl"))
    share = jnp.sum(shares.astype(F32), axis=0).astype(BF16)
    rest = exchange(jnp.broadcast_to(share[None], (8, 256, 128)), ("x", "zl"))
    rest = in_order(rest, swap(rest, "co"), core).reshape(2, 2048, 128).astype(F32)
    grad_qkv_weight = rest[:, :1536].reshape(2, 3, 512, 128).transpose(0, 2, 1, 3)
    grad_qkv_weight = grad_qkv_weight.reshape(width, 3, 128)
    grad_out_weight = rest[:, 1536:].reshape(2, 8, 64, 128).transpose(0, 2, 1, 3)
    grad_out_weight = grad_out_weight.reshape(128, width)
    grad_down_weight = in_order(grad_down, swap(grad_down, "co"), core)
    grad_down_weight = grad_down_weight.reshape(512, width).astype(F32)
    grad_up_weight = in_order(grad_up, swap(grad_up, "co"), core)
    grad_up_weight = grad_up_weight.reshape(width, 512).astype(F32)
    return (
        output,
        grad_tokens,
        tall[0],
        tall[1],
        grad_qkv_weight,
        grad_qv_bias,
        grad_out_weight,
        tall[2],
        tall[3],
        tall[4],
        grad_up_weight,
        grad_up_bias,
        grad_down_weight,
        tall[5],
    )


def solution(mesh):
    fine = Mesh(mesh.devices.reshape(4, 2, 2, 4, 2), AXES)
    slices, shards = ("x", "zl", "co"), ("y", "zh")
    return jax.shard_map(
        on_device,
        mesh=fine,
        in_specs=(
            P(AXES, None),
            P(slices),
            P(),
            P(),
            P(None, None, shards),
            P(None, shards),
            P(shards, None),
            P(),
            P(),
            P(),
            P(None, shards),
            P(shards),
            P(shards, None),
            P(),
            P(AXES, None),
        ),
        out_specs=(
            P(AXES, None),
            P(AXES, None),
            P(),
            P(),
            P(None, None, shards),
            P(None, shards),
            P(shards, None),
            P(),
            P(),
            P(),
            P(None, shards),
            P(shards),
            P(shards, None),
            P(),
        ),
        check_vma=False,
    )
```

time: 1930 us -> 589 us (0.31)
  waiting for transfers between devices: 1290 us -> 206 us
  loops' own time: 174 us -> 0 us
  local copies, waits for them, and re-layouts: 192 us -> 60.8 us
  starting transfers between devices: 1.2 us -> 114 us
  blocking collectives: 116 us -> 12.9 us
  Pallas kernels: 0 us -> 100 us
  matrix products: 77.2 us -> 30.8 us
  other arithmetic: 59.7 us -> 37.8 us
    reduce_scatter x6 -> x1, waiting for transfers between devices: 936 us -> 0.02 us  [on_device(): lax.psum_scatter(down_partial, 'y', scatter_dimension=0, tiled=True)]
    all_gather x6 -> x5, waiting for transfers between devices: 262 us -> 2.93 us  [the longest x1 2.88 us: on_device(): cotangent_all = lax.all_gather(cotangent, 'y', axis=0, tiled=True)]
    another operation x130 -> x0, loops' own time: 174 us -> none  [the longest x2 169 us: over_blocks(): return lax.fori_loop(0, total_rows // block_rows, advance, carried)]
    pallas_call x0 -> x2, Pallas kernels: none -> 100 us  [the longest x1 58 us: attention_backward(): pl.pallas_call(backward_kernel, out_shape=[jax.ShapeDtypeStruct((rows, HE...]
    psum x2 -> x0, blocking collectives: 95.5 us -> none  [the longest x1 68.9 us: on_device(): lax.psum((grad_ln1_gain, grad_ln1_shift, grad_out_bias, grad_ln2_gain, gr...]
    ppermute x0 -> x37, waiting for transfers between devices: none -> 82.3 us  [the longest x4 30.7 us: mirror(): return lax.ppermute(values, ('x', 'co'), [(i, 7 - i) for i in range(8)])]
    all_to_all x0 -> x12, waiting for transfers between devices: none -> 73.4 us  [exchange(): return lax.all_to_all(blocks, axes, 0, 0, tiled=True)]
    ppermute x0 -> x37, starting transfers between devices: none -> 65.7 us  [the longest x23 33.5 us: swap(): return lax.ppermute(values, axis, [(0, 1), (1, 0)])]
  transfers between devices with their start and end apart: 13 -> 56, of which waited for: 13 -> 28; matrix products, arithmetic and copies ran while one was open for 2% -> 19% of each run, Pallas kernels for 0% -> 7%
where the time goes in v1:
time: 589 us; the launch traced here: 579 us
  waiting for transfers between devices  206 us (35%)
  starting transfers between devices  114 us (19%)
  Pallas kernels  100 us (17%)
  local copies, waits for them, and re-layouts  60.8 us (10%)
  other arithmetic  37.8 us (6%)
  matrix products  30.8 us (5%)
  between operations  16.1 us (3%)
  blocking collectives  12.9 us (2%)
    all_to_all x12, waiting for transfers between devices, exchange(): return lax.all_to_all(blocks, axes, 0, 0, tiled=True)  73.4 us
    pallas_call x1, Pallas kernels, attention_backward(): pl.pallas_call(backward_kernel, out_shape=[jax.ShapeDtypeStruct((rows, HE...  58 us
    all_to_all x12, starting transfers between devices, exchange(): return lax.all_to_all(blocks, axes, 0, 0, tiled=True)  48.1 us
    psum x1, waiting for transfers between devices, on_device(): grad_down, grad_up = lax.psum((grad_down, grad_up), ('x', 'zl'))  45.6 us
    pallas_call x1, Pallas kernels, attention_forward(): pl.pallas_call(forward_kernel, out_shape=[jax.ShapeDtypeStruct((HEAD_DIM,...  42.4 us
    ppermute x23, starting transfers between devices, swap(): return lax.ppermute(values, axis, [(0, 1), (1, 0)])  33.5 us
    ppermute x4, waiting for transfers between devices, mirror(): return lax.ppermute(values, ('x', 'co'), [(i, 7 - i) for i in range(8)])  30.7 us
    dot_general x11, matrix products, contract(): lax.dot_general(left, right, (((left_dim,), (right_dim,)), ((), ())), pre...  28.7 us
  transfers between devices with their start and end apart: 56, of which 28 were waited for; matrix products, arithmetic and copies ran while one was open for 19% of the time, Pallas kernels for 7%

profile of v1, /device:TPU:1, one launch (start us, length us, event | category | flops | bytes accessed | tf_op | source)
XLA Modules:
  0.0 578.6 jit_solution(17196187959754134263)
XLA Ops:
  9.4 4.5 collective-permute-start.4
  16.8 4.2 all-to-all-start
  21.1 12.9 %collective-permute-done.5 = bf16[2,128]{1,0:T(2,128)(2,1)S(1)} collective-permute-done((bf16[2,128]{1,0:T(2,128)(2,1)}, bf16[2,128]{1,0:T(2,128)(2,1)S(1)}, u32[]{:S(2)}, u32[]{:S(2)}) %collective-permute-start.5) | collective-permute-done | bytes 544 | tf_op jit(solution)/shard_map/ppermute | solution.py:53
  35.8 2.8 all-to-all-done
  42.3 5.6 all-to-all-start.1
  49.2 2.3 collective-permute-done.2
  51.5 2.8 collective-permute-start.3
  54.4 2.2 collective-permute-done.3
  57.6 12.4 %all-to-all-done.1 = bf16[4,768,128]{2,1,0:T(8,128)(2,1)S(1)} async-done(((bf16[4,768,128]{2,1,0:T(8,128)(2,1)}), bf16[4,768,128]{2,1,0:T(8,128)(2,1)S(1)}, u32[]{:S(2)}, u32[]{:S(2)}) %all-to-all-start.1) | async-done | bytes 786464 | tf_op jit(solution)/shard_map/all_to_all | solution.py:61
  75.1 2.4 collective-permute-start.6
  77.9 6.4 %collective-permute-done.7.refs_1_ = bf16[2048,128]{1,0:T(8,128)(2,1)S(1)} collective-permute-done((bf16[2048,128]{1,0:T(8,128)(2,1)S(1)}, bf16[2048,128]{1,0:T(8,128)(2,1)S(1)}, u32[]{:S(2)}, u32[]{:S(2)}) %collective-permute-start.7) | collective-permute-done | bytes 524320 | tf_op jit(solution)/shard_map/ppermute | solution.py:49
  85.9 2.4 collective-permute-start.10
  88.3 3.3 collective-permute-start.12
  92.3 3.1 collective-permute-done.9.refs_3_
  99.5 42.4 %attention_forward.1 = (f32[64,2048]{1,0:T(8,128)S(1)}, bf16[2048,64]{1,0:T(8,128)(2,1)S(1)}, f32[1,2048]{1,0:T(1,128)S(1)}, bf16[16384,128]{1,0:T(8,128)(2,1)S(1)}) custom-call(s32[6]{0:T(128)S(1)} %pad_add_fusion.3.spot, bf16[2048,128]{1,0:T(8,128)(2,1)S(1)} %fusion.30.q_ref, s32[1,2048]{1,0:T(1,128)S(1)} %bitcast.236, bf16[2048,128]{1,0:T(8,128)(2,1)S(1)} %bitcast.235, ...), custom_call_target="tpu_custom_call" | custom-call | flops 40000000000 | bytes 9437184 | tf_op jit(solution)/shard_map/attention_forward/pallas_call | solution.py:169
  144.7 2.8 collective-permute-start.16
  147.7 6.5 %collective-permute-done.16 = bf16[1024,64]{1,0:T(8,128)(2,1)S(1)} collective-permute-done((bf16[1024,64]{1,0:T(8,128)(2,1)S(1)}, bf16[1024,64]{1,0:T(8,128)(2,1)S(1)}, u32[]{:S(2)}, u32[]{:S(2)}) %collective-permute-start.16) | collective-permute-done | bytes 131104 | tf_op jit(solution)/shard_map/ppermute | solution.py:57
  154.8 12.9 %all_to_all.65 = bf16[4,256,128]{1,2,0:T(8,128)(2,1)S(1)} all-to-all(bf16[4,256,128]{1,2,0:T(8,128)(2,1)S(1)} %pad_maximum_fusion.8), channel_id=1, replica_groups=mesh['x'=4,'zl'=2,'co'=2,'y'=4,'zh'=2] {'zl','zh'}, dimensions={0} | all-to-all | bytes 524288 | tf_op jit(solution)/shard_map/all_to_all | solution.py:61
  169.2 3.4 all-to-all-start.3
  172.7 6.2 %all-to-all-done.3 = bf16[4,128,256]{2,1,0:T(8,128)(2,1)S(1)} async-done(((bf16[4,128,256]{2,1,0:T(8,128)(2,1)}), bf16[4,128,256]{2,1,0:T(8,128)(2,1)S(1)}, u32[]{:S(2)}, u32[]{:S(2)}) %all-to-all-start.3) | async-done | bytes 262176 | tf_op jit(solution)/shard_map/all_to_all | solution.py:61
  179.0 2.1 fusion.63
  182.6 4.2 all-to-all-start.4
  187.8 3.9 collective-permute-done.17
  191.8 3.0 copy.187
  194.8 6.0 %all-to-all-done.4 = bf16[4,128,1024]{2,1,0:T(8,128)(2,1)} async-done(((bf16[4,128,1024]{2,1,0:T(8,128)(2,1)}), bf16[4,128,1024]{2,1,0:T(8,128)(2,1)}, u32[]{:S(2)}, u32[]{:S(2)}) %all-to-all-start.4) | async-done | bytes 1048608 | tf_op jit(solution)/shard_map/all_to_all | solution.py:61
  200.7 3.8 fusion.64
  204.6 4.7 convolution_convert_fusion.4
  209.3 2.9 all-gather.11.cloned.1.call-done
  212.2 5.4 convert_reduce_fusion.3
  217.6 2.2 convolution_convert_fusion.3
  219.9 3.6 all-to-all-start.5
  223.6 23.0 %all-to-all-done.5 = bf16[4,128,1024]{2,1,0:T(8,128)(2,1)S(1)} async-done(((bf16[4,128,1024]{2,1,0:T(8,128)(2,1)}), bf16[4,128,1024]{2,1,0:T(8,128)(2,1)S(1)}, u32[]{:S(2)}, u32[]{:S(2)}) %all-to-all-start.5) | async-done | bytes 1048608 | tf_op jit(solution)/shard_map/all_to_all | solution.py:61
  252.1 3.4 all-to-all-start.6
  255.5 5.5 all-to-all-done.6
  262.1 4.1 all-to-all-start.7
  266.3 5.2 all-to-all-done.7
  271.9 6.4 %collective-permute-start.18 = (bf16[1024,64]{1,0:T(8,128)(2,1)S(1)}, bf16[1024,64]{1,0:T(8,128)(2,1)S(1)}, u32[]{:S(2)}, u32[]{:S(2)}) collective-permute-start(bf16[1024,64]{1,0:T(8,128)(2,1)S(1)} %bitcast.290), channel_id=1, source_target_pairs={{0,104},{8,96},{32,72},{40,64},{64,40},{72,32},{96,8},{104,0},{1,1... | collective-permute-start | bytes 393224 | tf_op jit(solution)/shard_map/ppermute | solution.py:57
  278.7 6.6 %collective-permute-done.18 = bf16[1024,64]{1,0:T(8,128)(2,1)S(1)} collective-permute-done((bf16[1024,64]{1,0:T(8,128)(2,1)S(1)}, bf16[1024,64]{1,0:T(8,128)(2,1)S(1)}, u32[]{:S(2)}, u32[]{:S(2)}) %collective-permute-start.18) | collective-permute-done | bytes 131104 | tf_op jit(solution)/shard_map/ppermute | solution.py:57
  285.6 58.0 %attention_backward.1 = (bf16[2048,64]{1,0:T(8,128)(2,1)S(1)}, bf16[8192,128]{1,0:T(8,128)(2,1)S(1)}, bf16[8192,128]{1,0:T(8,128)(2,1)}) custom-call(s32[10]{0:T(128)S(1)} %pad_add_fusion.4.spot, bf16[2048,128]{1,0:T(8,128)(2,1)S(1)} %fusion.27.qdo_ref, f32[64,2048]{1,0:T(8,128)S(1)} %copy-done.2, f32[1,2048]{1,0:T(1,128)S(1)} %get-tuple-element.23.lse_ref, ...), custom_call_target="tpu_custom_call" | custom-call | flops 60000002048 | bytes 9437184 | tf_op jit(solution)/shard_map/attention_backward/pallas_call | solution.py:248
  343.8 4.2 convolution_convert_fusion.1
  348.0 4.5 reshape.418
  352.4 4.1 constant_dynamic-slice_fusion.2
  362.6 3.5 add_convert_fusion
  366.1 3.6 all-to-all-start.8
  375.3 3.2 collective-permute-start.20
  384.3 17.3 %collective-permute-done.20 = bf16[1024,64]{1,0:T(8,128)(2,1)S(1)} collective-permute-done((bf16[1024,64]{1,0:T(8,128)(2,1)}, bf16[1024,64]{1,0:T(8,128)(2,1)S(1)}, u32[]{:S(2)}, u32[]{:S(2)}) %collective-permute-start.20) | collective-permute-done | bytes 131104 | tf_op jit(solution)/shard_map/ppermute | solution.py:57
  403.7 2.1 maximum_maximum_fusion
  405.8 3.5 all-to-all-start.9
  415.8 5.8 all-to-all-done.9
  430.6 2.7 copy.204
  433.3 4.4 reshape.408
  439.2 45.6 %all-reduce.6.cloned.1.call-done = (bf16[512,512]{1,0:T(8,128)(2,1)}, bf16[256,1024]{1,0:T(8,128)(2,1)}) async-done(((bf16[512,512]{1,0:T(8,128)(2,1)}, bf16[256,1024]{1,0:T(8,128)(2,1)}), (bf16[512,512]{1,0:T(8,128)(2,1)}, bf16[256,1024]{1,0:T(8,128)(2,1)})) %all-reduce.6.cloned.1.call-update) | async-done | bytes 1048592 | tf_op jit(solution)/shard_map/psum | solution.py:414
  484.9 4.8 collective-permute-start.33
  492.0 2.8 collective-permute-start.29
  500.5 6.3 %collective-permute-done.22 = f32[8,1024]{1,0:T(8,128)S(1)} collective-permute-done((f32[8,1024]{1,0:T(8,128)S(1)}, f32[8,1024]{1,0:T(8,128)S(1)}, u32[]{:S(2)}, u32[]{:S(2)}) %collective-permute-start.22) | collective-permute-done | bytes 32800 | tf_op jit(solution)/shard_map/ppermute | solution.py:53
  510.7 3.5 all-to-all-start.11
  518.8 2.7 collective-permute-done.24
  521.5 2.4 collective-permute-start.25
  525.7 4.1 all-to-all-start.10
  532.0 8.5 %collective-permute-done.26 = f32[6,1024]{1,0:T(8,128)S(1)} collective-permute-done((f32[6,1024]{1,0:T(8,128)S(1)}, f32[6,1024]{1,0:T(8,128)S(1)}, u32[]{:S(2)}, u32[]{:S(2)}) %collective-permute-start.26) | collective-permute-done | bytes 24608 | tf_op jit(solution)/shard_map/ppermute | solution.py:471
  540.5 2.3 collective-permute-start.27
  547.2 4.8 all-to-all-start.12
  552.5 6.6 %all-to-all-done.12 = bf16[8,256,128]{2,1,0:T(8,128)(2,1)S(1)} async-done(((bf16[8,256,128]{2,1,0:T(8,128)(2,1)}), bf16[8,256,128]{2,1,0:T(8,128)(2,1)S(1)}, u32[]{:S(2)}, u32[]{:S(2)}) %all-to-all-start.12) | async-done | bytes 524320 | tf_op jit(solution)/shard_map/all_to_all | solution.py:61
  559.1 6.8 %collective-permute-start.30 = (bf16[8,256,128]{2,1,0:T(8,128)(2,1)S(1)}, bf16[8,256,128]{2,1,0:T(8,128)(2,1)S(1)}, u32[]{:S(2)}, u32[]{:S(2)}) collective-permute-start(bf16[8,256,128]{2,1,0:T(8,128)(2,1)S(1)} %all-to-all-done.12), channel_id=1, source_target_pairs={{0,8},{8,0},{1,9},{9,1},{2,10},{10,2},{3,11},{11,3},{4,12},{12,4},... | collective-permute-start | bytes 1572872 | tf_op jit(solution)/shard_map/ppermute | solution.py:53
  (378 shorter events, 106.8 us)
Async XLA Ops:
  7.2 171.8 %all-gather.7.cloned.1.call-start = ((), (), s32[]{:S(2)}) async-start(), calls=%async_computation.14 | async-start | bytes 2359296 | tf_op jit(solution)/shard_map/all_gather | solution.py:325
  9.4 24.9 %copy-start.41 = (s32[1024]{0:T(1024)S(1)}, s32[1024]{0:T(1024)}, u32[]{:S(2)}) copy-start(s32[1024]{0:T(1024)} %param.16) | copy-start | bytes 12292
  9.4 25.8 %collective-permute-start.4 = (bf16[1024,3,128]{0,2,1:T(8,128)(2,1)S(1)}, bf16[1024,3,128]{0,2,1:T(8,128)(2,1)S(1)}, u32[]{:S(2)}, u32[]{:S(2)}) collective-permute-start(bf16[1024,3,128]{0,2,1:T(8,128)(2,1)S(1)} %copy.166), channel_id=1, source_target_pairs={{0,1},{1,0},{2,3},{3,2},{4,5},{5,4},{6,7},{7,6},{8,9},{9,8},{10,11... | collective-permute-start | bytes 2359304 | tf_op jit(solution)/shard_map/ppermute | solution.py:53
  14.7 19.6 %collective-permute-start = (s32[16,1024]{1,0:T(8,128)S(1)}, s32[16,1024]{1,0:T(8,128)S(1)}, u32[]{:S(2)}, u32[]{:S(2)}) collective-permute-start(s32[16,1024]{1,0:T(8,128)S(1)} %dynamic_update_slice.5), channel_id=1, source_target_pairs={{0,8},{8,0},{1,9},{9,1},{2,10},{10,2},{3,11},{11,3},{4,12},{12,4},... | collective-permute-start | bytes 196616 | tf_op jit(solution)/shard_map/ppermute | solution.py:53
  15.7 18.3 %collective-permute-start.5 = (bf16[2,128]{1,0:T(2,128)(2,1)}, bf16[2,128]{1,0:T(2,128)(2,1)S(1)}, u32[]{:S(2)}, u32[]{:S(2)}) collective-permute-start(bf16[2,128]{1,0:T(2,128)(2,1)} %param.20), channel_id=1, source_target_pairs={{0,1},{1,0},{2,3},{3,2},{4,5},{5,4},{6,7},{7,6},{8,9},{9,8},{10,11... | collective-permute-start | bytes 1544 | tf_op jit(solution)/shard_map/ppermute | solution.py:53
  16.8 21.8 %all-to-all-start = ((bf16[4,128,1024]{2,1,0:T(8,128)(2,1)}), bf16[4,128,1024]{2,1,0:T(8,128)(2,1)S(1)}, u32[]{:S(2)}, u32[]{:S(2)}) async-start(bf16[4,128,1024]{2,1,0:T(8,128)(2,1)} %broadcast_in_dim.36), calls=%async_computation | async-start | bytes 2097152 | tf_op jit(solution)/shard_map/all_to_all | solution.py:61
  34.5 13.4 %collective-permute-start.1 = (s32[16,1024]{1,0:T(8,128)S(1)}, s32[16,1024]{1,0:T(8,128)S(1)}, u32[]{:S(2)}, u32[]{:S(2)}) collective-permute-start(s32[16,1024]{1,0:T(8,128)S(1)} %add.242), channel_id=1, source_target_pairs={{0,16},{16,0},{1,17},{17,1},{2,18},{18,2},{3,19},{19,3},{4,20},{20... | collective-permute-start | bytes 196616 | tf_op jit(solution)/shard_map/ppermute | solution.py:53
  42.3 27.7 %all-to-all-start.1 = ((bf16[4,768,128]{2,1,0:T(8,128)(2,1)}), bf16[4,768,128]{2,1,0:T(8,128)(2,1)S(1)}, u32[]{:S(2)}, u32[]{:S(2)}) async-start(bf16[4,768,128]{2,1,0:T(8,128)(2,1)} %pad_maximum_fusion.3), calls=%async_computation.1 | async-start | bytes 1572864 | tf_op jit(solution)/shard_map/all_to_all | solution.py:61
  47.9 143.9 %all-gather.15.cloned.1.call-start = ((), (), s32[]{:S(2)}) async-start(), calls=%async_computation.19 | async-start | bytes 3145728 | tf_op jit(solution)/shard_map/all_gather | solution.py:322
  47.9 3.6 collective-permute-start.2
  51.5 5.1 collective-permute-start.3
  54.4 150.2 %all-gather.9.cloned.1.call-start = ((), (), s32[]{:S(2)}) async-start(), calls=%async_computation.15 | async-start | bytes 3145728 | tf_op jit(solution)/shard_map/all_gather | solution.py:323
  70.1 14.1 %collective-permute-start.7 = (bf16[2048,128]{1,0:T(8,128)(2,1)S(1)}, bf16[2048,128]{1,0:T(8,128)(2,1)S(1)}, u32[]{:S(2)}, u32[]{:S(2)}) collective-permute-start(bf16[2048,128]{1,0:T(8,128)(2,1)S(1)} %bitcast.232), channel_id=1, source_target_pairs={{0,32},{32,64},{64,96},{96,0},{1,33},{33,65},{65,97},{97,1},{2,34}... | collective-permute-start | bytes 1572872 | tf_op jit(solution)/shard_map/ppermute | solution.py:49
  71.6 13.6 %collective-permute-start.8 = (bf16[2048,128]{1,0:T(8,128)(2,1)S(1)}, bf16[2048,128]{1,0:T(8,128)(2,1)S(1)}, u32[]{:S(2)}, u32[]{:S(2)}) collective-permute-start(bf16[2048,128]{1,0:T(8,128)(2,1)S(1)} %bitcast.233), channel_id=1, source_target_pairs={{0,96},{32,0},{64,32},{96,64},{1,97},{33,1},{65,33},{97,65},{2,98}... | collective-permute-start | bytes 1572872 | tf_op jit(solution)/shard_map/ppermute | solution.py:49
  75.1 16.8 %collective-permute-start.6 = (bf16[1024,64]{1,0:T(8,128)(2,1)}, bf16[1024,64]{1,0:T(8,128)(2,1)S(1)}, u32[]{:S(2)}, u32[]{:S(2)}) collective-permute-start(bf16[1024,64]{1,0:T(8,128)(2,1)} %bitcast.26), channel_id=1, source_target_pairs={{0,104},{8,96},{32,72},{40,64},{64,40},{72,32},{96,8},{104,0},{1,1... | collective-permute-start | bytes 393224 | tf_op jit(solution)/shard_map/ppermute | solution.py:57
  77.8 21.7 %collective-permute-start.11 = (bf16[2048,128]{1,0:T(8,128)(2,1)S(1)}, bf16[2048,128]{1,0:T(8,128)(2,1)S(1)}, u32[]{:S(2)}, u32[]{:S(2)}) collective-permute-start(bf16[2048,128]{1,0:T(8,128)(2,1)S(1)} %bitcast.234), channel_id=1, source_target_pairs={{0,8},{8,0},{1,9},{9,1},{2,10},{10,2},{3,11},{11,3},{4,12},{12,4},... | collective-permute-start | bytes 1572872 | tf_op jit(solution)/shard_map/ppermute | solution.py:53
  84.9 10.5 %collective-permute-start.9 = (bf16[1024,128]{1,0:T(8,128)(2,1)}, bf16[1024,128]{1,0:T(8,128)(2,1)S(1)}, u32[]{:S(2)}, u32[]{:S(2)}) collective-permute-start(bf16[1024,128]{1,0:T(8,128)(2,1)} %slice.264), channel_id=1, source_target_pairs={{0,32},{32,64},{64,96},{96,0},{1,33},{33,65},{65,97},{97,1},{2,34}... | collective-permute-start | bytes 786440 | tf_op jit(solution)/shard_map/ppermute | solution.py:49
  85.9 11.1 %collective-permute-start.10 = (bf16[1024,128]{1,0:T(8,128)(2,1)}, bf16[1024,128]{1,0:T(8,128)(2,1)S(1)}, u32[]{:S(2)}, u32[]{:S(2)}) collective-permute-start(bf16[1024,128]{1,0:T(8,128)(2,1)} %slice.265), channel_id=1, source_target_pairs={{0,96},{32,0},{64,32},{96,64},{1,97},{33,1},{65,33},{97,65},{2,98}... | collective-permute-start | bytes 786440 | tf_op jit(solution)/shard_map/ppermute | solution.py:49
  88.3 11.1 %collective-permute-start.12 = (bf16[2048,128]{1,0:T(8,128)(2,1)S(1)}, bf16[2048,128]{1,0:T(8,128)(2,1)S(1)}, u32[]{:S(2)}, u32[]{:S(2)}) collective-permute-start(bf16[2048,128]{1,0:T(8,128)(2,1)S(1)} %collective-permute-done.7.refs_1_), channel_id=1, source_target_pairs={{0,8},{8,0},{1,9},{9,1},{2,10},{10,2},{3,11},{11,3},{4,12},{12,4},... | collective-permute-start | bytes 1572872 | tf_op jit(solution)/shard_map/ppermute | solution.py:53
  91.9 7.6 %collective-permute-start.13 = (bf16[2048,128]{1,0:T(8,128)(2,1)S(1)}, bf16[2048,128]{1,0:T(8,128)(2,1)}, u32[]{:S(2)}, u32[]{:S(2)}) collective-permute-start(bf16[2048,128]{1,0:T(8,128)(2,1)S(1)} %collective-permute-done.8.refs_2_), channel_id=1, source_target_pairs={{0,8},{8,0},{1,9},{9,1},{2,10},{10,2},{3,11},{11,3},{4,12},{12,4},... | collective-permute-start | bytes 1572872 | tf_op jit(solution)/shard_map/ppermute | solution.py:53
  95.4 4.0 collective-permute-start.14
  97.0 2.5 collective-permute-start.15
  98.2 43.7 %copy-start.17 = (bf16[1,4,2,128,64]{4,3,2,1,0:T(8,128)(2,1)}, bf16[1,4,2,128,64]{4,3,2,1,0:T(8,128)(2,1)S(1)}, u32[]{:S(2)}) copy-start(bf16[1,4,2,128,64]{4,3,2,1,0:T(8,128)(2,1)S(1)} %copy.180) | copy-start | bytes 393220
  144.7 9.5 %collective-permute-start.16 = (bf16[1024,64]{1,0:T(8,128)(2,1)S(1)}, bf16[1024,64]{1,0:T(8,128)(2,1)S(1)}, u32[]{:S(2)}, u32[]{:S(2)}) collective-permute-start(bf16[1024,64]{1,0:T(8,128)(2,1)S(1)} %get-tuple-element.60), channel_id=1, source_target_pairs={{0,104},{8,96},{32,72},{40,64},{64,40},{72,32},{96,8},{104,0},{1,1... | collective-permute-start | bytes 393224 | tf_op jit(solution)/shard_map/ppermute | solution.py:57
  154.8 24.2 %copy-start.6 = (bf16[128,1024]{1,0:T(8,128)(2,1)S(1)}, bf16[128,1024]{1,0:T(8,128)(2,1)}, u32[]{:S(2)}) copy-start(bf16[128,1024]{1,0:T(8,128)(2,1)} %param.15) | copy-start | bytes 786436
  169.2 9.7 %all-to-all-start.3 = ((bf16[4,128,256]{2,1,0:T(8,128)(2,1)}), bf16[4,128,256]{2,1,0:T(8,128)(2,1)S(1)}, u32[]{:S(2)}, u32[]{:S(2)}) async-start(bf16[4,128,256]{2,1,0:T(8,128)(2,1)} %reshape.432), calls=%async_computation.3 | async-start | bytes 524288 | tf_op jit(solution)/shard_map/all_to_all | solution.py:61
  182.6 18.2 %all-to-all-start.4 = ((bf16[4,128,1024]{2,1,0:T(8,128)(2,1)}), bf16[4,128,1024]{2,1,0:T(8,128)(2,1)}, u32[]{:S(2)}, u32[]{:S(2)}) async-start(bf16[4,128,1024]{2,1,0:T(8,128)(2,1)} %broadcast_in_dim.38), calls=%async_computation.4 | async-start | bytes 2097152 | tf_op jit(solution)/shard_map/all_to_all | solution.py:61
  186.8 25.4 %all-gather.11.cloned.1.call-start = ((), (), s32[]{:S(2)}) async-start(), calls=%async_computation.17 | async-start | bytes 1310720 | tf_op jit(solution)/shard_map/all_gather | solution.py:326
  187.4 59.9 %reduce-scatter.2.cloned.1.call-start = ((), (), s32[]{:S(2)}) async-start(), calls=%async_computation.16 | async-start | bytes 1310720 | tf_op jit(solution)/shard_map/reduce_scatter | solution.py:399
  187.5 4.2 collective-permute-start.17
  219.9 26.7 %all-to-all-start.5 = ((bf16[4,128,1024]{2,1,0:T(8,128)(2,1)}), bf16[4,128,1024]{2,1,0:T(8,128)(2,1)S(1)}, u32[]{:S(2)}, u32[]{:S(2)}) async-start(bf16[4,128,1024]{2,1,0:T(8,128)(2,1)} %bitcast.273), calls=%async_computation.6 | async-start | bytes 2097152 | tf_op jit(solution)/shard_map/all_to_all | solution.py:61
  252.1 8.9 %all-to-all-start.6 = ((bf16[4,128,256]{1,2,0:T(8,128)(2,1)}), bf16[4,128,256]{1,2,0:T(8,128)(2,1)S(1)}, u32[]{:S(2)}, u32[]{:S(2)}) async-start(bf16[4,128,256]{1,2,0:T(8,128)(2,1)} %bitcast.44), calls=%async_computation.7 | async-start | bytes 524288 | tf_op jit(solution)/shard_map/all_to_all | solution.py:61
  261.4 24.0 %copy-start.18 = (bf16[1,4,2,128,64]{4,3,2,1,0:T(8,128)(2,1)S(1)}, bf16[1,4,2,128,64]{4,3,2,1,0:T(8,128)(2,1)}, u32[]{:S(2)}) copy-start(bf16[1,4,2,128,64]{4,3,2,1,0:T(8,128)(2,1)} %copy-done.17) | copy-start | bytes 393220
  261.4 24.0 %copy-start.34 = (bf16[1024,64]{1,0:T(8,128)(2,1)S(1)}, bf16[1024,64]{1,0:T(8,128)(2,1)}, u32[]{:S(2)}) copy-start(bf16[1024,64]{1,0:T(8,128)(2,1)} %copy-done.33) | copy-start | bytes 393220
  262.1 9.4 %all-to-all-start.7 = ((bf16[4,256,128]{1,2,0:T(8,128)(2,1)}), bf16[4,256,128]{1,2,0:T(8,128)(2,1)S(1)}, u32[]{:S(2)}, u32[]{:S(2)}) async-start(bf16[4,256,128]{1,2,0:T(8,128)(2,1)} %pad_maximum_fusion.10), calls=%async_computation.8 | async-start | bytes 524288 | tf_op jit(solution)/shard_map/all_to_all | solution.py:61
  271.9 13.4 %collective-permute-start.18 = (bf16[1024,64]{1,0:T(8,128)(2,1)S(1)}, bf16[1024,64]{1,0:T(8,128)(2,1)S(1)}, u32[]{:S(2)}, u32[]{:S(2)}) collective-permute-start(bf16[1024,64]{1,0:T(8,128)(2,1)S(1)} %bitcast.290), channel_id=1, source_target_pairs={{0,104},{8,96},{32,72},{40,64},{64,40},{72,32},{96,8},{104,0},{1,1... | collective-permute-start | bytes 393224 | tf_op jit(solution)/shard_map/ppermute | solution.py:57
  343.6 19.0 %collective-permute-start.19 = (bf16[8192,128]{1,0:T(8,128)(2,1)}, bf16[8192,128]{1,0:T(8,128)(2,1)}, u32[]{:S(2)}, u32[]{:S(2)}) collective-permute-start(bf16[8192,128]{1,0:T(8,128)(2,1)} %get-tuple-element.26), channel_id=1, source_target_pairs={{0,8},{8,0},{1,9},{9,1},{2,10},{10,2},{3,11},{11,3},{4,12},{12,4},... | collective-permute-start | bytes 6291464 | tf_op jit(solution)/shard_map/ppermute | solution.py:53
  357.8 12.0 %collective-permute-start.31 = (bf16[2,512,512]{2,1,0:T(8,128)(2,1)}, bf16[2,512,512]{2,1,0:T(8,128)(2,1)}, u32[]{:S(2)}, u32[]{:S(2)}) collective-permute-start(bf16[2,512,512]{2,1,0:T(8,128)(2,1)} %bitcast.228), channel_id=1, source_target_pairs={{0,8},{8,0},{1,9},{9,1},{2,10},{10,2},{3,11},{11,3},{4,12},{12,4},... | collective-permute-start | bytes 3145736 | tf_op jit(solution)/shard_map/ppermute | solution.py:53
  362.3 16.3 %collective-permute-start.34 = (bf16[2,256,1024]{2,1,0:T(8,128)(2,1)}, bf16[2,256,1024]{2,1,0:T(8,128)(2,1)}, u32[]{:S(2)}, u32[]{:S(2)}) collective-permute-start(bf16[2,256,1024]{2,1,0:T(8,128)(2,1)} %dynamic-slice_bitcast_fusion), channel_id=1, source_target_pairs={{0,8},{8,0},{1,9},{9,1},{2,10},{10,2},{3,11},{11,3},{4,12},{12,4},... | collective-permute-start | bytes 3145736 | tf_op jit(solution)/shard_map/ppermute | solution.py:53
  366.1 36.9 %all-to-all-start.8 = ((bf16[4,2048,128]{2,1,0:T(8,128)(2,1)}), bf16[4,2048,128]{2,1,0:T(8,128)(2,1)S(1)}, u32[]{:S(2)}, u32[]{:S(2)}) async-start(bf16[4,2048,128]{2,1,0:T(8,128)(2,1)} %bitcast.238), calls=%async_computation.9 | async-start | bytes 4194304 | tf_op jit(solution)/shard_map/all_to_all | solution.py:61
  369.7 44.0 %all-gather.13.cloned.1.call-start = ((), (), s32[]{:S(2)}) async-start(), calls=%async_computation.18 | async-start | bytes 1310720 | tf_op jit(solution)/shard_map/all_gather | solution.py:408
  373.4 36.2 %collective-permute-start.32 = (bf16[512,512]{1,0:T(8,128)(2,1)}, bf16[512,512]{1,0:T(8,128)(2,1)}, u32[]{:S(2)}, u32[]{:S(2)}) collective-permute-start(bf16[512,512]{1,0:T(8,128)(2,1)} %dynamic-slice_bitcast_fusion.2), channel_id=1, source_target_pairs={{0,1},{1,0},{2,3},{3,2},{4,5},{5,4},{6,7},{7,6},{8,9},{9,8},{10,11... | collective-permute-start | bytes 1572872 | tf_op jit(solution)/shard_map/ppermute | solution.py:53
  375.3 26.2 %collective-permute-start.20 = (bf16[1024,64]{1,0:T(8,128)(2,1)}, bf16[1024,64]{1,0:T(8,128)(2,1)S(1)}, u32[]{:S(2)}, u32[]{:S(2)}) collective-permute-start(bf16[1024,64]{1,0:T(8,128)(2,1)} %get-tuple-element.57), channel_id=1, source_target_pairs={{0,104},{8,96},{32,72},{40,64},{64,40},{72,32},{96,8},{104,0},{1,1... | collective-permute-start | bytes 393224 | tf_op jit(solution)/shard_map/ppermute | solution.py:57
  382.4 29.2 %collective-permute-start.35 = (bf16[256,1024]{1,0:T(8,128)(2,1)}, bf16[256,1024]{1,0:T(8,128)(2,1)}, u32[]{:S(2)}, u32[]{:S(2)}) collective-permute-start(bf16[256,1024]{1,0:T(8,128)(2,1)} %dynamic-slice_bitcast_fusion.1), channel_id=1, source_target_pairs={{0,1},{1,0},{2,3},{3,2},{4,5},{5,4},{6,7},{7,6},{8,9},{9,8},{10,11... | collective-permute-start | bytes 1572872 | tf_op jit(solution)/shard_map/ppermute | solution.py:53
  405.8 15.7 %all-to-all-start.9 = ((bf16[4,768,128]{2,1,0:T(8,128)(2,1)}), bf16[4,768,128]{2,1,0:T(8,128)(2,1)S(1)}, u32[]{:S(2)}, u32[]{:S(2)}) async-start(bf16[4,768,128]{2,1,0:T(8,128)(2,1)} %maximum_maximum_fusion), calls=%async_computation.10 | async-start | bytes 1572864 | tf_op jit(solution)/shard_map/all_to_all | solution.py:61
  409.3 75.5 %all-reduce.6.cloned.1.call-start = ((), (), s32[]{:S(2)}) async-start(), calls=%async_computation.20 | async-start | bytes 2097152 | tf_op jit(solution)/shard_map/psum | solution.py:414
  437.9 51.8 %collective-permute-start.28 = (bf16[2,2048,128]{1,2,0:T(8,128)(2,1)S(1)}, bf16[2,2048,128]{1,2,0:T(8,128)(2,1)}, u32[]{:S(2)}, u32[]{:S(2)}) collective-permute-start(bf16[2,2048,128]{1,2,0:T(8,128)(2,1)S(1)} %fusion.14), channel_id=1, source_target_pairs={{0,8},{8,0},{1,9},{9,1},{2,10},{10,2},{3,11},{11,3},{4,12},{12,4},... | collective-permute-start | bytes 3145736 | tf_op jit(solution)/shard_map/ppermute | solution.py:53
  484.9 14.3 %collective-permute-start.33 = (bf16[512,512]{1,0:T(8,128)(2,1)}, bf16[512,512]{1,0:T(8,128)(2,1)}, u32[]{:S(2)}, u32[]{:S(2)}) collective-permute-start(bf16[512,512]{1,0:T(8,128)(2,1)} %get-tuple-element.36), channel_id=1, source_target_pairs={{0,8},{8,0},{1,9},{9,1},{2,10},{10,2},{3,11},{11,3},{4,12},{12,4},... | collective-permute-start | bytes 1572872 | tf_op jit(solution)/shard_map/ppermute | solution.py:53
  492.0 16.7 %collective-permute-start.29 = (bf16[2048,128]{0,1:T(8,128)(2,1)}, bf16[2048,128]{0,1:T(8,128)(2,1)}, u32[]{:S(2)}, u32[]{:S(2)}) collective-permute-start(bf16[2048,128]{0,1:T(8,128)(2,1)} %dynamic-slice_bitcast_fusion.3), channel_id=1, source_target_pairs={{0,1},{1,0},{2,3},{3,2},{4,5},{5,4},{6,7},{7,6},{8,9},{9,8},{10,11... | collective-permute-start | bytes 1572872 | tf_op jit(solution)/shard_map/ppermute | solution.py:53
  497.5 1.4 collective-permute-start.21
  498.0 19.4 %collective-permute-start.36 = (bf16[256,1024]{1,0:T(8,128)(2,1)S(1)}, bf16[256,1024]{1,0:T(8,128)(2,1)}, u32[]{:S(2)}, u32[]{:S(2)}) collective-permute-start(bf16[256,1024]{1,0:T(8,128)(2,1)S(1)} %copy-done.35), channel_id=1, source_target_pairs={{0,8},{8,0},{1,9},{9,1},{2,10},{10,2},{3,11},{11,3},{4,12},{12,4},... | collective-permute-start | bytes 1572872 | tf_op jit(solution)/shard_map/ppermute | solution.py:53
  498.9 8.0 %collective-permute-start.22 = (f32[8,1024]{1,0:T(8,128)S(1)}, f32[8,1024]{1,0:T(8,128)S(1)}, u32[]{:S(2)}, u32[]{:S(2)}) collective-permute-start(f32[8,1024]{1,0:T(8,128)S(1)} %add.272), channel_id=1, source_target_pairs={{0,16},{16,0},{1,17},{17,1},{2,18},{18,2},{3,19},{19,3},{4,20},{20... | collective-permute-start | bytes 98312 | tf_op jit(solution)/shard_map/ppermute | solution.py:53
  506.9 9.0 %collective-permute-start.23 = (f32[8,1024]{1,0:T(8,128)S(1)}, f32[8,1024]{1,0:T(8,128)S(1)}, u32[]{:S(2)}, u32[]{:S(2)}) collective-permute-start(f32[8,1024]{1,0:T(8,128)S(1)} %add.273), channel_id=1, source_target_pairs={{0,1},{1,0},{2,3},{3,2},{4,5},{5,4},{6,7},{7,6},{8,9},{9,8},{10,11... | collective-permute-start | bytes 98312 | tf_op jit(solution)/shard_map/ppermute | solution.py:53
  510.7 15.0 %all-to-all-start.11 = ((bf16[8,256,128]{1,2,0:T(8,128)(2,1)}), bf16[8,256,128]{1,2,0:T(8,128)(2,1)S(1)}, u32[]{:S(2)}, u32[]{:S(2)}) async-start(bf16[8,256,128]{1,2,0:T(8,128)(2,1)} %bitcast.230), calls=%async_computation.12 | async-start | bytes 1048576 | tf_op jit(solution)/shard_map/all_to_all | solution.py:61
  515.9 5.5 collective-permute-start.24
  521.5 4.3 collective-permute-start.25
  525.7 20.6 %all-to-all-start.10 = ((bf16[4,128,1024]{2,1,0:T(8,128)(2,1)}), bf16[4,128,1024]{2,1,0:T(8,128)(2,1)S(1)}, u32[]{:S(2)}, u32[]{:S(2)}) async-start(bf16[4,128,1024]{2,1,0:T(8,128)(2,1)} %bitcast.61), calls=%async_computation.11 | async-start | bytes 2097152 | tf_op jit(solution)/shard_map/all_to_all | solution.py:61
  529.9 22.4 %copy-start.40 = (f32[1024]{0:T(1024)S(1)}, f32[1024]{0:T(1024)}, u32[]{:S(2)}) copy-start(f32[1024]{0:T(1024)} %copy-done.39) | copy-start | bytes 12292
  529.9 10.7 %collective-permute-start.26 = (f32[6,1024]{1,0:T(8,128)S(1)}, f32[6,1024]{1,0:T(8,128)S(1)}, u32[]{:S(2)}, u32[]{:S(2)}) collective-permute-start(f32[6,1024]{1,0:T(8,128)S(1)} %bitcast.293), channel_id=1, source_target_pairs={{0,2},{2,0},{4,6},{6,4},{1,3},{3,1},{5,7},{7,5},{8,10},{10,8},{12,... | collective-permute-start | bytes 73736 | tf_op jit(solution)/shard_map/ppermute | solution.py:471
  540.5 5.0 collective-permute-start.27
  547.2 18.9 %copy-start.11 = (f32[128,1024]{1,0:T(8,128)S(1)}, f32[128,1024]{1,0:T(8,128)}, u32[]{:S(2)}) copy-start(f32[128,1024]{1,0:T(8,128)} %copy-done.10) | copy-start | bytes 1572868
  547.2 18.9 %copy-start.20 = (bf16[128,1024]{1,0:T(8,128)(2,1)S(1)}, bf16[128,1024]{1,0:T(8,128)(2,1)}, u32[]{:S(2)}) copy-start(bf16[128,1024]{1,0:T(8,128)(2,1)} %param.29) | copy-start | bytes 786436
  547.2 11.8 %all-to-all-start.12 = ((bf16[8,256,128]{2,1,0:T(8,128)(2,1)}), bf16[8,256,128]{2,1,0:T(8,128)(2,1)S(1)}, u32[]{:S(2)}, u32[]{:S(2)}) async-start(bf16[8,256,128]{2,1,0:T(8,128)(2,1)} %broadcast_in_dim.43), calls=%async_computation.13 | async-start | bytes 1048576 | tf_op jit(solution)/shard_map/all_to_all | solution.py:61
  559.1 8.3 %collective-permute-start.30 = (bf16[8,256,128]{2,1,0:T(8,128)(2,1)S(1)}, bf16[8,256,128]{2,1,0:T(8,128)(2,1)S(1)}, u32[]{:S(2)}, u32[]{:S(2)}) collective-permute-start(bf16[8,256,128]{2,1,0:T(8,128)(2,1)S(1)} %all-to-all-done.12), channel_id=1, source_target_pairs={{0,8},{8,0},{1,9},{9,1},{2,10},{10,2},{3,11},{11,3},{4,12},{12,4},... | collective-permute-start | bytes 1572872 | tf_op jit(solution)/shard_map/ppermute | solution.py:53
  (50 other events, 299.0 us)
Sparse Core Ops, SparseCore 0:
  10.4 67.7 all-gather.6
  79.8 36.7 all-gather.14
  147.7 34.0 all-gather.8
  189.0 23.1 all-gather.10
  215.0 30.2 reduce-scatter.1
  374.7 21.6 all-gather.12
  413.8 71.0 all-reduce.5

commit v2 on v1

v2 whole, which is shorter than its diff:
```python
import functools

import jax
import jax.numpy as jnp
from jax import lax
from jax.experimental import pallas as pl
from jax.experimental.pallas import tpu as pltpu
from jax.sharding import Mesh
from jax.sharding import PartitionSpec as P

HEAD_DIM = 64
EPSILON = 1e-05
MASKED = -1e30
LOG2E = 1.4426950408889634
TO_LOG2 = LOG2E * HEAD_DIM ** (-0.5)
AXES = ("x", "zl", "co", "y", "zh")
BF16, F32 = jnp.bfloat16, jnp.float32
SLICE = 1024
FWD_Q, FWD_K = 1024, 1024
BWD_Q = 1024


def contract(left, right, left_dim, right_dim):
    return lax.dot_general(
        left, right, (((left_dim,), (right_dim,)), ((), ())), preferred_element_type=F32
    )


def matmul(left, right):
    return contract(left, right, 1, 0)


def shift(values, steps):
    return lax.ppermute(values, "y", [(i, (i + steps) % 4) for i in range(4)])


def hop(values, bit, axis="x"):
    return lax.ppermute(values, axis, [(i, i ^ bit) for i in range(4)])


def swap(values, axis):
    return lax.ppermute(values, axis, [(0, 1), (1, 0)])


def to_mirror(rows, zl):
    moved = lax.ppermute(rows, ("x", "zl"), [(i, 8 - i) for i in (1, 3, 5, 7)])
    return jnp.where(zl == 0, rows, moved)


def exchange(blocks, axes):
    return lax.all_to_all(blocks, axes, 0, 0, tiled=True)


def gather(rows, axes, size):
    return exchange(jnp.broadcast_to(rows[None], (size,) + rows.shape), axes)


def gather_y(rows):
    one, three = shift(rows, 1), shift(rows, 3)
    return rows, one, shift(rows, 2), three


def send_y(blocks):
    return blocks[0], shift(blocks[1], -1), shift(blocks[3], -3), shift(blocks[2], -2)


def total(parts):
    return functools.reduce(jnp.add, [part.astype(F32) for part in parts])


def after(value, *others):
    return lax.optimization_barrier((value, others))[0]


def turned(values, dim, index):
    return jnp.where(index == 0, values, jnp.flip(values, dim))


def halves(values, dim, index):
    half = values.shape[dim] // 2
    return (
        lax.dynamic_slice_in_dim(values, index * half, half, dim),
        lax.dynamic_slice_in_dim(values, (1 - index) * half, half, dim),
    )


def to_z(rows):
    n = rows.shape[-1]
    return rows.reshape(2, 4, 2, 128, n).transpose(0, 2, 1, 3, 4).reshape(4, 512, n)


def on_core(kernel, name, outputs, operands, flops, limit=32, scratch=()):
    whole = pl.BlockSpec(memory_space=pltpu.VMEM)
    outputs = [jax.ShapeDtypeStruct(shape, dtype) for shape, dtype in outputs]
    return pl.pallas_call(
        kernel,
        out_shape=outputs,
        in_specs=[pl.BlockSpec(memory_space=pltpu.SMEM)] + [whole] * (len(operands) - 1),
        out_specs=[whole] * len(outputs),
        scratch_shapes=list(scratch),
        compiler_params=pltpu.CompilerParams(vmem_limit_bytes=limit << 20),
        cost_estimate=pl.CostEstimate(flops=flops, bytes_accessed=4 << 20, transcendentals=0),
        name=name,
    )(*operands)


def joined(refs, dim=0):
    return jnp.concatenate([ref[...] for ref in refs], axis=dim)


def unit_rows(rows):
    centered = rows - jnp.mean(rows, axis=-1, keepdims=True)
    scale = lax.rsqrt(jnp.mean(centered * centered, axis=-1, keepdims=True) + EPSILON)
    return centered * scale, scale


def norm_back(grad, unit, scale, gain):
    grad = grad * gain
    along = jnp.mean(grad * unit, axis=-1, keepdims=True)
    return scale * (grad - jnp.mean(grad, axis=-1, keepdims=True) - unit * along)


def y_rows(place, steps):
    return pl.ds(pl.multiple_of(((place[3] - steps) & 3) * 128, 128), 128)


def merge_lanes(left, right):
    left, right = left.astype(F32), right.astype(F32)
    first = lax.broadcasted_iota(jnp.int32, left.shape, 1) < HEAD_DIM
    return (
        jnp.where(first, left, pltpu.roll(right, HEAD_DIM, 1)).astype(BF16),
        jnp.where(first, pltpu.roll(left, HEAD_DIM, 1), right).astype(BF16),
    )


def project_kernel(place, *refs):
    pieces, (gain, bent, own, near, far, own_bias, pair_bias) = refs[:4], refs[4:11]
    blocks, normed_ref, unit_ref = refs[11:]
    core, zh = place[2], place[4]
    for steps, piece in enumerate(pieces):
        rows = y_rows(place, steps)
        unit, _ = unit_rows(piece[...].astype(F32))
        unit_ref[rows, :] = unit.astype(BF16)
        normed_ref[rows, :] = (unit * gain[...] + bent[...]).astype(BF16)
    normed = normed_ref[...]
    first = normed_ref[:, pl.ds(pl.multiple_of(core * 512, 512), 512)]
    second = normed_ref[:, pl.ds(pl.multiple_of((1 - core) * 512, 512), 512)]
    for pair in range(2):
        bias = (pair_bias if pair else own_bias)[...].astype(F32)

        def projected(i, pair=pair):
            if pair:
                return matmul(first, near[i]) + matmul(second, far[i])
            return matmul(normed, own[i])

        queries = (projected(0) + bias[:1]).T.astype(BF16)
        mixed = merge_lanes(projected(1).astype(BF16), (projected(2) + bias[1:]).astype(BF16))
        for head in range(2):
            where = 2 * head + (zh ^ pair)
            blocks[where, pl.ds(0, 512), :] = mixed[head]
            for y in range(4):
                lanes = slice(y * 128, y * 128 + 128)
                piece = queries[head * HEAD_DIM : head * HEAD_DIM + HEAD_DIM, lanes]
                blocks[where, pl.ds(512 + y * HEAD_DIM, HEAD_DIM), :] = piece


def project_back_kernel(place, blocks, unit_ref, own, near, far, *refs):
    outs, sums, grad_ref = refs[:4], refs[4], refs[5]
    core, zh = place[2], place[4]
    for pair in range(2):
        heads = [blocks[2 * head + (zh ^ pair)] for head in range(2)]
        keys, values = merge_lanes(heads[0][:512], heads[1][:512])
        queries = [
            jnp.concatenate([head[512 + y * HEAD_DIM :][:HEAD_DIM] for y in range(4)], axis=1)
            for head in heads
        ]
        parts = (jnp.concatenate(queries, axis=0).T, keys, values)

        def back(weight, parts=parts):
            return functools.reduce(
                jnp.add, [contract(part, weight[i], 1, 1) for i, part in enumerate(parts)]
            )

        if pair:
            first = pl.ds(pl.multiple_of(core * 512, 512), 512)
            second = pl.ds(pl.multiple_of((1 - core) * 512, 512), 512)
            grad_ref[:, first] += back(near)
            grad_ref[:, second] += back(far)
        else:
            grad_ref[...] = back(own)
    grad = grad_ref[...]
    sums[...] = jnp.concatenate(
        [
            jnp.sum(grad * unit_ref[...].astype(F32), axis=0, keepdims=True),
            jnp.sum(grad, axis=0, keepdims=True),
        ]
    )
    for steps, out in enumerate(outs):
        out[...] = grad_ref[y_rows(place, steps), :].astype(BF16)


def qkv_grads_kernel(place, blocks_ref, normed_ref, grad_ref, sums_ref):
    normed, ones = normed_ref[...], jnp.ones((512, 128), BF16)
    for head in range(2):
        for zh in range(2):
            block = blocks_ref[2 * head + zh]
            queries = [block[512 + y * HEAD_DIM :][:HEAD_DIM] for y in range(4)]
            left = jnp.concatenate([block[:512].T, jnp.concatenate(queries, axis=1)], axis=0)
            grad = matmul(left, normed)
            for chunk in range(8):
                piece = grad[:, chunk * 128 : chunk * 128 + 128].astype(BF16)
                grad_ref[place[2] ^ (chunk // 4), chunk % 4, head, zh] = piece
            sums_ref[2 * head + zh] = matmul(left, ones)


def attend_out_kernel(place, heads, kept, sent, tokens, bias, gain, bent, resid_ref, mid_ref, att_ref):
    core, y, zh = place[2], place[3], place[4]
    for side in range(2):
        for steps in range(4):
            for pair in range(2):
                where = 8 * (core ^ side) + 2 * ((y - steps) & 3) + (zh ^ pair)
                att_ref[side, pl.ds(steps * 128 + pair * HEAD_DIM, HEAD_DIM), :] = heads[where]
    branch = matmul(att_ref[0].T, kept[...]) + matmul(att_ref[1].T, sent[...])
    resid = tokens[...].astype(F32) + branch + bias[...]
    resid_ref[...] = resid
    mid_ref[...] = (unit_rows(resid)[0] * gain[...] + bent[...]).astype(BF16)


def mid_back_kernel(place, *refs):
    parts, resid, cotangent, gain, kept, sent = refs[:6]
    grad_resid_ref, branch_ref, heads, sums = refs[6:]
    core, y, zh = place[2], place[3], place[4]
    grad = total([parts[i] for i in range(4)])
    unit, scale = unit_rows(resid[...])
    cot = cotangent[...].astype(F32)
    grad_resid = cot + norm_back(grad, unit, scale, gain[...])
    grad_resid_ref[...] = grad_resid
    branch = grad_resid.astype(BF16)
    branch_ref[...] = branch
    rows = [grad_resid, grad * unit, grad, cot]
    sums[...] = jnp.concatenate([jnp.sum(row, axis=0, keepdims=True) for row in rows])
    for side, weight in enumerate((kept, sent)):
        grads = contract(weight[...], branch, 1, 1).astype(BF16)
        for steps in range(4):
            for pair in range(2):
                where = 8 * (core ^ side) + 2 * ((y - steps) & 3) + (zh ^ pair)
                start = steps * 128 + pair * HEAD_DIM
                heads[where] = grads[start : start + HEAD_DIM]


def feed_forward_kernel(place, *refs):
    mids, cots, (bias,), ups, downs = refs[:4], refs[4:8], refs[8:9], refs[9:13], refs[13:17]
    active_ref, grad_ref, out, bias_grad = refs[17:]
    mid, cot = joined(mids), jnp.concatenate([ref[:128, :] for ref in cots])
    summed = None
    for i, (up_ref, down_ref) in enumerate(zip(ups, downs)):
        span = pl.ds(i * 256, 256)
        up = up_ref[...]
        hidden = matmul(mid, up) + bias[:, span]
        square = hidden * hidden
        bent = jnp.tanh(0.7978845608028654 * hidden * (1.0 + 0.044715 * square))
        active_ref[:, span] = (0.5 * hidden * (1.0 + bent)).astype(BF16)
        slope = 0.7978845608028654 * (1.0 + 3.0 * 0.044715 * square)
        slope = 0.5 * (1.0 + bent) + 0.5 * hidden * (1.0 - bent * bent) * slope
        grad = (slope * contract(cot, down_ref[...], 1, 1)).astype(BF16)
        grad_ref[:, span] = grad
        bias_grad[:, span] = jnp.sum(grad.astype(F32), axis=0, keepdims=True)
        part = contract(grad, up, 1, 1)
        summed = part if summed is None else summed + part
    for steps in range(4):
        piece = summed[steps * 128 : steps * 128 + 128].astype(BF16)
        out[(place[3] - steps) & 3] = piece


def unit_grads_kernel(kept, place, *refs):
    mids, cots, active, grad = refs[:4], refs[4:8], refs[8], refs[9]
    got, out = (refs[10], refs[11]) if kept else (None, refs[10])
    span = pl.ds(0 if kept else 512, 512)
    cot = jnp.concatenate([ref[:128, :] for ref in cots])
    for i, (left, right) in enumerate(((cot, active), (joined(mids), grad))):
        summed = contract(left, right[:, span], 0, 0)
        for share in range(8):
            block = summed[share * 128 : share * 128 + 128]
            if kept:
                block = (block + got[share, i].astype(F32)).astype(BF16)
                for pair in range(2):
                    half = block[:, pair * 256 : pair * 256 + 256]
                    out[2 * share + (place[4] ^ pair), pl.ds(i * 128, 128), :] = half
            else:
                out[share, i] = block.astype(BF16)


def out_down_kernel(place, att, branch, active, *refs):
    downs, outs = refs[:4], refs[4:]
    grads = [matmul(att[side], branch[...]).astype(BF16) for side in range(2)]
    down = total([matmul(active[:, i * 256 : i * 256 + 256], ref[...]) for i, ref in enumerate(downs)])
    for steps, out in enumerate(outs):
        rows = slice(steps * 128, steps * 128 + 128)
        out[pl.ds(0, 128), :] = grads[0][rows]
        out[pl.ds(128, 128), :] = grads[1][rows]
        out[pl.ds(256, 128), :] = down[rows].astype(BF16)


def out_sums_kernel(place, *refs):
    parts, (resid, bias, grad_resid, home, kept, sent) = refs[:4], refs[4:]
    home[0] = total([part[256:, :] for part in parts]) + resid[...] + bias[...]
    home[1] = grad_resid[...]
    for side, ref in enumerate((kept, sent)):
        summed = total([part[side * 128 : side * 128 + 128, :] for part in parts]).astype(ref.dtype)
        for pair in range(2):
            for share in range(8):
                lanes = slice(share * 128, share * 128 + 128)
                piece = summed[pair * HEAD_DIM : pair * HEAD_DIM + HEAD_DIM, lanes]
                ref[share // 2, share % 2, pair] = piece


def shares_kernel(place, heads, head_got, out, out_got, small, shares):
    for x in range(4):
        for zl in range(2):
            share = 2 * x + zl
            for zh in range(2):
                to = 2 * share + zh
                grad = total([heads[0, x, zl, zh], head_got[x, zl, zh]])
                shares[to, pl.ds(0, 192), :] = grad.astype(BF16)
                grad = total([out[x, zl, zh], out_got[x, zl, zh]])
                shares[2 * share + (place[4] ^ zh), pl.ds(192, HEAD_DIM), :] = grad.astype(BF16)
                rows = small[:, share * 128 : share * 128 + 128]
                rows = jnp.concatenate([rows, jnp.zeros_like(rows)]).astype(BF16)
                shares[to, pl.ds(256, 16), :] = rows


def last_norm_kernel(place, *refs):
    parts, (tokens, gain, resid, out) = refs[:4], refs[4:]
    unit, scale = unit_rows(tokens[...].astype(F32))
    out[...] = resid[...] + norm_back(total([part[...] for part in parts]), unit, scale, gain[...])


def unit_weights_kernel(place, own, other, down, up):
    for side, ref in enumerate((own, other)):
        half = place[2] ^ side
        for share in range(8):
            lanes = pl.ds(share * 128, 128)
            down[pl.ds(pl.multiple_of(half * 256, 256), 256), lanes] = ref[share, :256].astype(F32)
            for part in range(2):
                lanes = pl.ds(pl.multiple_of(half * 256 + part * 128, 128), 128)
                piece = ref[share, pl.ds(256 + part * 128, 128), :].astype(F32)
                up[pl.ds(share * 128, 128), lanes] = piece


def head_weights_kernel(place, own, other, qkv, out):
    for side, ref in enumerate((own, other)):
        half = place[2] ^ side
        for x in range(4):
            rows = pl.ds(pl.multiple_of(half * 512 + x * 128, 128), 128)
            for i, which in enumerate((1, 2, 0)):
                span = pl.ds(i * HEAD_DIM, HEAD_DIM)
                both = jnp.concatenate([ref[2 * x, span, :], ref[2 * x + 1, span, :]])
                qkv[which, rows, :] = both.astype(F32).T
            for zl in range(2):
                piece = ref[2 * x + zl, pl.ds(192, HEAD_DIM), :].astype(F32)
                span = pl.ds(pl.multiple_of(half * HEAD_DIM, HEAD_DIM), HEAD_DIM)
                out[span, pl.ds((2 * x + zl) * 128, 128)] = piece


def forward_kernel(spot, q_ref, end_ref, *refs):
    pieces, (state_ref, out, kv_ref, vt_ref, qt_ref, sems) = refs[:14], refs[14:]
    x, core = spot[0], spot[1]
    copies = []

    def bring(piece, half, x_from, slice_in_x, parity):
        where = (4 * x_from + 2 * slice_in_x + parity) * SLICE
        copy = pltpu.make_async_copy(
            piece.at[pl.ds(half * SLICE, SLICE), :],
            kv_ref.at[pl.ds(pl.multiple_of(where, SLICE), SLICE), :],
            sems.at[len(copies)],
        )
        copy.start()
        copies.append(copy)

    for side in range(2):
        parity = core if side == 0 else 1 - core
        pieces_here = pieces[7 * side : 7 * side + 7]
        bring(pieces_here[0], 0, x, 0, parity)
        bring(pieces_here[0], 1, x, 1, parity)
        for i, piece in enumerate(pieces_here[1:]):
            bring(piece, 0, x ^ (1, 1, 3, 3, 2, 2)[i], i % 2, parity)
    qt_ref[HEAD_DIM:, :] = jnp.zeros((HEAD_DIM, 2 * SLICE), BF16)
    for chunk in range(16):
        qt_ref[:HEAD_DIM, pl.ds(chunk * 128, 128)] = q_ref[chunk]
    vt_ref[HEAD_DIM:, :] = jnp.ones((16, vt_ref.shape[1]), BF16)
    for copy in copies:
        copy.wait()

    def turn(i, largest):
        rows = pl.ds(pl.multiple_of(i * SLICE, SLICE), SLICE)
        both = kv_ref[rows, :].T
        vt_ref[:HEAD_DIM, rows] = both[HEAD_DIM:, :]
        keys = both[:HEAD_DIM, :].astype(F32)
        return jnp.maximum(largest, jnp.sum(keys * keys, axis=0, keepdims=True))

    longest = jnp.max(lax.fori_loop(0, 16, turn, jnp.zeros((1, SLICE), F32)))
    norms = qt_ref[:HEAD_DIM, :].astype(F32)
    norms = jnp.sum(norms * norms, axis=0, keepdims=True)
    limit = jnp.sqrt(norms * longest) * TO_LOG2
    level = limit - 90.0

    def finish(total, log_top, start, wide):
        span = pl.ds(start, wide)
        weight_sum = total[HEAD_DIM : HEAD_DIM + 1]
        mixed = total[:HEAD_DIM] / weight_sum
        state_ref[:HEAD_DIM, span] = mixed
        for chunk in range(wide // 128):
            piece = mixed[:, chunk * 128 : chunk * 128 + 128].astype(BF16)
            out[start // 128 + chunk] = piece
        state_ref[HEAD_DIM:, span] = jnp.broadcast_to(log_top + jnp.log2(weight_sum), (8, wide))

    def masked_at(values, begin, end, other):
        place = begin + lax.broadcasted_iota(jnp.int32, values.shape, 0)
        return jnp.where(place < end, values, other)

    def bounded_tile(tile):
        span = pl.ds(tile * FWD_Q, FWD_Q)
        query, end = qt_ref[:, span], end_ref[:, span]
        base = level[:, tile * FWD_Q : tile * FWD_Q + FWD_Q]

        def step(masked, at, total):
            for piece in range(2):
                begin = pl.multiple_of(at * FWD_K + piece * (FWD_K // 2), FWD_K // 2)
                rows = pl.ds(begin, FWD_K // 2)
                weights = jnp.exp2(matmul(kv_ref[rows, :], query) * TO_LOG2 - base)
                if masked:
                    weights = masked_at(weights, begin, end, 0.0)
                total = total + matmul(vt_ref[:, rows], weights.astype(BF16))
            return total

        total = jnp.zeros((HEAD_DIM + 16, FWD_Q), F32)
        full, last = spot[2 + 2 * tile], spot[3 + 2 * tile]
        total = lax.fori_loop(0, full, functools.partial(step, False), total)
        total = lax.fori_loop(full, last, functools.partial(step, True), total)
        finish(total, base, tile * FWD_Q, FWD_Q)

    def running_tile(tile):
        wide = FWD_Q // 2
        starts = [tile * FWD_Q, tile * FWD_Q + wide]
        queries = [qt_ref[:, pl.ds(start, wide)] for start in starts]
        ends = [end_ref[:, pl.ds(start, wide)] for start in starts]

        def step(masked, at, carry):
            rows = pl.ds(pl.multiple_of(at * FWD_K, FWD_K), FWD_K)
            kv, vt = kv_ref[rows, :], vt_ref[:, rows]
            scores = [matmul(kv, query) for query in queries]
            after = []
            for (top, total), score, end in zip(carry, scores, ends):
                if masked:
                    score = masked_at(score, at * FWD_K, end, MASKED)
                new_top = jnp.maximum(top, jnp.max(score, axis=0, keepdims=True))
                weights = jnp.exp2(score * TO_LOG2 - new_top * TO_LOG2)
                factor = jnp.exp2((top - new_top) * TO_LOG2)
                total = total * factor + matmul(vt, weights.astype(BF16))
                after.append((new_top, total))
            return tuple(after)

        begin = (jnp.full((1, wide), MASKED, F32), jnp.zeros((HEAD_DIM + 16, wide), F32))
        full, last = spot[2 + 2 * tile], spot[3 + 2 * tile]
        carry = lax.fori_loop(0, full, functools.partial(step, False), (begin, begin))
        carry = lax.fori_loop(full, last, functools.partial(step, True), carry)
        for (top, total), start in zip(carry, starts):
            finish(total, top * TO_LOG2, start, wide)

    small = jnp.max(limit) <= 100.0

    @pl.when(small)
    def _():
        for tile in range(2 * SLICE // FWD_Q):
            bounded_tile(tile)

    @pl.when(jnp.logical_not(small))
    def _():
        for tile in range(2 * SLICE // FWD_Q):
            running_tile(tile)


def attention_forward(spot, queries, end, pieces):
    rows, total = 2 * SLICE, 16 * SLICE
    whole = pl.BlockSpec(memory_space=pltpu.VMEM)
    return pl.pallas_call(
        forward_kernel,
        out_shape=[
            jax.ShapeDtypeStruct((HEAD_DIM + 8, rows), F32),
            jax.ShapeDtypeStruct((16, HEAD_DIM, 128), BF16),
        ],
        in_specs=[pl.BlockSpec(memory_space=pltpu.SMEM), whole, whole]
        + [pl.BlockSpec(memory_space=pl.ANY)] * 14,
        out_specs=[whole] * 2,
        scratch_shapes=[
            pltpu.VMEM((total, 2 * HEAD_DIM), BF16),
            pltpu.VMEM((HEAD_DIM + 16, total), BF16),
            pltpu.VMEM((2 * HEAD_DIM, rows), BF16),
            pltpu.SemaphoreType.DMA((16,)),
        ],
        compiler_params=pltpu.CompilerParams(vmem_limit_bytes=58 << 20),
        cost_estimate=pl.CostEstimate(
            flops=20_000_000_000, bytes_accessed=9 << 20, transcendentals=1 << 20
        ),
        name="attention_forward",
    )(spot, queries, end, *pieces)


def backward_kernel(last, spot, *refs):
    q_refs, do_refs, state_refs, (end_ref, *kv_refs) = refs[:2], refs[2:4], refs[4:6], refs[6:11]
    if last:
        partial_ref, *refs = refs[11:]
        dq_refs, dkv_refs, scratch = refs[:2], refs[2:4], refs[4:]
    else:
        partial_ref, dkv_refs, scratch = refs[11], refs[12:14], refs[14:]
    kv_ref, kt_ref, q_ref, do_ref, qt_ref, dot_ref, lse_ref, delta_ref, sum_ref = scratch
    x, core = spot[0], spot[1]
    per_core = 2 * SLICE
    none = jnp.zeros((HEAD_DIM, 2 * per_core), BF16)
    qt_ref[HEAD_DIM:, :] = none
    dot_ref[:HEAD_DIM, :] = none
    for side in range(2):
        for chunk in range(16):
            lanes = pl.ds(side * per_core + chunk * 128, 128)
            qt_ref[:HEAD_DIM, lanes] = q_refs[side][chunk]
            dot_ref[HEAD_DIM:, lanes] = do_refs[side][chunk]
        rows = pl.ds(side * per_core, per_core)
        q_ref[rows, :] = qt_ref[:, rows].T
        do_ref[rows, :] = dot_ref[:, rows].T
        state = state_refs[side]
        lse_ref[:, rows] = state[HEAD_DIM:, :]
        product = state[:HEAD_DIM, :] * dot_ref[HEAD_DIM:, rows].astype(F32)
        delta_ref[:, rows] = jnp.broadcast_to(jnp.sum(product, axis=0, keepdims=True), (8, per_core))
    for i, ref in enumerate(kv_refs):
        rows = pl.ds(i * SLICE, SLICE)
        kv_ref[rows, :] = ref[:SLICE, :]
        kt_ref[:, rows] = kv_ref[rows, :].T[:HEAD_DIM, :]
    sum_ref[...] = jnp.zeros_like(sum_ref)

    @pl.loop(0, 2 * per_core // BWD_Q)
    def _(tile):
        span = pl.ds(pl.multiple_of(tile * BWD_Q, BWD_Q), BWD_Q)
        query_t, grad_t = qt_ref[:, span], dot_ref[:, span]
        query, grad = q_ref[span, :], do_ref[span, :]
        end, lse, delta = end_ref[:, span], lse_ref[:1, span], delta_ref[:1, span]
        full, upto = spot[2 + 2 * tile], spot[3 + 2 * tile]

        def step(masked, block, at, grad_query):
            held = pl.ds(pl.multiple_of(block * per_core + at * SLICE, SLICE), SLICE)
            kv = kv_ref[held, :]
            weights = jnp.exp2(matmul(kv, query_t) * TO_LOG2 - lse)
            if masked:
                begin = (4 * x_of[block] + 2 * at + core) * SLICE
                place = begin + lax.broadcasted_iota(jnp.int32, weights.shape, 0)
                weights = jnp.where(place < end, weights, 0.0)
            grad_scores = (weights * (matmul(kv, grad_t) - delta)).astype(BF16)
            sum_ref[held, :] += matmul(weights.astype(BF16), grad) + matmul(grad_scores, query)
            return grad_query + matmul(kt_ref[:, held], grad_scores)

        x_of = [x ^ 3, x] if last else [x ^ 1, x ^ 2]
        grad_query = partial_ref[:, span] if last else jnp.zeros((HEAD_DIM, BWD_Q), F32)
        for block in range(2):
            whole = jnp.clip(full - 2 * x_of[block], 0, 2)
            some = jnp.clip(upto - 2 * x_of[block], 0, 2)
            grad_query = lax.fori_loop(0, whole, functools.partial(step, False, block), grad_query)
            grad_query = lax.fori_loop(whole, some, functools.partial(step, True, block), grad_query)
        if last:
            done = (grad_query * HEAD_DIM ** (-0.5)).astype(BF16)
            chunks = BWD_Q // 128
            for side in range(2):

                @pl.when(tile // (per_core // BWD_Q) == side)
                def _(side=side):
                    base = (tile - side * (per_core // BWD_Q)) * chunks
                    for chunk in range(chunks):
                        dq_refs[side][base + chunk] = done[:, chunk * 128 : chunk * 128 + 128]

        else:
            partial_ref[:, span] = grad_query

    is_key = lax.broadcasted_iota(jnp.int32, (1, 2 * HEAD_DIM), 1) < HEAD_DIM
    scale = jnp.where(is_key, HEAD_DIM ** (-0.5), 1.0)
    for block in range(2):
        dkv_refs[block][...] = (sum_ref[pl.ds(block * per_core, per_core), :] * scale).astype(BF16)


def attention_backward(last, spot, queries, grads, states, end, kvs, partial=None):
    rows, wide = 2 * SLICE, 2 * HEAD_DIM
    whole = pl.BlockSpec(memory_space=pltpu.VMEM)
    block = jax.ShapeDtypeStruct((rows, wide), BF16)
    if last:
        out_shape = [jax.ShapeDtypeStruct((16, HEAD_DIM, 128), BF16)] * 2 + [block] * 2
        operands = (spot, *queries, *grads, *states, end, *kvs, partial)
    else:
        out_shape = [jax.ShapeDtypeStruct((HEAD_DIM, 2 * rows), F32), block, block]
        operands = (spot, *queries, *grads, *states, end, *kvs)
    return pl.pallas_call(
        functools.partial(backward_kernel, last),
        out_shape=out_shape,
        in_specs=[pl.BlockSpec(memory_space=pltpu.SMEM)] + [whole] * (len(operands) - 1),
        out_specs=[whole] * len(out_shape),
        scratch_shapes=[
            pltpu.VMEM((2 * rows, wide), BF16),
            pltpu.VMEM((HEAD_DIM, 2 * rows), BF16),
            pltpu.VMEM((2 * rows, wide), BF16),
            pltpu.VMEM((2 * rows, wide), BF16),
            pltpu.VMEM((wide, 2 * rows), BF16),
            pltpu.VMEM((wide, 2 * rows), BF16),
            pltpu.VMEM((8, 2 * rows), F32),
            pltpu.VMEM((8, 2 * rows), F32),
            pltpu.VMEM((2 * rows, wide), F32),
        ],
        compiler_params=pltpu.CompilerParams(vmem_limit_bytes=58 << 20),
        cost_estimate=pl.CostEstimate(
            flops=8_000_000_000, bytes_accessed=6 << 20, transcendentals=1 << 20
        ),
        name="attention_backward_two" if last else "attention_backward_one",
    )(*operands)


def on_device(
    tokens,
    block_ids,
    ln1_gain,
    ln1_shift,
    qkv_weight,
    qv_bias,
    out_weight,
    out_bias,
    ln2_gain,
    ln2_shift,
    up_weight,
    up_bias,
    down_weight,
    down_bias,
    cotangent,
):
    x, zl, core, y, zh = (lax.axis_index(name) for name in AXES)
    place = jnp.stack([x, zl, core, y, zh]).astype(jnp.int32)
    width = tokens.shape[1]
    gain_one, shift_one, gain_two, shift_two, bias_out = (
        values.astype(F32)[None]
        for values in (ln1_gain, ln1_shift, ln2_gain, ln2_shift, out_bias)
    )

    pieces = gather_y(tokens)
    own3 = qkv_weight.transpose(1, 0, 2)
    near3 = swap(halves(own3, 1, core)[0], "zh")
    far3 = swap(near3, "co")
    out_kept = halves(out_weight, 0, core)[0]
    biases = jnp.concatenate([qv_bias.reshape(256), up_bias])
    biases = jnp.pad(biases[None], ((0, 15), (0, width - 768)))
    out_near = swap(jnp.concatenate([out_kept, biases]), "zh")
    pair_bias, pair_up_bias = out_near[HEAD_DIM, :256].reshape(2, 128), out_near[HEAD_DIM, 256:768]
    out_kept = jnp.concatenate([out_kept, out_near[:HEAD_DIM]])

    table = gather(block_ids, ("x", "zl", "co"), 16)
    counts = jnp.sum(
        (table.reshape(-1)[None, :] <= jnp.arange(128, dtype=jnp.int32)[:, None]).astype(jnp.int32),
        axis=1,
    )
    places = (4 * x + core, 14 - 4 * x + core, 4 * x + 1 - core, 15 - 4 * x - core)
    query_ids = jnp.concatenate([lax.dynamic_index_in_dim(table, p, 0, False) for p in places])
    same = query_ids[None, :] == jnp.arange(128, dtype=jnp.int32)[:, None]
    end = jnp.sum(jnp.where(same, counts[:, None], 0), axis=0)
    spot = jnp.stack([x, core]).astype(jnp.int32)
    ends = end[: 2 * SLICE].reshape(-1, FWD_Q)
    bounds = jnp.stack([ends[:, 0] // FWD_K, (ends[:, -1] + FWD_K - 1) // FWD_K], axis=1)
    forward_spot = jnp.concatenate([spot, bounds.reshape(-1)])
    ends = end.reshape(-1, BWD_Q)
    bounds = jnp.stack([ends[:, 0] // SLICE, (ends[:, -1] + SLICE - 1) // SLICE], axis=1)
    backward_spot = jnp.concatenate([spot, ((bounds - core + 1) // 2).reshape(-1)])
    end = end[None, :]

    blocks, normed, unit = on_core(
        project_kernel,
        "project",
        [((4, 768, 128), BF16), ((512, width), BF16), ((512, width), BF16)],
        (place, *pieces, gain_one, shift_one, own3, near3, far3, qv_bias, pair_bias),
        800_000_000,
    )
    blocks, forward_spot, backward_spot, end, out_kept = lax.optimization_barrier(
        (blocks, forward_spot, backward_spot, end, out_kept)
    )
    mine = exchange(blocks, ("zl", "zh"))
    up_parts, down_parts = halves(up_weight, 1, core), halves(down_weight, 0, core)
    units = jnp.concatenate(
        [up_parts[0], down_parts[0].reshape(256, 4, 256).transpose(1, 0, 2).reshape(width, 256)]
    )
    rows_here = to_mirror(jnp.stack([tokens, cotangent]), zl)
    units = after(units, mine)
    tokens_here, cotangent_here = rows_here[0], rows_here[1]
    kv = mine[:, :512].reshape(2, 2, 4, 128, 128).transpose(0, 2, 1, 3, 4).reshape(2, SLICE, 128)
    near, next_near = [None] * 2, [None] * 2
    queries = mine[:, 512:].reshape(2, 2, 4, HEAD_DIM, 128).transpose(0, 2, 1, 3, 4)
    queries = queries.reshape(2, 512, 128)
    near[0], next_near[1] = hop(kv[0], 1), hop(jnp.concatenate([kv[1], queries[1]]), 3)
    near[1], next_near[0] = hop(kv[1], 1), hop(kv[0], 3)
    units_near = swap(units, "zh")
    far = [hop(near[0], 3), hop(next_near[1][:SLICE], 1)]
    far, near[1], next_near[0], units_near = lax.optimization_barrier(
        (far, near[1], next_near[0], units_near)
    )
    kv_pieces = [kv.reshape(2 * SLICE, 128), *near, *next_near, *far]
    kv_pieces += [swap(piece, "co") for piece in kv_pieces]

    queries = jnp.concatenate([queries[0], next_near[1][SLICE:]]).reshape(16, HEAD_DIM, 128)
    both = gather_y(jnp.concatenate([cotangent_here, out_kept]))
    state, mixed = attention_forward(forward_spot, queries, end[:, : 2 * SLICE], kv_pieces)
    mixed, both = lax.optimization_barrier((mixed, both))
    out_kept = jnp.concatenate([piece[128:] for piece in both])
    out_sent = swap(out_kept, "co")
    units_far = swap(units_near, "co")

    def parts_of(units):
        return units[:width], units[width:].reshape(4, 256, 256).transpose(1, 0, 2).reshape(256, width)

    (up_near, down_near), (up_far, down_far) = parts_of(units_near), parts_of(units_far)
    ups = (up_parts[0], up_near, up_parts[1], up_far)
    downs = (down_parts[0], down_near, down_parts[1], down_far)
    own_half, pair_half = halves(up_bias, 0, core), halves(pair_up_bias, 0, core)
    up_bias_all = jnp.concatenate([own_half[0], pair_half[0], own_half[1], pair_half[1]])
    up_bias_all = up_bias_all.astype(F32)[None]
    other_state, other_queries = swap(state, "co"), swap(queries, "co")

    heads = exchange(mixed, ("zl", "y", "zh"))
    resid, mid, att = on_core(
        attend_out_kernel,
        "attend_out",
        [((128, width), F32), ((128, width), BF16), ((2, 512, 128), BF16)],
        (place, heads, out_kept, out_sent, tokens_here, bias_out, gain_two, shift_two),
        270_000_000,
    )

    mids = gather_y(mid)
    row = ((128, width), BF16)
    active, grad_hidden, grad_mids, grad_up_bias = on_core(
        feed_forward_kernel,
        "feed_forward",
        [((512, width), BF16)] * 2 + [((4, 128, width), BF16), ((1, 1024), F32)],
        (place, *mids, *both, up_bias_all, *ups, *downs),
        3_300_000_000,
    )
    grad_mids = exchange(grad_mids, "y")
    (sent,) = on_core(
        functools.partial(unit_grads_kernel, False),
        "unit_grads_sent",
        [((8, 2, 128, 512), BF16)],
        (place, *mids, *both, active, grad_hidden),
        6_000_000_000,
    )
    got = swap(sent, "co")
    (ff_blocks,) = on_core(
        functools.partial(unit_grads_kernel, True),
        "unit_grads_kept",
        [((16, 256, 256), BF16)],
        (place, *mids, *both, active, grad_hidden, got),
        6_000_000_000,
        limit=56,
    )
    grad_mids = after(grad_mids, ff_blocks)
    grad_resid, grad_branch, grad_heads, norm_sums = on_core(
        mid_back_kernel,
        "mid_back",
        [((128, width), F32), row, ((16, HEAD_DIM, 128), BF16), ((4, width), F32)],
        (place, grad_mids, resid, cotangent_here, gain_two, out_kept, out_sent),
        270_000_000,
    )

    grad_mixed = exchange(grad_heads, ("zl", "y", "zh"))
    late = after((att, grad_branch, active), grad_heads)
    out_downs = on_core(
        out_down_kernel,
        "out_down",
        [((384, width), BF16)] * 4,
        (place, *late, *downs),
        1_400_000_000,
    )
    grad_mixed, backward_spot = after((grad_mixed, backward_spot), ff_blocks, out_downs)
    ff_blocks = after(ff_blocks, out_downs)
    out_downs = send_y(out_downs)
    other_grad = swap(grad_mixed, "co")
    ff_shares = exchange(ff_blocks, ("x", "zl", "zh"))
    all_queries, grads = [queries, other_queries], [grad_mixed, other_grad]
    states = [state, other_state]
    partial, to_near, to_far = attention_backward(
        False, backward_spot, all_queries, grads, states, end, [*near, *far]
    )
    from_near, from_far = hop(to_near, 1), hop(to_far, 2)
    grad_q, grad_q_sent, to_next, grad_kv = attention_backward(
        True, backward_spot, all_queries, grads, states, end, [*next_near, kv[0], kv[1]], partial
    )
    to_next, grad_q_sent, from_near, from_far, ff_shares, out_downs = lax.optimization_barrier(
        (to_next, grad_q_sent, from_near, from_far, ff_shares, out_downs)
    )
    from_next = hop(to_next, 3)
    grad_q = total([grad_q, swap(grad_q_sent, "co")]).astype(BF16)
    grad_q = jnp.stack([grad_q[:8], hop(grad_q[8:], 3)])
    grad_q = grad_q.reshape(2, 4, 2, HEAD_DIM, 128).transpose(0, 2, 1, 3, 4).reshape(4, 256, 128)

    grad_kv = total([grad_kv, from_near, from_far, from_next])
    grad_kv = grad_kv.astype(BF16).reshape(2, SLICE, 128)
    blocks = jnp.concatenate([to_z(grad_kv), grad_q], axis=1)
    ff_shares, out_downs = after((ff_shares, out_downs), blocks)
    blocks = exchange(blocks, ("zl", "zh"))

    ff_share = jnp.sum(ff_shares.astype(F32), axis=0)
    ff_share = jnp.concatenate(
        [ff_share[:128].T, ff_share[128:, :128], ff_share[128:, 128:]]
    ).astype(BF16)
    rows_home, out_kept_sum, out_sent_sum = on_core(
        out_sums_kernel,
        "out_sums",
        [((2, 128, width), F32), ((4, 2, 2, HEAD_DIM, 128), F32), ((4, 2, 2, HEAD_DIM, 128), BF16)],
        (place, *out_downs, resid, down_bias.astype(F32)[None], grad_resid),
        1_000_000,
    )
    unit, out_sent_sum = after((unit, out_sent_sum), rows_home)
    out_got = swap(out_sent_sum, "co")

    *grad_normed, part_sums = on_core(
        project_back_kernel,
        "project_back",
        [row] * 4 + [((2, width), F32)],
        (place, blocks, unit, own3, near3, far3),
        800_000_000,
        scratch=[pltpu.VMEM((512, width), F32)],
    )
    grad_normed = send_y(grad_normed)
    blocks, ff_share = after((blocks, ff_share), part_sums)
    ff_rest = gather(ff_share, ("x", "zl"), 8)

    by_head, head_sums = on_core(
        qkv_grads_kernel,
        "qkv_grads",
        [((2, 4, 2, 2, 192, 128), BF16), ((4, 192, 128), F32)],
        (place, blocks, normed),
        900_000_000,
    )
    head_got = swap(by_head[1], "co")
    rows_home = to_mirror(after(rows_home, head_got), zl)

    head_sums = head_sums[:, :, 0].reshape(2, 2, 3, HEAD_DIM)
    bias = jnp.stack([head_sums[:, :, 2], head_sums[:, :, 1]]).transpose(2, 0, 1, 3)
    up_sums = grad_up_bias.reshape(2, 2, 256)
    up_sums = turned(turned(up_sums, 0, core), 1, zh).transpose(1, 0, 2).reshape(1, width)
    bias = jnp.pad(bias.reshape(1, 512), ((0, 0), (0, 512)))
    small = jnp.concatenate([part_sums, norm_sums, up_sums, bias])
    small = small + swap(small, "co")
    (shares,) = on_core(
        shares_kernel,
        "shares",
        [((16, 272, 128), BF16)],
        (place, by_head, head_got, out_kept_sum, out_got, small),
        1_000_000,
    )
    shares = exchange(shares, ("x", "zl", "zh"))
    share = jnp.sum(shares.astype(F32), axis=0).astype(BF16)
    rest = gather(share, ("x", "zl"), 8)
    small = rest[:, 256:264].astype(F32).transpose(1, 0, 2).reshape(8, width)
    for bit in (1, 3):
        small = jnp.concatenate([small[:6] + hop(small[:6], bit, "y"), small[6:]])
    grad_up_bias = lax.dynamic_slice_in_dim(small[6], zh * 512, 512, 0)
    grad_qv_bias = lax.dynamic_slice_in_dim(small[7], zh * 256, 256, 0).reshape(2, 128)

    (grad_tokens,) = on_core(
        last_norm_kernel,
        "last_norm",
        [((128, width), F32)],
        (place, *grad_normed, tokens, gain_one, rows_home[1]),
        1_000_000,
    )
    grad_down_weight, grad_up_weight = on_core(
        unit_weights_kernel,
        "unit_weights",
        [((512, width), F32), ((width, 512), F32)],
        (place, ff_rest, swap(ff_rest, "co")),
        1_000_000,
    )
    grad_qkv_weight, grad_out_weight = on_core(
        head_weights_kernel,
        "head_weights",
        [((3, width, 128), F32), ((128, width), F32)],
        (place, rest, swap(rest, "co")),
        1_000_000,
    )
    return (
        rows_home[0],
        grad_tokens,
        small[0],
        small[1],
        grad_qkv_weight.transpose(1, 0, 2),
        grad_qv_bias,
        grad_out_weight,
        small[2],
        small[3],
        small[4],
        grad_up_weight,
        grad_up_bias,
        grad_down_weight,
        small[5],
    )


def solution(mesh):
    fine = Mesh(mesh.devices.reshape(4, 2, 2, 4, 2), AXES)
    slices, shards = ("x", "zl", "co"), ("y", "zh")
    return jax.shard_map(
        on_device,
        mesh=fine,
        in_specs=(
            P(AXES, None),
            P(slices),
            P(),
            P(),
            P(None, None, shards),
            P(None, shards),
            P(shards, None),
            P(),
            P(),
            P(),
            P(None, shards),
            P(shards),
            P(shards, None),
            P(),
            P(AXES, None),
        ),
        out_specs=(
            P(AXES, None),
            P(AXES, None),
            P(),
            P(),
            P(None, None, shards),
            P(None, shards),
            P(shards, None),
            P(),
            P(),
            P(),
            P(None, shards),
            P(shards),
            P(shards, None),
            P(),
        ),
        check_vma=False,
    )
```

time: 589 us -> 432 us (0.73)
  waiting for transfers between devices: 206 us -> 86.6 us
  Pallas kernels: 100 us -> 138 us
  matrix products: 30.8 us -> 0 us
  other arithmetic: 37.8 us -> 20.7 us
  between operations: 16.1 us -> 2.23 us
  blocking collectives: 12.9 us -> 0 us
  starting transfers between devices: 114 us -> 120 us
    psum x1 -> x0, waiting for transfers between devices: 45.6 us -> none  [on_device(): grad_down, grad_up = lax.psum((grad_down, grad_up), ('x', 'zl'))]
    pallas_call x2 -> x17, Pallas kernels: 100 us -> 138 us  [the longest x2 59.5 us: attention_backward(): pl.pallas_call(functools.partial(backward_kernel, last), out_shape=out_sh...]
    all_to_all x12 -> x10, waiting for transfers between devices: 73.4 us -> 42.4 us  [exchange(): return lax.all_to_all(blocks, axes, 0, 0, tiled=True)]
    dot_general x12 -> x0, matrix products: 30.8 us -> none  [the longest x11 28.7 us: contract(): lax.dot_general(left, right, (((left_dim,), (right_dim,)), ((), ())), pre...]
    ppermute x14 -> x29, waiting for transfers between devices: 58.2 us -> 35 us  [the longest x12 25.7 us: hop(): return lax.ppermute(values, axis, [(i, i ^ bit) for i in range(4)])]
    unnamed x118 -> x198, local copies, waits for them, and re-layouts: 14 us -> 32 us
    convert_element_type x18 -> x3, other arithmetic: 18.1 us -> 2.57 us  [the longest x1 1.48 us: on_device(): grad_kv = grad_kv.astype(BF16).reshape(2, SLICE, 128)]
    ppermute x23, waiting for transfers between devices: 24.1 us -> 9.23 us  [swap(): return lax.ppermute(values, axis, [(0, 1), (1, 0)])]
  transfers between devices with their start and end apart: 56 -> 62, of which waited for: 28 -> 17; matrix products, arithmetic and copies ran while one was open for 19% -> 10% of each run, Pallas kernels for 7% -> 28%
where the time goes in v2:
time: 432 us; the launch traced here: 425 us
  Pallas kernels  138 us (32%)
  starting transfers between devices  120 us (28%)
  waiting for transfers between devices  86.6 us (20%)
  local copies, waits for them, and re-layouts  57.8 us (13%)
  other arithmetic  20.7 us (5%)
    pallas_call x2, Pallas kernels, attention_backward(): pl.pallas_call(functools.partial(backward_kernel, last), out_shape=out_sh...  59.5 us
    all_to_all x10, starting transfers between devices, exchange(): return lax.all_to_all(blocks, axes, 0, 0, tiled=True)  52.5 us
    all_to_all x10, waiting for transfers between devices, exchange(): return lax.all_to_all(blocks, axes, 0, 0, tiled=True)  42.4 us
    pallas_call x14, Pallas kernels, on_core(): pl.pallas_call(kernel, out_shape=outputs, in_specs=[pl.BlockSpec(memory_s...  39.6 us
    pallas_call x1, Pallas kernels, attention_forward(): pl.pallas_call(forward_kernel, out_shape=[jax.ShapeDtypeStruct((HEAD_DIM...  38.5 us
    unnamed x198, local copies, waits for them, and re-layouts  32 us
    ppermute x23, starting transfers between devices, swap(): return lax.ppermute(values, axis, [(0, 1), (1, 0)])  29.7 us
    ppermute x12, waiting for transfers between devices, hop(): return lax.ppermute(values, axis, [(i, i ^ bit) for i in range(4)])  25.7 us
  transfers between devices with their start and end apart: 62, of which 17 were waited for; matrix products, arithmetic and copies ran while one was open for 10% of the time, Pallas kernels for 28%

profile of v2, /device:TPU:1, one launch (start us, length us, event | category | flops | bytes accessed | tf_op | source)
XLA Modules:
  0.0 424.6 jit_solution(1754341157782543886)
XLA Ops:
  0.7 2.2 collective-permute-start
  2.9 2.6 collective-permute-start.1
  7.9 7.2 %all-to-all-start = ((s32[16,1,1024]{2,1,0:T(1,128)}), s32[16,1,1024]{2,1,0:T(1,128)S(1)}, u32[]{:S(2)}, u32[]{:S(2)}) async-start(s32[16,1,1024]{2,1,0:T(1,128)} %broadcast_in_dim.76), calls=%async_computation | async-start | bytes 131072 | tf_op jit(solution)/shard_map/all_to_all | solution.py:51
  16.1 3.4 collective-permute-start.3
  23.6 5.8 %collective-permute-done.3.refs_7_.near = bf16[3,512,128]{2,1,0:T(8,128)(2,1)S(1)} collective-permute-done((bf16[3,512,128]{2,1,0:T(8,128)(2,1)S(1)}, bf16[3,512,128]{2,1,0:T(8,128)(2,1)S(1)}, u32[]{:S(2)}, u32[]{:S(2)}) %collective-permute-start.3) | collective-permute-done | bytes 393248 | tf_op jit(solution)/shard_map/ppermute | solution.py:42
  33.8 4.0 project.1
  39.8 3.5 all-to-all-start.1
  45.6 2.1 constant_dynamic-slice_fusion
  48.8 2.1 constant_dynamic-slice_fusion.1
  52.0 3.3 all-to-all-done.1
  56.3 2.4 collective-permute-start.6
  60.5 6.1 %collective-permute-done.6.refs_4_.refs_8_ = bf16[1536,128]{1,0:T(8,128)(2,1)S(1)} collective-permute-done((bf16[1536,128]{1,0:T(8,128)(2,1)S(1)}, bf16[1536,128]{1,0:T(8,128)(2,1)S(1)}, u32[]{:S(2)}, u32[]{:S(2)}) %collective-permute-start.6) | collective-permute-done | bytes 393248 | tf_op jit(solution)/shard_map/ppermute | solution.py:38
  66.6 4.7 %collective-permute-start.13 = (bf16[2048,128]{1,0:T(8,128)(2,1)S(1)}, bf16[2048,128]{1,0:T(8,128)(2,1)}, u32[]{:S(2)}, u32[]{:S(2)}) collective-permute-start(bf16[2048,128]{1,0:T(8,128)(2,1)S(1)} %bitcast.117), channel_id=1, source_target_pairs={{0,8},{8,0},{1,9},{9,1},{2,10},{10,2},{3,11},{11,3},{4,12},{12,4},... | collective-permute-start | bytes 1572872 | tf_op jit(solution)/shard_map/ppermute | solution.py:42
  71.4 2.4 collective-permute-start.8
  76.5 4.4 %collective-permute-done.8.refs_5_.refs_9_ = bf16[1024,128]{1,0:T(8,128)(2,1)} collective-permute-done((bf16[1024,128]{1,0:T(8,128)(2,1)}, bf16[1024,128]{1,0:T(8,128)(2,1)}, u32[]{:S(2)}, u32[]{:S(2)}) %collective-permute-start.8) | collective-permute-done | bytes 262176 | tf_op jit(solution)/shard_map/ppermute | solution.py:38
  87.7 2.0 collective-permute-start.23
  90.4 38.5 %attention_forward.1 = (f32[72,2048]{1,0:T(8,128)}, bf16[16,64,128]{2,1,0:T(8,128)(2,1)}) custom-call(s32[6]{0:T(128)} %pad_add_fusion.2.spot, bf16[16,64,128]{2,1,0:T(8,128)(2,1)} %bitcast.138, s32[1,2048]{1,0:T(1,128)} %slice.189.end_ref, bf16[2048,128]{1,0:T(8,128)(2,1)} %bitcast.118, bf16[1024,128]{1,0:T(8,128)(2,1)} %collective-permute-done.7.refs_1_.refs_7_, ...), custom_call_target="tpu_custom_call" | custom-call | flops 20000000000 | bytes 9437184 | tf_op jit(solution)/shard_map/attention_forward/pallas_call | solution.py:486
  131.5 6.9 %all-to-all-start.2 = ((bf16[16,64,128]{2,1,0:T(8,128)(2,1)}), bf16[16,64,128]{2,1,0:T(8,128)(2,1)}, u32[]{:S(2)}, u32[]{:S(2)}) async-start(bf16[16,64,128]{2,1,0:T(8,128)(2,1)} %get-tuple-element.108), calls=%async_computation.2 | async-start | bytes 524288 | tf_op jit(solution)/shard_map/all_to_all | solution.py:51
  138.4 2.1 fusion.11
  141.8 4.8 %all-to-all-done.2.heads = bf16[16,64,128]{2,1,0:T(8,128)(2,1)} async-done(((bf16[16,64,128]{2,1,0:T(8,128)(2,1)}), bf16[16,64,128]{2,1,0:T(8,128)(2,1)}, u32[]{:S(2)}, u32[]{:S(2)}) %all-to-all-start.2) | async-done | bytes 262176 | tf_op jit(solution)/shard_map/all_to_all | solution.py:51
  147.5 1.7 attend_out.1
  149.4 1.7 collective-permute-start.26
  151.2 1.7 collective-permute-start.27
  154.7 2.9 collective-permute-done.25.refs_1_
  157.7 3.8 collective-permute-done.26.refs_2_
  161.4 2.6 collective-permute-done.27.refs_3_
  164.1 5.1 %feed_forward.1 = (bf16[512,1024]{1,0:T(8,128)(2,1)S(1)}, bf16[512,1024]{1,0:T(8,128)(2,1)S(1)}, bf16[4,128,1024]{2,1,0:T(8,128)(2,1)S(1)}, f32[1,1024]{1,0:T(1,128)S(1)}) custom-call(s32[5]{0:T(128)S(1)} %stack.57.place, bf16[128,1024]{1,0:T(8,128)(2,1)S(1)} %get-tuple-element.113.refs_0_, bf16[128,1024]{1,0:T(8,128)(2,1)S(1)} %collective-permute-done.25.refs_1_, ...), custom_call_target="tpu_custom_call" | custom-call | flops 3300000000 | bytes 4194304 | tf_op jit(solution)/shard_map/feed_forward/pallas_call | solution.py:95
  169.3 3.2 unit_grads_sent.1
  172.4 1.6 collective-permute-start.29
  174.1 3.6 all-to-all-start.3
  178.2 5.8 %unit_grads_kept.1 = bf16[16,256,256]{2,1,0:T(8,128)(2,1)} custom-call(s32[5]{0:T(128)} %copy-done.52, bf16[128,1024]{1,0:T(8,128)(2,1)} %copy-done.60, bf16[128,1024]{1,0:T(8,128)(2,1)} %copy-done.61, bf16[128,1024]{1,0:T(8,128)(2,1)} %copy-done.62, bf16[128,1024]{1,0:T(8,128)(2,1)} %copy-done.63, bf16[256,1024]{1,0:T(8,128)(2,1)} %copy-done.13, ...), custom_call_target="tpu_custom_call" | custom-call | flops 6000000000 | bytes 4194304 | tf_op jit(solution)/shard_map/unit_grads_kept/pallas_call | solution.py:95
  184.0 8.6 %all-to-all-done.3.refs_0_ = bf16[4,128,1024]{2,1,0:T(8,128)(2,1)S(1)} async-done(((bf16[4,128,1024]{2,1,0:T(8,128)(2,1)}), bf16[4,128,1024]{2,1,0:T(8,128)(2,1)S(1)}, u32[]{:S(2)}, u32[]{:S(2)}) %all-to-all-start.3) | async-done | bytes 1048608 | tf_op jit(solution)/shard_map/all_to_all | solution.py:51
  193.7 1.8 mid_back.1
  197.6 3.5 all-to-all-start.4
  209.7 2.3 out_down.1
  213.8 7.2 %all-to-all-start.5 = ((bf16[16,256,256]{2,1,0:T(8,128)(2,1)}), bf16[16,256,256]{2,1,0:T(8,128)(2,1)}, u32[]{:S(2)}, u32[]{:S(2)}) async-start(bf16[16,256,256]{2,1,0:T(8,128)(2,1)} %unit_grads_kept.1), calls=%async_computation.5 | async-start | bytes 4194304 | tf_op jit(solution)/shard_map/all_to_all | solution.py:51
  221.6 2.4 collective-permute-start.35
  224.0 2.1 collective-permute-start.37
  226.8 26.7 %attention_backward_one.1 = (f32[64,4096]{1,0:T(8,128)}, bf16[2048,128]{1,0:T(8,128)(2,1)}, bf16[2048,128]{1,0:T(8,128)(2,1)}) custom-call(s32[10]{0:T(128)} %pad_add_fusion.3.spot, bf16[16,64,128]{2,1,0:T(8,128)(2,1)} %bitcast.139, bf16[16,64,128]{2,1,0:T(8,128)(2,1)} %copy-done.95, bf16[16,64,128]{2,1,0:T(8,128)(2,1)} %copy-done.81, ...), custom_call_target="tpu_custom_call" | custom-call | flops 8000000000 | bytes 6291456 | tf_op jit(solution)/shard_map/attention_backward_one/pallas_call | solution.py:597
  253.5 1.6 collective-permute-start.33
  255.1 2.4 collective-permute-start.34
  257.5 32.9 %attention_backward_two.1 = (bf16[16,64,128]{2,1,0:T(8,128)(2,1)}, bf16[16,64,128]{2,1,0:T(8,128)(2,1)}, bf16[2048,128]{1,0:T(8,128)(2,1)}, bf16[2048,128]{1,0:T(8,128)(2,1)}) custom-call(s32[10]{0:T(128)} %pad_add_fusion.3.spot, bf16[16,64,128]{2,1,0:T(8,128)(2,1)} %bitcast.140, bf16[16,64,128]{2,1,0:T(8,128)(2,1)} %copy-done.95, ...), custom_call_target="tpu_custom_call" | custom-call | flops 8000000000 | bytes 6291456 | tf_op jit(solution)/shard_map/attention_backward_two/pallas_call | solution.py:597
  292.2 7.5 %collective-permute-start.39 = (bf16[16,64,128]{2,1,0:T(8,128)(2,1)}, bf16[16,64,128]{2,1,0:T(8,128)(2,1)S(1)}, u32[]{:S(2)}, u32[]{:S(2)}) collective-permute-start(bf16[16,64,128]{2,1,0:T(8,128)(2,1)} %get-tuple-element.150), channel_id=1, source_target_pairs={{0,8},{8,0},{1,9},{9,1},{2,10},{10,2},{3,11},{11,3},{4,12},{12,4},... | collective-permute-start | bytes 786440 | tf_op jit(solution)/shard_map/ppermute | solution.py:42
  304.9 12.5 %collective-permute-done.40 = bf16[8,64,128]{2,1,0:T(8,128)(2,1)S(1)} collective-permute-done((bf16[8,64,128]{2,1,0:T(8,128)(2,1)S(1)}, bf16[8,64,128]{2,1,0:T(8,128)(2,1)S(1)}, u32[]{:S(2)}, u32[]{:S(2)}) %collective-permute-start.40) | collective-permute-done | bytes 131104 | tf_op jit(solution)/shard_map/ppermute | solution.py:38
  317.5 1.5 add_convert_fusion
  320.0 4.0 all-to-all-start.6
  329.7 2.7 reduce.1
  334.8 1.5 pad_maximum_fusion.9
  336.4 3.7 project_back.1
  341.9 4.6 %all-to-all-start.9 = ((bf16[8,512,128]{2,1,0:T(8,128)(2,1)}), bf16[8,512,128]{2,1,0:T(8,128)(2,1)S(1)}, u32[]{:S(2)}, u32[]{:S(2)}) async-start(bf16[8,512,128]{2,1,0:T(8,128)(2,1)} %broadcast_in_dim.89), calls=%async_computation.9 | async-start | bytes 2097152 | tf_op jit(solution)/shard_map/all_to_all | solution.py:51
  348.8 1.8 qkv_grads.1
  352.3 1.7 collective-permute-start.41
  356.4 1.6 collective-permute-start.42
  358.1 2.4 shares.1
  360.9 6.9 %all-to-all-start.7 = ((bf16[16,272,128]{2,1,0:T(8,128)(2,1)}), bf16[16,272,128]{2,1,0:T(8,128)(2,1)}, u32[]{:S(2)}, u32[]{:S(2)}) async-start(bf16[16,272,128]{2,1,0:T(8,128)(2,1)} %shares.1), calls=%async_computation.7 | async-start | bytes 2228224 | tf_op jit(solution)/shard_map/all_to_all | solution.py:51
  370.3 1.8 collective-permute-start.45
  372.1 25.3 %all-to-all-done.7 = bf16[16,272,128]{2,1,0:T(8,128)(2,1)} async-done(((bf16[16,272,128]{2,1,0:T(8,128)(2,1)}), bf16[16,272,128]{2,1,0:T(8,128)(2,1)}, u32[]{:S(2)}, u32[]{:S(2)}) %all-to-all-start.7) | async-done | bytes 1114144 | tf_op jit(solution)/shard_map/all_to_all | solution.py:51
  399.7 5.0 %all-to-all-start.8 = ((bf16[8,272,128]{2,1,0:T(8,128)(2,1)}), bf16[8,272,128]{2,1,0:T(8,128)(2,1)S(1)}, u32[]{:S(2)}, u32[]{:S(2)}) async-start(bf16[8,272,128]{2,1,0:T(8,128)(2,1)} %broadcast_in_dim.88), calls=%async_computation.8 | async-start | bytes 1114112 | tf_op jit(solution)/shard_map/all_to_all | solution.py:51
  408.8 1.8 last_norm.1
  410.6 3.0 unit_weights.1
  413.6 1.6 collective-permute-start.48
  415.2 2.3 collective-permute-start.50
  418.9 2.7 collective-permute-done.49
  422.2 2.1 head_weights.1
  (384 shorter events, 88.6 us)
Async XLA Ops:
  0.7 33.0 %collective-permute-start = (bf16[128,1024]{1,0:T(8,128)(2,1)}, bf16[128,1024]{1,0:T(8,128)(2,1)S(1)}, u32[]{:S(2)}, u32[]{:S(2)}) collective-permute-start(bf16[128,1024]{1,0:T(8,128)(2,1)} %refs_4_.1), channel_id=1, source_target_pairs={{0,2},{2,4},{4,6},{6,0},{1,3},{3,5},{5,7},{7,1},{8,10},{10,12},{12... | collective-permute-start | bytes 786440 | tf_op jit(solution)/shard_map/ppermute | solution.py:34
  2.9 30.8 %collective-permute-start.1 = (bf16[128,1024]{1,0:T(8,128)(2,1)}, bf16[128,1024]{1,0:T(8,128)(2,1)S(1)}, u32[]{:S(2)}, u32[]{:S(2)}) collective-permute-start(bf16[128,1024]{1,0:T(8,128)(2,1)} %refs_4_.1), channel_id=1, source_target_pairs={{0,4},{2,6},{4,0},{6,2},{1,5},{3,7},{5,1},{7,3},{8,12},{10,14},{12... | collective-permute-start | bytes 786440 | tf_op jit(solution)/shard_map/ppermute | solution.py:34
  5.5 28.2 %collective-permute-start.2 = (bf16[128,1024]{1,0:T(8,128)(2,1)}, bf16[128,1024]{1,0:T(8,128)(2,1)S(1)}, u32[]{:S(2)}, u32[]{:S(2)}) collective-permute-start(bf16[128,1024]{1,0:T(8,128)(2,1)} %refs_4_.1), channel_id=1, source_target_pairs={{0,6},{2,0},{4,2},{6,4},{1,7},{3,1},{5,3},{7,5},{8,14},{10,8},{12,... | collective-permute-start | bytes 786440 | tf_op jit(solution)/shard_map/ppermute | solution.py:34
  7.9 13.9 %all-to-all-start = ((s32[16,1,1024]{2,1,0:T(1,128)}), s32[16,1,1024]{2,1,0:T(1,128)S(1)}, u32[]{:S(2)}, u32[]{:S(2)}) async-start(s32[16,1,1024]{2,1,0:T(1,128)} %broadcast_in_dim.76), calls=%async_computation | async-start | bytes 131072 | tf_op jit(solution)/shard_map/all_to_all | solution.py:51
  16.1 13.3 %collective-permute-start.3 = (bf16[3,512,128]{2,1,0:T(8,128)(2,1)S(1)}, bf16[3,512,128]{2,1,0:T(8,128)(2,1)S(1)}, u32[]{:S(2)}, u32[]{:S(2)}) collective-permute-start(bf16[3,512,128]{2,1,0:T(8,128)(2,1)S(1)} %dynamic-slice_bitcast_fusion), channel_id=1, source_target_pairs={{0,1},{1,0},{2,3},{3,2},{4,5},{5,4},{6,7},{7,6},{8,9},{9,8},{10,11... | collective-permute-start | bytes 1179656 | tf_op jit(solution)/shard_map/ppermute | solution.py:42
  20.3 12.7 %collective-permute-start.5 = (bf16[80,1024]{1,0:T(8,128)(2,1)S(1)}, bf16[80,1024]{1,0:T(8,128)(2,1)S(1)}, u32[]{:S(2)}, u32[]{:S(2)}) collective-permute-start(bf16[80,1024]{1,0:T(8,128)(2,1)S(1)} %fusion.1), channel_id=1, source_target_pairs={{0,1},{1,0},{2,3},{3,2},{4,5},{5,4},{6,7},{7,6},{8,9},{9,8},{10,11... | collective-permute-start | bytes 491528 | tf_op jit(solution)/shard_map/ppermute | solution.py:42
  21.8 147.4 %copy-start.52 = (s32[5]{0:T(128)}, s32[5]{0:T(128)S(1)}, u32[]{:S(2)}) copy-start(s32[5]{0:T(128)S(1)} %stack.57.place) | copy-start | bytes 64
  29.4 4.3 %collective-permute-start.4 = (bf16[3,512,128]{2,1,0:T(8,128)(2,1)S(1)}, bf16[3,512,128]{2,1,0:T(8,128)(2,1)S(1)}, u32[]{:S(2)}, u32[]{:S(2)}) collective-permute-start(bf16[3,512,128]{2,1,0:T(8,128)(2,1)S(1)} %collective-permute-done.3.refs_7_.near), channel_id=1, source_target_pairs={{0,8},{8,0},{1,9},{9,1},{2,10},{10,2},{3,11},{11,3},{4,12},{12,4},... | collective-permute-start | bytes 1179656 | tf_op jit(solution)/shard_map/ppermute | solution.py:42
  39.8 15.6 %all-to-all-start.1 = ((bf16[4,768,128]{2,1,0:T(8,128)(2,1)}), bf16[4,768,128]{2,1,0:T(8,128)(2,1)S(1)}, u32[]{:S(2)}, u32[]{:S(2)}) async-start(bf16[4,768,128]{2,1,0:T(8,128)(2,1)} %get-tuple-element.99), calls=%async_computation.1 | async-start | bytes 1572864 | tf_op jit(solution)/shard_map/all_to_all | solution.py:51
  44.1 16.0 %collective-permute-start.20 = (bf16[2,128,1024]{2,1,0:T(8,128)(2,1)}, bf16[2,128,1024]{2,1,0:T(8,128)(2,1)}, u32[]{:S(2)}, u32[]{:S(2)}) collective-permute-start(bf16[2,128,1024]{2,1,0:T(8,128)(2,1)} %pad_maximum_fusion.3), channel_id=1, source_target_pairs={{16,112},{48,80},{80,48},{112,16},{17,113},{49,81},{81,49},{113,17... | collective-permute-start | bytes 1572872 | tf_op jit(solution)/shard_map/ppermute | solution.py:46
  47.6 116.4 %copy-start.9 = (bf16[256,1024]{1,0:T(8,128)(2,1)}, bf16[256,1024]{1,0:T(8,128)(2,1)S(1)}, u32[]{:S(2)}) copy-start(bf16[256,1024]{1,0:T(8,128)(2,1)S(1)} %get-tuple-element.185.refs_13_.refs_0_) | copy-start | bytes 1572868
  55.3 26.4 %collective-permute-start.12 = (bf16[2048,256]{1,0:T(8,128)(2,1)}, bf16[2048,256]{1,0:T(8,128)(2,1)}, u32[]{:S(2)}, u32[]{:S(2)}) collective-permute-start(bf16[2048,256]{1,0:T(8,128)(2,1)} %pad_maximum_fusion), channel_id=1, source_target_pairs={{0,1},{1,0},{2,3},{3,2},{4,5},{5,4},{6,7},{7,6},{8,9},{9,8},{10,11... | collective-permute-start | bytes 3145736 | tf_op jit(solution)/shard_map/ppermute | solution.py:42
  56.3 10.3 %collective-permute-start.6 = (bf16[1536,128]{1,0:T(8,128)(2,1)S(1)}, bf16[1536,128]{1,0:T(8,128)(2,1)S(1)}, u32[]{:S(2)}, u32[]{:S(2)}) collective-permute-start(bf16[1536,128]{1,0:T(8,128)(2,1)S(1)} %pad_maximum_fusion.5), channel_id=1, source_target_pairs={{0,96},{32,64},{64,32},{96,0},{1,97},{33,65},{65,33},{97,1},{2,98}... | collective-permute-start | bytes 1179656 | tf_op jit(solution)/shard_map/ppermute | solution.py:38
  58.7 12.7 %collective-permute-start.7 = (bf16[1024,128]{1,0:T(8,128)(2,1)S(1)}, bf16[1024,128]{1,0:T(8,128)(2,1)}, u32[]{:S(2)}, u32[]{:S(2)}) collective-permute-start(bf16[1024,128]{1,0:T(8,128)(2,1)S(1)} %bitcast.142), channel_id=1, source_target_pairs={{0,32},{32,0},{64,96},{96,64},{1,33},{33,1},{65,97},{97,65},{2,34}... | collective-permute-start | bytes 786440 | tf_op jit(solution)/shard_map/ppermute | solution.py:38
  58.7 15.1 %collective-permute-start.10 = (bf16[1024,128]{1,0:T(8,128)(2,1)S(1)}, bf16[1024,128]{1,0:T(8,128)(2,1)S(1)}, u32[]{:S(2)}, u32[]{:S(2)}) collective-permute-start(bf16[1024,128]{1,0:T(8,128)(2,1)S(1)} %bitcast.127), channel_id=1, source_target_pairs={{0,32},{32,0},{64,96},{96,64},{1,33},{33,1},{65,97},{97,65},{2,34}... | collective-permute-start | bytes 786440 | tf_op jit(solution)/shard_map/ppermute | solution.py:38
  60.2 13.7 %collective-permute-start.11 = (bf16[1024,128]{1,0:T(8,128)(2,1)S(1)}, bf16[1024,128]{1,0:T(8,128)(2,1)S(1)}, u32[]{:S(2)}, u32[]{:S(2)}) collective-permute-start(bf16[1024,128]{1,0:T(8,128)(2,1)S(1)} %bitcast.143), channel_id=1, source_target_pairs={{0,96},{32,64},{64,32},{96,0},{1,97},{33,65},{65,33},{97,1},{2,98}... | collective-permute-start | bytes 786440 | tf_op jit(solution)/shard_map/ppermute | solution.py:38
  66.6 16.6 %collective-permute-start.13 = (bf16[2048,128]{1,0:T(8,128)(2,1)S(1)}, bf16[2048,128]{1,0:T(8,128)(2,1)}, u32[]{:S(2)}, u32[]{:S(2)}) collective-permute-start(bf16[2048,128]{1,0:T(8,128)(2,1)S(1)} %bitcast.117), channel_id=1, source_target_pairs={{0,8},{8,0},{1,9},{9,1},{2,10},{10,2},{3,11},{11,3},{4,12},{12,4},... | collective-permute-start | bytes 1572872 | tf_op jit(solution)/shard_map/ppermute | solution.py:42
  71.4 9.5 %collective-permute-start.8 = (bf16[1024,128]{1,0:T(8,128)(2,1)}, bf16[1024,128]{1,0:T(8,128)(2,1)}, u32[]{:S(2)}, u32[]{:S(2)}) collective-permute-start(bf16[1024,128]{1,0:T(8,128)(2,1)} %collective-permute-done.7.refs_1_.refs_7_), channel_id=1, source_target_pairs={{0,96},{32,64},{64,32},{96,0},{1,97},{33,65},{65,33},{97,1},{2,98}... | collective-permute-start | bytes 786440 | tf_op jit(solution)/shard_map/ppermute | solution.py:38
  73.8 7.9 %collective-permute-start.9 = (bf16[1024,128]{1,0:T(8,128)(2,1)S(1)}, bf16[1024,128]{1,0:T(8,128)(2,1)}, u32[]{:S(2)}, u32[]{:S(2)}) collective-permute-start(bf16[1024,128]{1,0:T(8,128)(2,1)S(1)} %slice.239), channel_id=1, source_target_pairs={{0,32},{32,0},{64,96},{96,64},{1,33},{33,1},{65,97},{97,65},{2,34}... | collective-permute-start | bytes 786440 | tf_op jit(solution)/shard_map/ppermute | solution.py:38
  75.2 7.5 %collective-permute-start.14 = (bf16[1024,128]{1,0:T(8,128)(2,1)}, bf16[1024,128]{1,0:T(8,128)(2,1)}, u32[]{:S(2)}, u32[]{:S(2)}) collective-permute-start(bf16[1024,128]{1,0:T(8,128)(2,1)} %collective-permute-done.7.refs_1_.refs_7_), channel_id=1, source_target_pairs={{0,8},{8,0},{1,9},{9,1},{2,10},{10,2},{3,11},{11,3},{4,12},{12,4},... | collective-permute-start | bytes 786440 | tf_op jit(solution)/shard_map/ppermute | solution.py:42
  80.9 5.6 %collective-permute-start.17 = (bf16[1536,128]{1,0:T(8,128)(2,1)}, bf16[1536,128]{1,0:T(8,128)(2,1)S(1)}, u32[]{:S(2)}, u32[]{:S(2)}) collective-permute-start(bf16[1536,128]{1,0:T(8,128)(2,1)} %copy-done.79), channel_id=1, source_target_pairs={{0,8},{8,0},{1,9},{9,1},{2,10},{10,2},{3,11},{11,3},{4,12},{12,4},... | collective-permute-start | bytes 1179656 | tf_op jit(solution)/shard_map/ppermute | solution.py:42
  81.7 5.4 %collective-permute-start.15 = (bf16[1024,128]{1,0:T(8,128)(2,1)}, bf16[1024,128]{1,0:T(8,128)(2,1)S(1)}, u32[]{:S(2)}, u32[]{:S(2)}) collective-permute-start(bf16[1024,128]{1,0:T(8,128)(2,1)} %copy-done.92), channel_id=1, source_target_pairs={{0,8},{8,0},{1,9},{9,1},{2,10},{10,2},{3,11},{11,3},{4,12},{12,4},... | collective-permute-start | bytes 786440 | tf_op jit(solution)/shard_map/ppermute | solution.py:42
  82.7 4.9 %collective-permute-start.16 = (bf16[1024,128]{1,0:T(8,128)(2,1)}, bf16[1024,128]{1,0:T(8,128)(2,1)S(1)}, u32[]{:S(2)}, u32[]{:S(2)}) collective-permute-start(bf16[1024,128]{1,0:T(8,128)(2,1)} %copy-done.91), channel_id=1, source_target_pairs={{0,8},{8,0},{1,9},{9,1},{2,10},{10,2},{3,11},{11,3},{4,12},{12,4},... | collective-permute-start | bytes 786440 | tf_op jit(solution)/shard_map/ppermute | solution.py:42
  82.7 6.9 %collective-permute-start.18 = (bf16[1024,128]{1,0:T(8,128)(2,1)}, bf16[1024,128]{1,0:T(8,128)(2,1)}, u32[]{:S(2)}, u32[]{:S(2)}) collective-permute-start(bf16[1024,128]{1,0:T(8,128)(2,1)} %collective-permute-done.8.refs_5_.refs_9_), channel_id=1, source_target_pairs={{0,8},{8,0},{1,9},{9,1},{2,10},{10,2},{3,11},{11,3},{4,12},{12,4},... | collective-permute-start | bytes 786440 | tf_op jit(solution)/shard_map/ppermute | solution.py:42
  83.2 6.4 %collective-permute-start.19 = (bf16[1024,128]{1,0:T(8,128)(2,1)}, bf16[1024,128]{1,0:T(8,128)(2,1)S(1)}, u32[]{:S(2)}, u32[]{:S(2)}) collective-permute-start(bf16[1024,128]{1,0:T(8,128)(2,1)} %collective-permute-done.9.refs_6_.refs_10_), channel_id=1, source_target_pairs={{0,8},{8,0},{1,9},{9,1},{2,10},{10,2},{3,11},{11,3},{4,12},{12,4},... | collective-permute-start | bytes 786440 | tf_op jit(solution)/shard_map/ppermute | solution.py:42
  86.5 42.4 %collective-permute-start.21 = (bf16[256,1024]{1,0:T(8,128)(2,1)S(1)}, bf16[256,1024]{1,0:T(8,128)(2,1)S(1)}, u32[]{:S(2)}, u32[]{:S(2)}) collective-permute-start(bf16[256,1024]{1,0:T(8,128)(2,1)S(1)} %pad_maximum_fusion.4.refs_4_), channel_id=1, source_target_pairs={{0,2},{2,4},{4,6},{6,0},{1,3},{3,5},{5,7},{7,1},{8,10},{10,12},{12... | collective-permute-start | bytes 1572872 | tf_op jit(solution)/shard_map/ppermute | solution.py:34
  87.1 41.8 %collective-permute-start.22 = (bf16[256,1024]{1,0:T(8,128)(2,1)S(1)}, bf16[256,1024]{1,0:T(8,128)(2,1)S(1)}, u32[]{:S(2)}, u32[]{:S(2)}) collective-permute-start(bf16[256,1024]{1,0:T(8,128)(2,1)S(1)} %pad_maximum_fusion.4.refs_4_), channel_id=1, source_target_pairs={{0,4},{2,6},{4,0},{6,2},{1,5},{3,7},{5,1},{7,3},{8,12},{10,14},{12... | collective-permute-start | bytes 1572872 | tf_op jit(solution)/shard_map/ppermute | solution.py:34
  87.7 41.3 %collective-permute-start.23 = (bf16[256,1024]{1,0:T(8,128)(2,1)S(1)}, bf16[256,1024]{1,0:T(8,128)(2,1)S(1)}, u32[]{:S(2)}, u32[]{:S(2)}) collective-permute-start(bf16[256,1024]{1,0:T(8,128)(2,1)S(1)} %pad_maximum_fusion.4.refs_4_), channel_id=1, source_target_pairs={{0,6},{2,0},{4,2},{6,4},{1,7},{3,1},{5,3},{7,5},{8,14},{10,8},{12,... | collective-permute-start | bytes 1572872 | tf_op jit(solution)/shard_map/ppermute | solution.py:34
  130.1 16.4 %collective-permute-start.24 = (bf16[512,1024]{1,0:T(8,128)(2,1)S(1)}, bf16[512,1024]{1,0:T(8,128)(2,1)S(1)}, u32[]{:S(2)}, u32[]{:S(2)}) collective-permute-start(bf16[512,1024]{1,0:T(8,128)(2,1)S(1)} %pad_maximum_fusion.1.kept.refs_4_), channel_id=1, source_target_pairs={{0,8},{8,0},{1,9},{9,1},{2,10},{10,2},{3,11},{11,3},{4,12},{12,4},... | collective-permute-start | bytes 3145736 | tf_op jit(solution)/shard_map/ppermute | solution.py:42
  130.1 22.8 %collective-permute-start.28 = (bf16[2048,256]{1,0:T(8,128)(2,1)}, bf16[2048,256]{1,0:T(8,128)(2,1)}, u32[]{:S(2)}, u32[]{:S(2)}) collective-permute-start(bf16[2048,256]{1,0:T(8,128)(2,1)} %collective-permute-done.12), channel_id=1, source_target_pairs={{0,8},{8,0},{1,9},{9,1},{2,10},{10,2},{3,11},{11,3},{4,12},{12,4},... | collective-permute-start | bytes 3145736 | tf_op jit(solution)/shard_map/ppermute | solution.py:42
  131.5 15.1 %all-to-all-start.2 = ((bf16[16,64,128]{2,1,0:T(8,128)(2,1)}), bf16[16,64,128]{2,1,0:T(8,128)(2,1)}, u32[]{:S(2)}, u32[]{:S(2)}) async-start(bf16[16,64,128]{2,1,0:T(8,128)(2,1)} %get-tuple-element.108), calls=%async_computation.2 | async-start | bytes 524288 | tf_op jit(solution)/shard_map/all_to_all | solution.py:51
  149.3 8.3 %collective-permute-start.25 = (bf16[128,1024]{1,0:T(8,128)(2,1)S(1)}, bf16[128,1024]{1,0:T(8,128)(2,1)S(1)}, u32[]{:S(2)}, u32[]{:S(2)}) collective-permute-start(bf16[128,1024]{1,0:T(8,128)(2,1)S(1)} %get-tuple-element.113.refs_0_), channel_id=1, source_target_pairs={{0,2},{2,4},{4,6},{6,0},{1,3},{3,5},{5,7},{7,1},{8,10},{10,12},{12... | collective-permute-start | bytes 786440 | tf_op jit(solution)/shard_map/ppermute | solution.py:34
  149.4 12.0 %collective-permute-start.26 = (bf16[128,1024]{1,0:T(8,128)(2,1)S(1)}, bf16[128,1024]{1,0:T(8,128)(2,1)S(1)}, u32[]{:S(2)}, u32[]{:S(2)}) collective-permute-start(bf16[128,1024]{1,0:T(8,128)(2,1)S(1)} %get-tuple-element.113.refs_0_), channel_id=1, source_target_pairs={{0,4},{2,6},{4,0},{6,2},{1,5},{3,7},{5,1},{7,3},{8,12},{10,14},{12... | collective-permute-start | bytes 786440 | tf_op jit(solution)/shard_map/ppermute | solution.py:34
  151.2 12.8 %collective-permute-start.27 = (bf16[128,1024]{1,0:T(8,128)(2,1)S(1)}, bf16[128,1024]{1,0:T(8,128)(2,1)S(1)}, u32[]{:S(2)}, u32[]{:S(2)}) collective-permute-start(bf16[128,1024]{1,0:T(8,128)(2,1)S(1)} %get-tuple-element.113.refs_0_), channel_id=1, source_target_pairs={{0,6},{2,0},{4,2},{6,4},{1,7},{3,1},{5,3},{7,5},{8,14},{10,8},{12,... | collective-permute-start | bytes 786440 | tf_op jit(solution)/shard_map/ppermute | solution.py:34
  172.4 5.8 %collective-permute-start.29 = (bf16[8,2,128,512]{3,2,1,0:T(8,128)(2,1)}, bf16[8,2,128,512]{3,2,1,0:T(8,128)(2,1)}, u32[]{:S(2)}, u32[]{:S(2)}) collective-permute-start(bf16[8,2,128,512]{3,2,1,0:T(8,128)(2,1)} %unit_grads_sent.1), channel_id=1, source_target_pairs={{0,8},{8,0},{1,9},{9,1},{2,10},{10,2},{3,11},{11,3},{4,12},{12,4},... | collective-permute-start | bytes 6291464 | tf_op jit(solution)/shard_map/ppermute | solution.py:42
  174.1 18.5 %all-to-all-start.3 = ((bf16[4,128,1024]{2,1,0:T(8,128)(2,1)}), bf16[4,128,1024]{2,1,0:T(8,128)(2,1)S(1)}, u32[]{:S(2)}, u32[]{:S(2)}) async-start(bf16[4,128,1024]{2,1,0:T(8,128)(2,1)} %copy-done.18), calls=%async_computation.3 | async-start | bytes 2097152 | tf_op jit(solution)/shard_map/all_to_all | solution.py:51
  197.6 15.2 %all-to-all-start.4 = ((bf16[16,64,128]{2,1,0:T(8,128)(2,1)}), bf16[16,64,128]{2,1,0:T(8,128)(2,1)S(1)}, u32[]{:S(2)}, u32[]{:S(2)}) async-start(bf16[16,64,128]{2,1,0:T(8,128)(2,1)} %copy-done.41), calls=%async_computation.4 | async-start | bytes 524288 | tf_op jit(solution)/shard_map/all_to_all | solution.py:51
  201.2 24.9 %collective-permute-start.32 = (f32[72,2048]{1,0:T(8,128)}, f32[72,2048]{1,0:T(8,128)}, u32[]{:S(2)}, u32[]{:S(2)}) collective-permute-start(f32[72,2048]{1,0:T(8,128)} %get-tuple-element.133.refs_4_), channel_id=1, source_target_pairs={{0,8},{8,0},{1,9},{9,1},{2,10},{10,2},{3,11},{11,3},{4,12},{12,4},... | collective-permute-start | bytes 1769480 | tf_op jit(solution)/shard_map/ppermute | solution.py:42
  213.8 78.4 %all-to-all-start.5 = ((bf16[16,256,256]{2,1,0:T(8,128)(2,1)}), bf16[16,256,256]{2,1,0:T(8,128)(2,1)}, u32[]{:S(2)}, u32[]{:S(2)}) async-start(bf16[16,256,256]{2,1,0:T(8,128)(2,1)} %unit_grads_kept.1), calls=%async_computation.5 | async-start | bytes 4194304 | tf_op jit(solution)/shard_map/all_to_all | solution.py:51
  221.0 3.0 collective-permute-start.30
  221.3 4.8 %collective-permute-start.31 = (bf16[16,64,128]{2,1,0:T(8,128)(2,1)S(1)}, bf16[16,64,128]{2,1,0:T(8,128)(2,1)S(1)}, u32[]{:S(2)}, u32[]{:S(2)}) collective-permute-start(bf16[16,64,128]{2,1,0:T(8,128)(2,1)S(1)} %all-to-all-done.4.refs_2_), channel_id=1, source_target_pairs={{0,8},{8,0},{1,9},{9,1},{2,10},{10,2},{3,11},{11,3},{4,12},{12,4},... | collective-permute-start | bytes 786440 | tf_op jit(solution)/shard_map/ppermute | solution.py:42
  221.6 68.9 %collective-permute-start.35 = (bf16[384,1024]{1,0:T(8,128)(2,1)}, bf16[384,1024]{1,0:T(8,128)(2,1)S(1)}, u32[]{:S(2)}, u32[]{:S(2)}) collective-permute-start(bf16[384,1024]{1,0:T(8,128)(2,1)} %copy-done.56), channel_id=1, source_target_pairs={{0,6},{2,0},{4,2},{6,4},{1,7},{3,1},{5,3},{7,5},{8,14},{10,8},{12,... | collective-permute-start | bytes 2359304 | tf_op jit(solution)/shard_map/ppermute | solution.py:34
  224.0 66.4 %collective-permute-start.36 = (bf16[384,1024]{1,0:T(8,128)(2,1)}, bf16[384,1024]{1,0:T(8,128)(2,1)S(1)}, u32[]{:S(2)}, u32[]{:S(2)}) collective-permute-start(bf16[384,1024]{1,0:T(8,128)(2,1)} %copy-done.55), channel_id=1, source_target_pairs={{0,2},{2,4},{4,6},{6,0},{1,3},{3,5},{5,7},{7,1},{8,10},{10,12},{12... | collective-permute-start | bytes 2359304 | tf_op jit(solution)/shard_map/ppermute | solution.py:34
  224.0 67.3 %collective-permute-start.37 = (bf16[384,1024]{1,0:T(8,128)(2,1)S(1)}, bf16[384,1024]{1,0:T(8,128)(2,1)S(1)}, u32[]{:S(2)}, u32[]{:S(2)}) collective-permute-start(bf16[384,1024]{1,0:T(8,128)(2,1)S(1)} %get-tuple-element.129), channel_id=1, source_target_pairs={{0,4},{2,6},{4,0},{6,2},{1,5},{3,7},{5,1},{7,3},{8,12},{10,14},{12... | collective-permute-start | bytes 2359304 | tf_op jit(solution)/shard_map/ppermute | solution.py:34
  253.5 38.7 %collective-permute-start.33 = (bf16[2048,128]{1,0:T(8,128)(2,1)}, bf16[2048,128]{1,0:T(8,128)(2,1)S(1)}, u32[]{:S(2)}, u32[]{:S(2)}) collective-permute-start(bf16[2048,128]{1,0:T(8,128)(2,1)} %get-tuple-element.137), channel_id=1, source_target_pairs={{0,32},{32,0},{64,96},{96,64},{1,33},{33,1},{65,97},{97,65},{2,34}... | collective-permute-start | bytes 1572872 | tf_op jit(solution)/shard_map/ppermute | solution.py:38
  255.1 37.1 %collective-permute-start.34 = (bf16[2048,128]{1,0:T(8,128)(2,1)}, bf16[2048,128]{1,0:T(8,128)(2,1)S(1)}, u32[]{:S(2)}, u32[]{:S(2)}) collective-permute-start(bf16[2048,128]{1,0:T(8,128)(2,1)} %get-tuple-element.138), channel_id=1, source_target_pairs={{0,64},{32,96},{64,0},{96,32},{1,65},{33,97},{65,1},{97,33},{2,66}... | collective-permute-start | bytes 1572872 | tf_op jit(solution)/shard_map/ppermute | solution.py:38
  292.2 8.9 %collective-permute-start.39 = (bf16[16,64,128]{2,1,0:T(8,128)(2,1)}, bf16[16,64,128]{2,1,0:T(8,128)(2,1)S(1)}, u32[]{:S(2)}, u32[]{:S(2)}) collective-permute-start(bf16[16,64,128]{2,1,0:T(8,128)(2,1)} %get-tuple-element.150), channel_id=1, source_target_pairs={{0,8},{8,0},{1,9},{9,1},{2,10},{10,2},{3,11},{11,3},{4,12},{12,4},... | collective-permute-start | bytes 786440 | tf_op jit(solution)/shard_map/ppermute | solution.py:42
  299.7 17.8 %collective-permute-start.38 = (bf16[2048,128]{1,0:T(8,128)(2,1)}, bf16[2048,128]{1,0:T(8,128)(2,1)}, u32[]{:S(2)}, u32[]{:S(2)}) collective-permute-start(bf16[2048,128]{1,0:T(8,128)(2,1)} %get-tuple-element.148), channel_id=1, source_target_pairs={{0,96},{32,64},{64,32},{96,0},{1,97},{33,65},{65,33},{97,1},{2,98}... | collective-permute-start | bytes 1572872 | tf_op jit(solution)/shard_map/ppermute | solution.py:38
  302.2 15.2 %collective-permute-start.40 = (bf16[8,64,128]{2,1,0:T(8,128)(2,1)S(1)}, bf16[8,64,128]{2,1,0:T(8,128)(2,1)S(1)}, u32[]{:S(2)}, u32[]{:S(2)}) collective-permute-start(bf16[8,64,128]{2,1,0:T(8,128)(2,1)S(1)} %get-tuple-element.197), channel_id=1, source_target_pairs={{0,96},{32,64},{64,32},{96,0},{1,97},{33,65},{65,33},{97,1},{2,98}... | collective-permute-start | bytes 393224 | tf_op jit(solution)/shard_map/ppermute | solution.py:38
  320.0 16.3 %all-to-all-start.6 = ((bf16[4,768,128]{2,1,0:T(8,128)(2,1)}), bf16[4,768,128]{2,1,0:T(8,128)(2,1)S(1)}, u32[]{:S(2)}, u32[]{:S(2)}) async-start(bf16[4,768,128]{2,1,0:T(8,128)(2,1)} %pad_maximum_fusion.2), calls=%async_computation.6 | async-start | bytes 1572864 | tf_op jit(solution)/shard_map/all_to_all | solution.py:51
  341.9 19.0 %all-to-all-start.9 = ((bf16[8,512,128]{2,1,0:T(8,128)(2,1)}), bf16[8,512,128]{2,1,0:T(8,128)(2,1)S(1)}, u32[]{:S(2)}, u32[]{:S(2)}) async-start(bf16[8,512,128]{2,1,0:T(8,128)(2,1)} %broadcast_in_dim.89), calls=%async_computation.9 | async-start | bytes 2097152 | tf_op jit(solution)/shard_map/all_to_all | solution.py:51
  352.3 4.1 collective-permute-start.41
  354.1 4.0 collective-permute-start.46
  355.6 2.5 collective-permute-start.47
  356.4 48.4 %collective-permute-start.42 = (f32[2,128,1024]{2,1,0:T(8,128)}, f32[2,128,1024]{2,1,0:T(8,128)}, u32[]{:S(2)}, u32[]{:S(2)}) collective-permute-start(f32[2,128,1024]{2,1,0:T(8,128)} %copy-done.17), channel_id=1, source_target_pairs={{16,112},{48,80},{80,48},{112,16},{17,113},{49,81},{81,49},{113,17... | collective-permute-start | bytes 3145736 | tf_op jit(solution)/shard_map/ppermute | solution.py:46
  360.9 36.6 %all-to-all-start.7 = ((bf16[16,272,128]{2,1,0:T(8,128)(2,1)}), bf16[16,272,128]{2,1,0:T(8,128)(2,1)}, u32[]{:S(2)}, u32[]{:S(2)}) async-start(bf16[16,272,128]{2,1,0:T(8,128)(2,1)} %shares.1), calls=%async_computation.7 | async-start | bytes 2228224 | tf_op jit(solution)/shard_map/all_to_all | solution.py:51
  367.8 42.8 %collective-permute-start.51 = (bf16[8,512,128]{2,1,0:T(8,128)(2,1)S(1)}, bf16[8,512,128]{2,1,0:T(8,128)(2,1)S(1)}, u32[]{:S(2)}, u32[]{:S(2)}) collective-permute-start(bf16[8,512,128]{2,1,0:T(8,128)(2,1)S(1)} %all-to-all-done.9.own), channel_id=1, source_target_pairs={{0,8},{8,0},{1,9},{9,1},{2,10},{10,2},{3,11},{11,3},{4,12},{12,4},... | collective-permute-start | bytes 3145736 | tf_op jit(solution)/shard_map/ppermute | solution.py:42
  368.8 38.2 %collective-permute-start.43 = (bf16[128,1024]{1,0:T(8,128)(2,1)}, bf16[128,1024]{1,0:T(8,128)(2,1)S(1)}, u32[]{:S(2)}, u32[]{:S(2)}) collective-permute-start(bf16[128,1024]{1,0:T(8,128)(2,1)} %get-tuple-element.167), channel_id=1, source_target_pairs={{0,6},{2,0},{4,2},{6,4},{1,7},{3,1},{5,3},{7,5},{8,14},{10,8},{12,... | collective-permute-start | bytes 786440 | tf_op jit(solution)/shard_map/ppermute | solution.py:34
  369.8 37.3 %collective-permute-start.44 = (bf16[128,1024]{1,0:T(8,128)(2,1)}, bf16[128,1024]{1,0:T(8,128)(2,1)S(1)}, u32[]{:S(2)}, u32[]{:S(2)}) collective-permute-start(bf16[128,1024]{1,0:T(8,128)(2,1)} %get-tuple-element.168), channel_id=1, source_target_pairs={{0,2},{2,4},{4,6},{6,0},{1,3},{3,5},{5,7},{7,1},{8,10},{10,12},{12... | collective-permute-start | bytes 786440 | tf_op jit(solution)/shard_map/ppermute | solution.py:34
  370.3 36.7 %collective-permute-start.45 = (bf16[128,1024]{1,0:T(8,128)(2,1)}, bf16[128,1024]{1,0:T(8,128)(2,1)S(1)}, u32[]{:S(2)}, u32[]{:S(2)}) collective-permute-start(bf16[128,1024]{1,0:T(8,128)(2,1)} %get-tuple-element.169), channel_id=1, source_target_pairs={{0,4},{2,6},{4,0},{6,2},{1,5},{3,7},{5,1},{7,3},{8,12},{10,14},{12... | collective-permute-start | bytes 786440 | tf_op jit(solution)/shard_map/ppermute | solution.py:34
  399.7 13.9 %all-to-all-start.8 = ((bf16[8,272,128]{2,1,0:T(8,128)(2,1)}), bf16[8,272,128]{2,1,0:T(8,128)(2,1)S(1)}, u32[]{:S(2)}, u32[]{:S(2)}) async-start(bf16[8,272,128]{2,1,0:T(8,128)(2,1)} %broadcast_in_dim.88), calls=%async_computation.8 | async-start | bytes 1114112 | tf_op jit(solution)/shard_map/all_to_all | solution.py:51
  413.6 3.9 collective-permute-start.48
  415.2 7.0 %collective-permute-start.50 = (bf16[8,272,128]{2,1,0:T(8,128)(2,1)S(1)}, bf16[8,272,128]{2,1,0:T(8,128)(2,1)S(1)}, u32[]{:S(2)}, u32[]{:S(2)}) collective-permute-start(bf16[8,272,128]{2,1,0:T(8,128)(2,1)S(1)} %all-to-all-done.8.own), channel_id=1, source_target_pairs={{0,8},{8,0},{1,9},{9,1},{2,10},{10,2},{3,11},{11,3},{4,12},{12,4},... | collective-permute-start | bytes 1671176 | tf_op jit(solution)/shard_map/ppermute | solution.py:42
  417.5 4.1 collective-permute-start.49
  (96 other events, 774.3 us)
